TPU v7x, 128 devices: a whole 4x4x4 slice. The times are simulated.
128 devices in a mesh: seq: 8 (over x_lo, y), dp: 16 (over z, x_hi, core).
Axes of the slice: x: 4 (x_hi: 2, x_lo: 2; x = x_hi * 2 + x_lo), y: 4, z: 4, core: 2. Of those that a mesh axis runs over, the one named last changes fastest.
Arguments:
- tokens: bfloat16 [16, 1024, 2048], P('dp', 'seq'), may hold values from -6 to 6
- valid_counts: int32 [16, 8], P('dp', 'seq'), may hold values from 32 to 128, as said below
- block_owner: int32 [16, 8], P('dp'), may hold values from 0 to 7, each once within a row
- norm1_gain: bfloat16 [2048], P(('seq', 'dp')), may hold values from 0.099609375 to 1.8984375
- attn_weight: bfloat16 [2048, 4, 2048], P(('seq', 'dp'))
- norm2_gain: bfloat16 [2048], P(('seq', 'dp')), may hold values from 0.099609375 to 1.8984375
- mlp_weight: bfloat16 [2048, 3, 5504], P(('seq', 'dp')), may hold values from -0.125 to 0.125
- cotangent: bfloat16 [16, 1024, 2048], P('dp', 'seq'), may hold values from -6 to 6
Outputs:
- layer_out: bfloat16 [16, 1024, 2048], P('dp', 'seq')
- input_grad: float32 [16, 1024, 2048], P('dp', 'seq')
- norm1_grad: float32 [2048], P(('seq', 'dp'))
- attn_grad: float32 [2048, 4, 2048], P(('seq', 'dp'))
- norm2_grad: float32 [2048], P(('seq', 'dp'))
- mlp_grad: float32 [2048, 3, 5504], P(('seq', 'dp'))
Inputs may be any that keep to these rules, and one draw needn't show every extreme that they name: Device i of sequence s holds 128 tokens, of which the first valid_counts[s, i] are real and the rest padding; in every sequence some device holds no padding. block_owner[s, i] is the place, in blocks of 128 tokens, of the block held by device i of sequence s; each row names every block once.
All inputs are finite; a program needn't handle non-finite values.
Results may differ from a plain program's by a relative error of at most 0.02.
Values may be sent and summed in bfloat16 or wider, within the bound.
A program may use at most 704 MiB of HBM per device.

v0:
```python
import math

import jax
import jax.numpy as jnp
from jax import lax
from jax.sharding import PartitionSpec as P

HEADS = 16


EPS = 1e-05


def lookup(table, index):
    match = index[:, None] == jnp.arange(table.shape[0], dtype=jnp.int32)[None, :]
    return jnp.sum(jnp.where(match, table[None, :], 0), axis=1)


def norm_scale(values):
    return lax.rsqrt(jnp.mean(values * values, axis=-1, keepdims=True) + EPS)


def norm_back(grad_norm, values, scale, gain):
    normed = values * scale
    grad_hat = grad_norm * gain[None, :]
    inner = jnp.mean(grad_hat * normed, axis=-1, keepdims=True)
    return (scale * (grad_hat - normed * inner), jnp.sum(grad_norm * normed, axis=0))


def head_split(values):
    return values.reshape(values.shape[0], HEADS, values.shape[1] // HEADS)


def sigmoid_probs(query_heads, query_pos, key_heads, key_pos, key_live, score_bias):
    scale = 1.0 / math.sqrt(key_heads.shape[2])
    scores = jnp.einsum("qhd,khd->hqk", query_heads, key_heads, preferred_element_type=jnp.float32)
    allowed = (key_pos[None, :] <= query_pos[:, None]) & key_live[None, :]
    return jnp.where(allowed[None], jax.nn.sigmoid(scores * scale + score_bias), 0.0)


def local(
    tokens, valid_counts, block_owner, norm1_gain, attn_weight, norm2_gain, mlp_weight, cotangent
):
    tok_rows = tokens.shape[1]
    model_width = tokens.shape[2]
    units = mlp_weight.shape[2]
    inputs = tokens[0].astype(jnp.float32)
    target_grad = cotangent[0].astype(jnp.float32)
    seq_parts = lax.axis_size("seq")
    seq_length = tok_rows * seq_parts
    score_bias = -math.log(seq_length)
    head_scale = 1.0 / math.sqrt(model_width // HEADS)
    owners = block_owner[0]
    my_index = jnp.reshape(lax.axis_index("seq"), (1,))
    my_block = lookup(owners, my_index)[0]
    row_index = jnp.arange(tok_rows, dtype=jnp.int32)
    key_pos = my_block * tok_rows + row_index
    key_live = row_index < valid_counts[0, 0]
    live_rows = key_live.astype(jnp.float32)[:, None]

    def query_positions(start, count):
        index = start + jnp.arange(count, dtype=jnp.int32)
        return lookup(owners, index // tok_rows) * tok_rows + index % tok_rows

    scale_one = norm_scale(inputs)
    piece_one = lax.all_gather(norm1_gain, ("seq", "dp"), axis=0, tiled=True)
    piece_two = lax.all_gather(norm2_gain, ("seq", "dp"), axis=0, tiled=True)
    piece_w = lax.all_gather(attn_weight[:, :3, :], ("seq", "dp"), axis=0, tiled=True)
    count = piece_w.shape[0]
    columns = inputs
    gain_part = piece_one.astype(jnp.float32)
    block = (columns * scale_one * gain_part[None, :]).astype(jnp.bfloat16)
    projected = jnp.einsum("tc,cjd->tjd", block, piece_w, preferred_element_type=jnp.float32)
    gain_one = gain_part
    gain_two = piece_two.astype(jnp.float32)
    projected, normed_one, gain_one, gain_two = (projected, block, gain_one, gain_two)
    qkv_low = projected.astype(jnp.bfloat16)
    key_heads = head_split(qkv_low[:, 1])
    value_heads = head_split(qkv_low[:, 2])
    all_queries = lax.all_gather(qkv_low[:, 0], "seq", axis=0, tiled=True)
    chosen = head_split(all_queries)
    probs = sigmoid_probs(
        chosen,
        query_positions(jnp.int32(0), lax.axis_size("seq") * tok_rows),
        key_heads,
        key_pos,
        key_live,
        score_bias,
    )
    mixed = jnp.einsum(
        "hqk,khd->qhd", probs.astype(jnp.bfloat16), value_heads, preferred_element_type=jnp.float32
    )
    attended = lax.psum_scatter(
        mixed.reshape(lax.axis_size("seq") * tok_rows, model_width).astype(jnp.bfloat16),
        "seq",
        scatter_dimension=0,
        tiled=True,
    )
    columns = attended
    branch = jnp.dot(
        columns,
        lax.all_gather(attn_weight[:, 3, :], ("seq", "dp"), axis=0, tiled=True),
        preferred_element_type=jnp.float32,
    )
    resid = inputs + branch
    scale_two = norm_scale(resid)
    normed_two = (resid * scale_two * gain_two[None, :]).astype(jnp.bfloat16)
    columns = normed_two
    gate_up = jnp.einsum(
        "tc,cjf->tjf",
        columns,
        lax.all_gather(mlp_weight[:, :2, :], ("seq", "dp"), axis=0, tiled=True),
        preferred_element_type=jnp.float32,
    )
    gate_act = gate_up[:, 0]
    up_act = gate_up[:, 1]
    squashed = jax.nn.sigmoid(gate_act)
    activated = gate_act * squashed
    hidden = (activated * up_act).astype(jnp.bfloat16)
    grad_out = target_grad * live_rows
    grad_low = grad_out.astype(jnp.bfloat16)

    def down_pass(front, back):
        piece = lax.all_gather(mlp_weight[:, 2, :], ("seq", "dp"), axis=0, tiled=True)
        produced = jnp.zeros((tok_rows, model_width), jnp.float32)
        returned = jnp.zeros((tok_rows, units), jnp.float32)
        if front:
            columns = lax.dot_general(
                hidden, piece, (((1,), (1,)), ((), ())), preferred_element_type=jnp.float32
            )
            produced = columns
        if back:
            returned = jnp.dot(grad_low, piece, preferred_element_type=jnp.float32)
        return (produced, returned)

    branch_two, unused = down_pass(True, False)
    unused, grad_hidden = down_pass(False, True)
    output = (live_rows * (resid + branch_two)).astype(jnp.bfloat16)
    silu_slope = squashed * (1.0 + gate_act * (1.0 - squashed))
    grad_gate = (grad_hidden * up_act * silu_slope).astype(jnp.bfloat16)
    grad_up = (grad_hidden * activated).astype(jnp.bfloat16)
    grad_pair = jnp.stack([grad_gate, grad_up], axis=1)
    grad_normed_two = jnp.einsum(
        "tjf,cjf->tc",
        grad_pair,
        lax.all_gather(mlp_weight[:, :2, :], ("seq", "dp"), axis=0, tiled=True),
        preferred_element_type=jnp.float32,
    )
    normed_cols = normed_two
    pair_part = jnp.einsum(
        "tc,tjf->cjf", normed_cols, grad_pair, preferred_element_type=jnp.float32
    )
    down_part = jnp.einsum("tc,tf->cf", grad_low, hidden, preferred_element_type=jnp.float32)
    mlp_grad = lax.psum_scatter(
        jnp.concatenate([pair_part, down_part[:, None, :]], axis=1),
        ("seq", "dp"),
        scatter_dimension=0,
        tiled=True,
    )
    grad_norm_two, gain_two_grad = norm_back(grad_normed_two, resid, scale_two, gain_two)
    grad_resid = grad_out + grad_norm_two
    grad_branch = grad_resid.astype(jnp.bfloat16)
    grad_attended = lax.dot_general(
        grad_branch,
        lax.all_gather(attn_weight[:, 3, :], ("seq", "dp"), axis=0, tiled=True),
        (((1,), (1,)), ((), ())),
        preferred_element_type=jnp.float32,
    ).astype(jnp.bfloat16)
    gathered_grad, again_queries = (
        lax.all_gather(grad_attended, "seq", axis=0, tiled=True),
        lax.all_gather(qkv_low[:, 0], "seq", axis=0, tiled=True),
    )

    def score_grads(start, count):
        chosen_q = head_split(lax.dynamic_slice_in_dim(again_queries, start, count, 0))
        chosen_g = head_split(lax.dynamic_slice_in_dim(gathered_grad, start, count, 0))
        probs = sigmoid_probs(
            chosen_q, query_positions(start, count), key_heads, key_pos, key_live, score_bias
        )
        grad_probs = jnp.einsum(
            "qhd,khd->hqk", chosen_g, value_heads, preferred_element_type=jnp.float32
        )
        grad_scores = (grad_probs * probs * (1.0 - probs)).astype(jnp.bfloat16)
        return (chosen_q, chosen_g, probs, grad_scores)

    block_rows = min(seq_length, 512)
    blocks = seq_length // block_rows

    def key_grads(carry, index):
        grad_keys, grad_values = carry
        chosen_q, chosen_g, probs, grad_scores = score_grads(index * block_rows, block_rows)
        grad_values = grad_values + jnp.einsum(
            "hqk,qhd->khd", probs.astype(jnp.bfloat16), chosen_g, preferred_element_type=jnp.float32
        )
        grad_keys = grad_keys + jnp.einsum(
            "hqk,qhd->khd", grad_scores, chosen_q, preferred_element_type=jnp.float32
        )
        return ((grad_keys, grad_values), None)

    head_zeros = jnp.zeros(key_heads.shape, jnp.float32)
    (grad_keys, grad_values), unused_out = lax.scan(
        key_grads, (head_zeros, head_zeros), jnp.arange(blocks, dtype=jnp.int32)
    )
    grad_keys = (grad_keys * head_scale).reshape(tok_rows, model_width).astype(jnp.bfloat16)
    grad_values = grad_values.reshape(tok_rows, model_width).astype(jnp.bfloat16)
    chosen_q, chosen_g, probs, grad_scores = score_grads(
        jnp.int32(0), lax.axis_size("seq") * tok_rows
    )
    grad_q = jnp.einsum("hqk,khd->qhd", grad_scores, key_heads, preferred_element_type=jnp.float32)
    grad_queries = lax.psum_scatter(
        (grad_q * head_scale)
        .reshape(lax.axis_size("seq") * tok_rows, model_width)
        .astype(jnp.bfloat16),
        "seq",
        scatter_dimension=0,
        tiled=True,
    )
    grad_proj = jnp.stack([grad_queries, grad_keys, grad_values], axis=1)
    grad_normed_one = jnp.einsum(
        "tjd,cjd->tc",
        grad_proj,
        lax.all_gather(attn_weight[:, :3, :], ("seq", "dp"), axis=0, tiled=True),
        preferred_element_type=jnp.float32,
    )
    normed_cols = normed_one
    proj_part = jnp.einsum(
        "tc,tjd->cjd", normed_cols, grad_proj, preferred_element_type=jnp.float32
    )
    out_part = jnp.einsum("tc,td->cd", attended, grad_branch, preferred_element_type=jnp.float32)
    attn_grad = lax.psum_scatter(
        jnp.concatenate([proj_part, out_part[:, None, :]], axis=1),
        ("seq", "dp"),
        scatter_dimension=0,
        tiled=True,
    )
    grad_norm_one, gain_one_grad = norm_back(grad_normed_one, inputs, scale_one, gain_one)
    input_grad = grad_resid + grad_norm_one
    gain_grads = (
        lax.psum_scatter(gain_one_grad, ("seq", "dp"), scatter_dimension=0, tiled=True),
        lax.psum_scatter(gain_two_grad, ("seq", "dp"), scatter_dimension=0, tiled=True),
    )
    return (output[None], input_grad[None], gain_grads[0], attn_grad, gain_grads[1], mlp_grad)


def solution(mesh):
    in_specs = (
        P("dp", "seq", None),
        P("dp", "seq"),
        P("dp", None),
        P(("seq", "dp")),
        P(("seq", "dp"), None, None),
        P(("seq", "dp")),
        P(("seq", "dp"), None, None),
        P("dp", "seq", None),
    )
    out_specs = (
        P("dp", "seq", None),
        P("dp", "seq", None),
        P(("seq", "dp")),
        P(("seq", "dp"), None, None),
        P(("seq", "dp")),
        P(("seq", "dp"), None, None),
    )
    return jax.shard_map(local, mesh=mesh, in_specs=in_specs, out_specs=out_specs, check_vma=False)
```

profile of v0, /device:TPU:0, one launch (start us, length us, event | category | flops | bytes accessed | tf_op | source)
XLA Modules:
  0.0 3597.5 jit_solution(3021058814239542874)
XLA Ops:
  10.8 68.4 %all-reduce.5 = (bf16[2048]{0:T(1024)(128)(2,1)S(1)}, bf16[2048]{0:T(1024)(128)(2,1)S(1)}) all-reduce(bf16[2048]{0:T(1024)(128)(2,1)S(1)} %dynamic-update-slice, bf16[2048]{0:T(1024)(128)(2,1)S(1)} %dynamic-update-slice.1), channel_id=1, replica_groups=mesh['seq'=8,'dp'=16] {'seq','dp'}, use_global_device_ids=true, to_apply=%add | all-reduce | flops 4096 | bytes 16384
  80.5 160.4 %all-gather.10.cloned.1.call-done = bf16[2048,3,2048]{2,0,1:T(8,128)(2,1)} async-done(((bf16[16,3,2048]{2,0,1:T(8,128)(2,1)}), bf16[2048,3,2048]{2,0,1:T(8,128)(2,1)}) %all-gather.10.cloned.1.call-update) | async-done | bytes 25165840 | tf_op jit(solution)/shard_map/all_gather | solution.py:68
  240.8 11.9 convolution_convert_fusion
  257.7 47.2 %all-gather.16.cloned.1.call-done = bf16[1024,1,2048]{2,0,1:T(8,128)(2,1)} async-done(((bf16[128,1,2048]{2,0,1:T(8,128)(2,1)}), bf16[1024,1,2048]{2,0,1:T(8,128)(2,1)}) %all-gather.16.cloned.1.call-update) | async-done | bytes 4194320 | tf_op jit(solution)/shard_map/all_gather | solution.py:80
  316.0 6.5 copy.111
  325.2 184.0 %all-gather.18.cloned.1.call-done = bf16[2048,1,2048]{2,0,1:T(8,128)(2,1)} async-done(((bf16[16,1,2048]{2,0,1:T(8,128)(2,1)}), bf16[2048,1,2048]{2,0,1:T(8,128)(2,1)}) %all-gather.18.cloned.1.call-update) | async-done | bytes 8388624 | tf_op jit(solution)/shard_map/all_gather | solution.py:102
  509.2 53.7 %reduce-scatter.13.cloned.1.call-done = bf16[128,2048]{1,0:T(8,128)(2,1)} async-done(((bf16[1024,2048]{1,0:T(8,128)(2,1)}), bf16[128,2048]{1,0:T(8,128)(2,1)}) %reduce-scatter.13.cloned.1.call-update) | async-done | bytes 524304
  567.9 253.6 %all-gather.12.cloned.1.call-done = bf16[2048,2,5504]{2,0,1:T(8,128)(2,1)} async-done(((bf16[16,2,5504]{2,0,1:T(8,128)(2,1)}), bf16[2048,2,5504]{2,0,1:T(8,128)(2,1)}) %all-gather.12.cloned.1.call-update) | async-done | bytes 45088784 | tf_op jit(solution)/shard_map/all_gather | solution.py:112
  821.4 20.0 fusion.108
  841.4 205.2 %all-gather.20.cloned.1.call-done = bf16[2048,1,5504]{2,0,1:T(8,128)(2,1)} async-done(((bf16[16,1,5504]{2,0,1:T(8,128)(2,1)}), bf16[2048,1,5504]{2,0,1:T(8,128)(2,1)}) %all-gather.20.cloned.1.call-update) | async-done | bytes 22544400 | tf_op jit(solution)/shard_map/all_gather | solution.py:124
  1046.6 14.2 fusion.82
  1060.9 22.2 multiply_reduce_fusion
  1084.9 7.4 fusion.68
  1092.6 50.7 %all-gather.14.cloned.1.call-done = bf16[1024,2048]{1,0:T(8,128)(2,1)} async-done(((bf16[128,2048]{1,0:T(8,128)(2,1)}), bf16[1024,2048]{1,0:T(8,128)(2,1)}) %all-gather.14.cloned.1.call-update) | async-done | bytes 4194320 | tf_op jit(solution)/shard_map/all_gather | solution.py:170
  1143.3 10.1 multiply_convert_fusion.1
  1153.4 6.5 copy.93
  1162.8 9.4 convolution_bitcast_fusion.1
  1172.1 52.2 %while.15 = (s32[]{:T(128)}, f32[128,16,128]{0,2,1:T(8,128)}, f32[128,16,128]{0,2,1:T(8,128)S(1)}, s32[2]{0:T(128)S(1)}, bf16[1024,2048]{1,0:T(8,128)(2,1)}, /*i...) while((s32[]{:T(128)}, f32[128,16,128]{0,2,1:T(8,128)}, ...), condition=%wide.region_9.10_spmd.clone, body=%wide.region_7.9_spmd.clone.sunk | while | flops 1086483200 | bytes 43136524 | solution.py:201
  1184.2 5.2 divide_select_fusion.3
  1189.4 5.7 fusion.167
  1210.0 5.2 divide_select_fusion.3
  1215.2 5.8 fusion.167
  1226.5 20.6 fusion.95
  1247.1 44.6 %pad_maximum_fusion.1 = f32[2048,4,2048]{2,0,1:T(8,128)} fusion(f32[2048,1,2048]{2,0,1:T(8,128)} %convolution_bitcast_fusion.1, f32[2048,3,2048]{2,0,1:T(8,128)} %fusion.95), kind=kLoop, calls=%fused_computation.31 | loop fusion | flops 16777216 | bytes 134217728 | tf_op jit(solution)/shard_map/concatenate | solution.py:231
  1292.7 20.6 convolution_bitcast_fusion
  1313.3 33.4 fusion.74
  1346.7 88.7 %pad_maximum_fusion = f32[2048,3,5504]{2,0,1:T(8,128)} fusion(f32[2048,1,5504]{2,0,1:T(8,128)} %convolution_bitcast_fusion, f32[2048,2,5504]{2,0,1:T(8,128)} %fusion.74), kind=kLoop, calls=%fused_computation.30 | loop fusion | flops 33816576 | bytes 270532608 | tf_op jit(solution)/shard_map/concatenate | solution.py:155
  1435.4 14.3 fusion.71
  1449.7 14.9 fusion.93
  1464.6 604.4 %all-reduce.4 = (f32[2048]{0:T(1024)S(1)}, f32[2048]{0:T(1024)S(1)}) all-reduce(f32[2048]{0:T(1024)S(1)} %get-tuple-element.278, f32[2048]{0:T(1024)S(1)} %copy-done.28), channel_id=7, replica_groups=mesh['seq'=8,'dp'=16] {'seq','dp'}, use_global_device_ids=true, to_apply=%region_12.13.clone | all-reduce | flops 4096 | bytes 32768
  2072.7 59.4 %reduce-scatter.9.cloned.1.call-done = f32[16,4,2048]{2,0,1:T(8,128)} async-done(((f32[2048,4,2048]{2,0,1:T(8,128)}), f32[16,4,2048]{2,0,1:T(8,128)}) %reduce-scatter.9.cloned.1.call-update) | async-done | bytes 524304 | tf_op jit(solution)/shard_map/reduce_scatter | solution.py:230
  2134.3 1456.2 %reduce-scatter.11.cloned.1.call-done = f32[16,3,5504]{2,0,1:T(8,128)} async-done(((f32[2048,3,5504]{2,0,1:T(8,128)}), f32[16,3,5504]{2,0,1:T(8,128)}) %reduce-scatter.11.cloned.1.call-update) | async-done | bytes 1056784 | tf_op jit(solution)/shard_map/reduce_scatter | solution.py:154
  (162 shorter events, 69.6 us)
Async XLA Ops:
  7.2 233.6 %all-gather.10.cloned.1.call-start = ((), (), s32[]{:S(2)}) async-start(), calls=%async_computation.4 | async-start | bytes 25362432 | tf_op jit(solution)/shard_map/all_gather | solution.py:68
  9.0 295.8 %all-gather.16.cloned.1.call-start = ((), (), s32[]{:S(2)}) async-start(), calls=%async_computation.10 | async-start | bytes 4718592 | tf_op jit(solution)/shard_map/all_gather | solution.py:80
  79.2 161.6 %copy-start.25 = (f32[2048]{0:T(1024)}, f32[2048]{0:T(1024)S(1)}, u32[]{:S(2)}) copy-start(f32[2048]{0:T(1024)S(1)} %convert_element_type.133) | copy-start | bytes 24580
  80.4 160.4 %copy-start.34 = (f32[128]{0:T(128)}, f32[128]{0:T(128)S(1)}, u32[]{:S(2)}) copy-start(f32[128]{0:T(128)S(1)} %add_rsqrt_fusion.1) | copy-start | bytes 1540
  80.4 173.3 %copy-start.22 = (bf16[16,4,2048]{2,1,0:T(4,128)(2,1)S(1)}, bf16[16,4,2048]{2,1,0:T(4,128)(2,1)}, u32[]{:S(2)}) copy-start(bf16[16,4,2048]{2,1,0:T(4,128)(2,1)} %param.14) | copy-start | bytes 786436
  253.6 255.5 %all-gather.18.cloned.1.call-start = ((), (), s32[]{:S(2)}) async-start(), calls=%async_computation.11 | async-start | bytes 8454144 | tf_op jit(solution)/shard_map/all_gather | solution.py:102
  254.6 308.3 %reduce-scatter.13.cloned.1.call-start = ((), (), s32[]{:S(2)}) async-start(), calls=%async_computation.13 | async-start | bytes 4718592
  257.5 885.8 %copy-start.8 = (bf16[16,8,16,128]{3,2,1,0:T(8,128)(2,1)}, bf16[16,8,16,128]{3,2,1,0:T(8,128)(2,1)S(1)}, u32[]{:S(2)}) copy-start(bf16[16,8,16,128]{3,2,1,0:T(8,128)(2,1)S(1)} %copy.118) | copy-start | bytes 1572868
  257.7 885.6 %copy-start.12 = (bf16[16,8,16,128]{3,2,1,0:T(8,128)(2,1)}, bf16[16,8,16,128]{3,2,1,0:T(8,128)(2,1)S(1)}, u32[]{:S(2)}) copy-start(bf16[16,8,16,128]{3,2,1,0:T(8,128)(2,1)S(1)} %copy.120) | copy-start | bytes 1572868
  322.5 240.4 %copy-start.3 = (bf16[1,128,2048]{2,1,0:T(8,128)(2,1)S(1)}, bf16[1,128,2048]{2,1,0:T(8,128)(2,1)}, u32[]{:S(2)}) copy-start(bf16[1,128,2048]{2,1,0:T(8,128)(2,1)} %param.10) | copy-start | bytes 1572868
  322.6 498.9 %all-gather.12.cloned.1.call-start = ((), (), s32[]{:S(2)}) async-start(), calls=%async_computation.5 | async-start | bytes 45441024 | tf_op jit(solution)/shard_map/all_gather | solution.py:112
  324.3 722.3 %all-gather.20.cloned.1.call-start = ((), (), s32[]{:S(2)}) async-start(), calls=%async_computation.12 | async-start | bytes 22720512 | tf_op jit(solution)/shard_map/all_gather | solution.py:124
  325.1 818.2 %all-gather.14.cloned.1.call-start = ((), (), s32[]{:S(2)}) async-start(), calls=%async_computation.6 | async-start | bytes 4718592 | tf_op jit(solution)/shard_map/all_gather | solution.py:170
  325.2 758.0 %copy-start.20 = (f32[2048]{0:T(1024)}, f32[2048]{0:T(1024)S(1)}, u32[]{:S(2)}) copy-start(f32[2048]{0:T(1024)S(1)} %convert_element_type.140) | copy-start | bytes 24580
  325.2 757.9 %copy-start.32 = (f32[128]{0:T(128)}, f32[128]{0:T(128)S(1)}, u32[]{:S(2)}) copy-start(f32[128]{0:T(128)S(1)} %fusion.126) | copy-start | bytes 1540
  567.9 515.3 %copy-start.1 = (f32[128,2048]{1,0:T(8,128)}, f32[128,2048]{1,0:T(8,128)S(1)}, u32[]{:S(2)}) copy-start(f32[128,2048]{1,0:T(8,128)S(1)} %get-tuple-element.314) | copy-start | bytes 3145732
  567.9 515.3 %copy-start.29 = (f32[128]{0:T(128)}, f32[128]{0:T(128)S(1)}, u32[]{:S(2)}) copy-start(f32[128]{0:T(128)S(1)} %add_rsqrt_fusion) | copy-start | bytes 1540
  821.4 225.2 %copy-start.14 = (bf16[1,128,2048]{2,1,0:T(8,128)(2,1)S(1)}, bf16[1,128,2048]{2,1,0:T(8,128)(2,1)}, u32[]{:S(2)}) copy-start(bf16[1,128,2048]{2,1,0:T(8,128)(2,1)} %param.17) | copy-start | bytes 1572868
  1060.9 22.2 copy-start.10
  1084.9 77.9 %copy-start.6 = (f32[128,2048]{1,0:T(8,128)}, f32[128,2048]{1,0:T(8,128)S(1)}, u32[]{:S(2)}) copy-start(f32[128,2048]{1,0:T(8,128)S(1)} %fusion.84) | copy-start | bytes 3145732
  1092.4 134.1 %reduce-scatter.7.cloned.1.call-start = ((), (), s32[]{:S(2)}) async-start(), calls=%async_computation.7 | async-start | bytes 4718592 | tf_op jit(solution)/shard_map/reduce_scatter | solution.py:210
  1159.9 972.2 %reduce-scatter.9.cloned.1.call-start = ((), (), s32[]{:S(2)}) async-start(), calls=%async_computation.8 | async-start | bytes 67633152 | tf_op jit(solution)/shard_map/reduce_scatter | solution.py:230
  1224.6 22.4 copy-start.16
  1226.4 20.7 copy-start.18
  1291.7 21.6 copy-start.2
  1291.7 21.6 copy-start.11
  1291.7 21.6 copy-start.21
  1291.7 21.6 copy-start.30
  1291.8 2298.7 %reduce-scatter.11.cloned.1.call-start = ((), (), s32[]{:S(2)}) async-start(), calls=%async_computation.9 | async-start | bytes 136323072 | tf_op jit(solution)/shard_map/reduce_scatter | solution.py:154
  1435.4 14.3 copy-start.5
  1449.7 14.9 copy-start.28
  1449.7 620.4 %copy-start.7 = (f32[128,2048]{1,0:T(8,128)S(1)}, f32[128,2048]{1,0:T(8,128)}, u32[]{:S(2)}) copy-start(f32[128,2048]{1,0:T(8,128)} %copy-done.6) | copy-start | bytes 3145732
  (15 other events, 91.9 us)
Sparse Core Ops, SparseCore 0:
  10.3 230.4 all-gather.9
  253.8 51.0 all-gather.15
  307.1 201.9 all-gather.17
  511.4 51.4 reduce-scatter.12
  565.0 256.4 all-gather.11
  823.6 222.9 all-gather.19
  1092.5 50.7 all-gather.13
  1160.0 51.8 reduce-scatter.6
  1291.8 840.2 reduce-scatter.8
  2134.9 1455.5 reduce-scatter.10
where the time goes:
time: 3600 us
  waiting for transfers between devices  2470 us (69%)
  blocking collectives  673 us (19%)
  matrix products  239 us (7%)
  other arithmetic  143 us (4%)
  local copies, waits for them, and re-layouts  52.9 us (1%)
    reduce_scatter x1, waiting for transfers between devices, local(): lax.psum_scatter(jnp.concatenate([pair_part, down_part[:, None, :]], axis...  1460 us
    unnamed x2, blocking collectives  673 us
    all_gather x1, waiting for transfers between devices, local(): lax.all_gather(mlp_weight[:, :2, :], ('seq', 'dp'), axis=0, tiled=True)  254 us
    all_gather x1, waiting for transfers between devices, down_pass(): lax.all_gather(mlp_weight[:, 2, :], ('seq', 'dp'), axis=0, tiled=True)  205 us
    all_gather x1, waiting for transfers between devices, local(): lax.all_gather(attn_weight[:, 3, :], ('seq', 'dp'), axis=0, tiled=True)  184 us
    all_gather x1, waiting for transfers between devices, local(): lax.all_gather(attn_weight[:, :3, :], ('seq', 'dp'), axis=0, tiled=True)  160 us
    concatenate x1, other arithmetic, local(): jnp.concatenate([pair_part, down_part[:, None, :]], axis=1)  88.7 us
  transfers between devices with their start and end apart: 10, of which 9 were waited for; matrix products, arithmetic and copies ran while one was open for 8% of the time, Pallas kernels for 0%

commit v1 on v0

v1 whole, which is shorter than its diff:
```python
import math

import jax
import jax.numpy as jnp
from jax import lax
from jax.sharding import PartitionSpec as P

HEAD_DIM = 128
EPS = 1e-05
LOW = jnp.bfloat16
WIDE = jnp.float32


def dot(a, b, dims):
    return lax.dot_general(a, b, (dims, ((), ())), preferred_element_type=WIDE)


def norm_scale(values):
    return lax.rsqrt(jnp.mean(values * values, axis=-1, keepdims=True) + EPS)


def norm_back(grad_hat, normed, scale):
    inner = jnp.mean(grad_hat * normed, axis=-1, keepdims=True)
    return scale * (grad_hat - normed * inner)


def gather_tokens(rows):
    return lax.all_gather(rows, "seq", axis=0, tiled=True)


def scatter_tokens(partial):
    return lax.psum_scatter(partial.astype(LOW), "seq", scatter_dimension=0, tiled=True).astype(WIDE)


def columns_in(rows):
    count, slots, width = rows.shape
    seq, dp = lax.axis_size("seq"), lax.axis_size("dp")
    cut = rows.reshape(count, slots, seq, width // seq)
    mine = lax.all_to_all(cut, "seq", split_axis=2, concat_axis=0, tiled=True)[:, :, 0]
    mine = mine.reshape(seq, count, slots, width // seq)
    whole = lax.all_gather(mine, "dp", axis=0)
    return whole.transpose(1, 0, 2, 3, 4).reshape(seq * dp * count, slots, width // seq)


def columns_out(grads):
    rows, slots, part = grads.shape
    seq, dp = lax.axis_size("seq"), lax.axis_size("dp")
    count = rows // (seq * dp)
    cut = grads.astype(LOW).reshape(seq, dp, count, slots, part).transpose(1, 0, 2, 3, 4)
    mine = lax.psum_scatter(cut, "dp", scatter_dimension=0)
    mine = lax.all_to_all(mine, "seq", split_axis=0, concat_axis=0, tiled=True)
    return mine.transpose(1, 2, 0, 3).reshape(count, slots, seq * part).astype(WIDE)


def local(
    tokens, valid_counts, block_owner, norm1_gain, attn_weight, norm2_gain, mlp_weight, cotangent
):
    rows, model = tokens.shape[1], tokens.shape[2]
    seq = lax.axis_size("seq")
    length = rows * seq
    score_bias = -math.log(length)
    head_scale = 1.0 / math.sqrt(HEAD_DIM)
    heads = model // HEAD_DIM // seq
    live = (jnp.arange(rows, dtype=jnp.int32) < valid_counts[0, 0]).astype(WIDE)[:, None]
    inputs = tokens[0].astype(WIDE)
    grad_out = cotangent[0].astype(WIDE) * live
    gain_one = norm1_gain.astype(WIDE)[:, None, None]
    gain_two = norm2_gain.astype(WIDE)[:, None, None]

    w_in = columns_in((attn_weight[:, :3].astype(WIDE) * gain_one).astype(LOW))
    w_out = lax.all_gather(attn_weight[:, 3], "dp", axis=0, tiled=True)
    m_in = columns_in(
        jnp.concatenate(
            [(mlp_weight[:, :2].astype(WIDE) * gain_two).astype(LOW), mlp_weight[:, 2:]], axis=1
        )
    )
    m_pair, m_down = m_in[:, :2], m_in[:, 2]
    units = m_down.shape[1]

    scale_one = norm_scale(inputs)
    hat_one = inputs * scale_one
    all_one = gather_tokens((hat_one * live).astype(LOW))
    all_grad = gather_tokens(grad_out.astype(LOW))

    w_flat = w_in.reshape(model, -1)
    proj = dot(all_one, w_flat, ((1,), (0,))).astype(LOW).reshape(length, 3, heads, HEAD_DIM)
    q, k, v = proj[:, 0], proj[:, 1], proj[:, 2]
    pos = (block_owner[0][:, None] * rows + jnp.arange(rows, dtype=jnp.int32)[None]).reshape(-1)
    allowed = (pos[None, :] <= pos[:, None])[None]

    def probabilities():
        scores = jnp.einsum("qhd,khd->hqk", q, k, preferred_element_type=WIDE)
        return jnp.where(allowed, jax.nn.sigmoid(scores * head_scale + score_bias), 0.0)

    probs = probabilities()
    weights = probs.astype(LOW)
    attended = jnp.einsum("hqk,khd->qhd", weights, v, preferred_element_type=WIDE)
    attended = attended.astype(LOW).reshape(length, heads * HEAD_DIM)
    resid = inputs + scatter_tokens(dot(attended, w_out, ((1,), (0,))))

    scale_two = norm_scale(resid)
    hat_two = resid * scale_two
    all_two = gather_tokens((hat_two * live).astype(LOW))
    m_flat = m_pair.reshape(model, 2 * units)
    gate_up = dot(all_two, m_flat, ((1,), (0,)))
    gate_act, up_act = gate_up[:, :units], gate_up[:, units:]
    squashed = jax.nn.sigmoid(gate_act)
    activated = gate_act * squashed
    hidden = (activated * up_act).astype(LOW)
    grad_hidden = dot(all_grad, m_down, ((1,), (0,)))
    slope = squashed * (1.0 + gate_act * (1.0 - squashed))
    grad_pair = jnp.concatenate(
        [(grad_hidden * up_act * slope).astype(LOW), (grad_hidden * activated).astype(LOW)], axis=1
    )
    e_two = scatter_tokens(dot(grad_pair, m_flat, ((1,), (1,))))
    grad_resid = grad_out + norm_back(e_two, hat_two, scale_two)
    all_branch = gather_tokens(grad_resid.astype(LOW))

    branch_two = scatter_tokens(dot(hidden, m_down, ((1,), (1,))))
    layer_out = (live * (resid + branch_two)).astype(LOW)
    mlp_terms = jnp.concatenate(
        [
            dot(all_two, grad_pair, ((0,), (0,))).reshape(model, 2, units),
            dot(all_grad, hidden, ((0,), (0,)))[:, None],
        ],
        axis=1,
    )
    mlp_sum = columns_out(mlp_terms)

    g_att = dot(all_branch, w_out, ((1,), (1,))).astype(LOW).reshape(length, heads, HEAD_DIM)
    grad_v = jnp.einsum("hqk,qhd->khd", weights, g_att, preferred_element_type=WIDE)
    grad_w = jnp.einsum("qhd,khd->hqk", g_att, v, preferred_element_type=WIDE)
    grad_s = (grad_w * probs * (1.0 - probs)).astype(LOW)
    grad_k = jnp.einsum("hqk,qhd->khd", grad_s, q, preferred_element_type=WIDE) * head_scale
    grad_q = jnp.einsum("hqk,khd->qhd", grad_s, k, preferred_element_type=WIDE) * head_scale
    grad_proj = jnp.stack([grad_q, grad_k, grad_v], axis=1).astype(LOW)
    grad_proj = grad_proj.reshape(length, 3 * heads * HEAD_DIM)
    e_one = scatter_tokens(dot(grad_proj, w_flat, ((1,), (1,))))
    input_grad = grad_resid + live * norm_back(e_one, hat_one, scale_one)

    in_terms = dot(all_one, grad_proj, ((0,), (0,))).reshape(model, 3, heads * HEAD_DIM)
    in_sum = columns_out(in_terms)
    out_terms = dot(attended, all_branch, ((0,), (0,))).astype(LOW)
    out_sum = lax.psum_scatter(out_terms, "dp", scatter_dimension=0, tiled=True).astype(WIDE)
    attn_grad = jnp.concatenate([in_sum * gain_one, out_sum[:, None]], axis=1)
    mlp_grad = jnp.concatenate([mlp_sum[:, :2] * gain_two, mlp_sum[:, 2:]], axis=1)
    gain_one_grad = jnp.sum(in_sum * attn_weight[:, :3].astype(WIDE), axis=(1, 2))
    gain_two_grad = jnp.sum(mlp_sum[:, :2] * mlp_weight[:, :2].astype(WIDE), axis=(1, 2))
    return (layer_out[None], input_grad[None], gain_one_grad, attn_grad, gain_two_grad, mlp_grad)


def solution(mesh):
    token_spec = P("dp", "seq", None)
    row_spec = P(("seq", "dp"), None, None)
    gain_spec = P(("seq", "dp"))
    in_specs = (
        token_spec, P("dp", "seq"), P("dp", None), gain_spec, row_spec, gain_spec, row_spec, token_spec
    )
    out_specs = (token_spec, token_spec, gain_spec, row_spec, gain_spec, row_spec)
    return jax.shard_map(local, mesh=mesh, in_specs=in_specs, out_specs=out_specs, check_vma=False)
```

time: 3600 us -> 962 us (0.27)
  waiting for transfers between devices: 2470 us -> 646 us
  blocking collectives: 673 us -> 48.4 us
  matrix products: 239 us -> 96.5 us
  other arithmetic: 143 us -> 42.2 us
  local copies, waits for them, and re-layouts: 52.9 us -> 95.9 us
    reduce_scatter x3 -> x7, waiting for transfers between devices: 1520 us -> 377 us  [the longest x4 190 us: scatter_tokens(): lax.psum_scatter(partial.astype(LOW), 'seq', scatter_dimension=0, tiled=T...]
    unnamed x2 -> x0, blocking collectives: 673 us -> none
    all_gather x6 -> x7, waiting for transfers between devices: 901 us -> 267 us  [the longest x4 120 us: gather_tokens(): return lax.all_gather(rows, 'seq', axis=0, tiled=True)]
    dot_general x21 -> x18, matrix products: 239 us -> 96.5 us  [the longest x12 83.4 us: dot(): return lax.dot_general(a, b, (dims, ((), ())), preferred_element_type=WIDE)]
    concatenate x2 -> x3, other arithmetic: 133 us -> 1.14 us  [the longest x1 1.04 us: local(): jnp.concatenate([mlp_sum[:, :2] * gain_two, mlp_sum[:, 2:]], axis=1)]
    unnamed x11 -> x14, waiting for transfers between devices: 53.9 us -> 0.91 us
    all_to_all x0 -> x3, blocking collectives: none -> 48.4 us  [the longest x2 34 us: columns_in(): lax.all_to_all(cut, 'seq', split_axis=2, concat_axis=0, tiled=True)[:, :, 0]]
  transfers between devices with their start and end apart: 10 -> 15, of which waited for: 9 -> 13; matrix products, arithmetic and copies ran while one was open for 8% -> 20% of each run, Pallas kernels for 0% -> 0%
where the time goes in v1:
time: 962 us; the launch traced here: 950 us
  waiting for transfers between devices  646 us (67%)
  matrix products  96.5 us (10%)
  local copies, waits for them, and re-layouts  95.9 us (10%)
  blocking collectives  48.4 us (5%)
  other arithmetic  42.2 us (4%)
  between operations  15.5 us (2%)
    reduce_scatter x4, waiting for transfers between devices, scatter_tokens(): lax.psum_scatter(partial.astype(LOW), 'seq', scatter_dimension=0, tiled=T...  190 us
    reduce_scatter x2, waiting for transfers between devices, columns_out(): mine = lax.psum_scatter(cut, 'dp', scatter_dimension=0)  121 us
    all_gather x4, waiting for transfers between devices, gather_tokens(): return lax.all_gather(rows, 'seq', axis=0, tiled=True)  120 us
    all_gather x2, waiting for transfers between devices, columns_in(): whole = lax.all_gather(mine, 'dp', axis=0)  114 us
    dot_general x12, matrix products, dot(): return lax.dot_general(a, b, (dims, ((), ())), preferred_element_type=WIDE)  83.4 us
    reduce_scatter x1, waiting for transfers between devices, local(): lax.psum_scatter(out_terms, 'dp', scatter_dimension=0, tiled=True)  66.2 us
    all_to_all x2, blocking collectives, columns_in(): lax.all_to_all(cut, 'seq', split_axis=2, concat_axis=0, tiled=True)[:, :, 0]  34 us
    all_gather x1, waiting for transfers between devices, local(): w_out = lax.all_gather(attn_weight[:, 3], 'dp', axis=0, tiled=True)  32.8 us
  transfers between devices with their start and end apart: 15, of which 13 were waited for; matrix products, arithmetic and copies ran while one was open for 20% of the time, Pallas kernels for 0%

profile of v1, /device:TPU:0, one launch (start us, length us, event | category | flops | bytes accessed | tf_op | source)
XLA Modules:
  0.0 949.5 jit_solution(12575539675633086863)
XLA Ops:
  9.0 12.3 %all_to_all.40 = bf16[16,3,8,256]{3,0,1,2:T(8,128)(2,1)} all-to-all(bf16[16,3,8,256]{3,0,1,2:T(8,128)(2,1)S(1)} %bitcast.190), channel_id=1, replica_groups=mesh['seq'=8,'dp'=16] {'seq'}, dimensions={2} | all-to-all | bytes 393216 | tf_op jit(solution)/shard_map/all_to_all | solution.py:39
  30.3 41.9 %all-gather.19.cloned.1.call-done = bf16[128,16,3,1,256]{4,1,3,2,0:T(8,128)(2,1)} async-done(((bf16[8,16,3,1,256]{4,1,3,2,0:T(8,128)(2,1)}), bf16[128,16,3,1,256]{4,1,3,2,0:T(8,128)(2,1)}) %all-gather.19.cloned.1.call-update) | async-done | bytes 3145744 | tf_op jit(solution)/shard_map/all_gather | solution.py:41
  78.3 47.5 %all-gather.11.cloned.1.call-done = bf16[1024,2048]{1,0:T(8,128)(2,1)} async-done(((bf16[128,2048]{1,0:T(8,128)(2,1)}), bf16[1024,2048]{1,0:T(8,128)(2,1)}) %all-gather.11.cloned.1.call-update) | async-done | bytes 4194320 | tf_op jit(solution)/shard_map/all_gather | solution.py:28
  125.8 5.7 convolution_convert_fusion.7
  139.7 32.8 %all-gather.21.cloned.1.call-done = bf16[256,1,2048]{2,0,1:T(8,128)(2,1)} async-done(((bf16[16,1,2048]{2,0,1:T(8,128)(2,1)}), bf16[256,1,2048]{2,0,1:T(8,128)(2,1)}) %all-gather.21.cloned.1.call-update) | async-done | bytes 1048592 | tf_op jit(solution)/shard_map/all_gather | solution.py:71
  179.5 21.7 %all_to_all.41 = bf16[16,3,8,688]{3,0,1,2:T(8,128)(2,1)} all-to-all(bf16[16,3,8,688]{3,0,1,2:T(8,128)(2,1)S(1)} %copy.113), channel_id=1, replica_groups=mesh['seq'=8,'dp'=16] {'seq'}, dimensions={2} | all-to-all | bytes 1056768 | tf_op jit(solution)/shard_map/all_to_all | solution.py:39
  201.2 34.0 %reduce-scatter.8.cloned.1.call-done = bf16[128,2048]{1,0:T(8,128)(2,1)} async-done(((bf16[1024,2048]{1,0:T(8,128)(2,1)}), bf16[128,2048]{1,0:T(8,128)(2,1)}) %reduce-scatter.8.cloned.1.call-update) | async-done | bytes 524304 | tf_op jit(solution)/shard_map/reduce_scatter | solution.py:32
  239.8 72.5 %all-gather.23.cloned.1.call-done = bf16[128,16,3,1,688]{4,1,3,2,0:T(8,128)(2,1)} async-done(((bf16[8,16,3,1,688]{4,1,3,2,0:T(8,128)(2,1)}), bf16[128,16,3,1,688]{4,1,3,2,0:T(8,128)(2,1)}) %all-gather.23.cloned.1.call-update) | async-done | bytes 8454160 | tf_op jit(solution)/shard_map/all_gather | solution.py:41
  312.3 8.4 copy.115
  320.7 5.8 slice.58
  326.5 8.4 copy.116
  335.0 29.7 %all-gather.13.cloned.1.call-done = bf16[1024,2048]{1,0:T(8,128)(2,1)} async-done(((bf16[128,2048]{1,0:T(8,128)(2,1)}), bf16[1024,2048]{1,0:T(8,128)(2,1)}) %all-gather.13.cloned.1.call-update) | async-done | bytes 4194320 | tf_op jit(solution)/shard_map/all_gather | solution.py:28
  364.7 10.8 %fusion.44 = f32[1024,1376]{0,1:T(8,128)} fusion(bf16[1024,2048]{1,0:T(8,128)(2,1)} %all-gather.13.cloned.1.call-done, bf16[2048,1376]{0,1:T(8,128)(2,1)} %bitcast.168), kind=kOutput, calls=%fused_computation.94 | convolution fusion | flops 5771362304 | bytes 15466496 | tf_op jit(solution)/shard_map/dot_general | solution.py:15
  375.5 42.8 %all-gather.15.cloned.1.call-done = bf16[1024,2048]{1,0:T(8,128)(2,1)} async-done(((bf16[128,2048]{1,0:T(8,128)(2,1)}), bf16[1024,2048]{1,0:T(8,128)(2,1)}) %all-gather.15.cloned.1.call-update) | async-done | bytes 4194320 | tf_op jit(solution)/shard_map/all_gather | solution.py:28
  418.3 9.1 multiply_convert_fusion.2
  429.0 8.6 convolution_convert_fusion.1
  437.9 51.8 %reduce-scatter.12.cloned.1.call-done = bf16[128,2048]{1,0:T(8,128)(2,1)} async-done(((bf16[1024,2048]{1,0:T(8,128)(2,1)}), bf16[128,2048]{1,0:T(8,128)(2,1)}) %reduce-scatter.12.cloned.1.call-update) | async-done | bytes 524304 | tf_op jit(solution)/shard_map/reduce_scatter | solution.py:32
  493.4 10.2 %convolution_convert_fusion = bf16[2048,1376]{0,1:T(8,128)(2,1)} fusion(bf16[1024,2048]{1,0:T(8,128)(2,1)} %all-gather.13.cloned.1.call-done, bf16[1024,688]{0,1:T(8,128)(2,1)} %copy-done.28, bf16[1024,688]{0,1:T(8,128)(2,1)} %copy-done.27), kind=kOutput, calls=%fused_computation.3 | convolution fusion | flops 5779816448 | bytes 12648448 | tf_op jit(solution)/shard_map/dot_general | solution.py:15
  503.6 8.3 copy.125
  512.0 6.6 convolution_convert_fusion.5
  523.2 15.4 %concatenate.24 = bf16[8,16,16,2,688]{4,3,2,1,0:T(2,128)(2,1)} reshape(bf16[2048,1376]{1,0:T(8,128)(2,1)} %copy.125) | data formatting | bytes 11272192 | tf_op jit(solution)/shard_map/concatenate | solution.py:121
  538.7 8.1 copy.127
  546.8 17.6 %maximum_bitcast_fusion = bf16[16,8,16,3,688]{4,3,2,0,1:T(4,128)(2,1)} fusion(bf16[8,16,16,1,688]{4,3,2,1,0:T(2,128)(2,1)S(1)} %copy.127, bf16[8,16,16,2,688]{4,3,2,1,0:T(2,128)(2,1)S(1)} %copy-done.2), kind=kLoop, calls=%fused_computation | loop fusion | flops 16908288 | bytes 16908288 | tf_op jit(solution)/shard_map/transpose | solution.py:49
  564.4 10.7 %copy.128 = bf16[16,8,16,3,688]{4,2,3,1,0:T(8,128)(2,1)} copy(bf16[16,8,16,3,688]{4,3,2,0,1:T(4,128)(2,1)} %maximum_bitcast_fusion) | data formatting | bytes 16908288 | tf_op jit(solution)/shard_map/transpose | solution.py:49
  601.6 7.8 convolution_convert_fusion.4
  610.8 7.7 convolution_convert_fusion.2
  618.5 62.8 %reduce-scatter.20.cloned.1.call-done = bf16[1,8,16,3,688]{4,2,3,1,0:T(8,128)(2,1)} async-done(((bf16[16,8,16,3,688]{4,2,3,1,0:T(8,128)(2,1)}), bf16[1,8,16,3,688]{4,2,3,1,0:T(8,128)(2,1)}) %reduce-scatter.20.cloned.1.call-update) | async-done | bytes 528400 | tf_op jit(solution)/shard_map/reduce_scatter | solution.py:50
  681.3 14.4 %all_to_all.42 = bf16[8,16,3,688]{3,1,2,0:T(8,128)(2,1)S(1)} all-to-all(bf16[8,16,3,688]{3,1,2,0:T(8,128)(2,1)} %bitcast.192), channel_id=1, replica_groups=mesh['seq'=8,'dp'=16] {'seq'}, dimensions={0} | all-to-all | bytes 1056768 | tf_op jit(solution)/shard_map/all_to_all | solution.py:51
  701.9 58.2 %reduce-scatter.16.cloned.1.call-done = bf16[1,8,16,3,256]{4,2,3,1,0:T(8,128)(2,1)} async-done(((bf16[16,8,16,3,256]{4,2,3,1,0:T(8,128)(2,1)}), bf16[1,8,16,3,256]{4,2,3,1,0:T(8,128)(2,1)}) %reduce-scatter.16.cloned.1.call-update) | async-done | bytes 196624 | tf_op jit(solution)/shard_map/reduce_scatter | solution.py:50
  764.5 66.2 %reduce-scatter.18.cloned.1.call-done = bf16[16,2048]{1,0:T(8,128)(2,1)} async-done(((bf16[256,2048]{1,0:T(8,128)(2,1)}), bf16[16,2048]{1,0:T(8,128)(2,1)}) %reduce-scatter.18.cloned.1.call-update) | async-done | bytes 65552 | tf_op jit(solution)/shard_map/reduce_scatter | solution.py:144
  833.5 51.6 %reduce-scatter.14.cloned.1.call-done = bf16[128,2048]{1,0:T(8,128)(2,1)} async-done(((bf16[1024,2048]{1,0:T(8,128)(2,1)}), bf16[128,2048]{1,0:T(8,128)(2,1)}) %reduce-scatter.14.cloned.1.call-update) | async-done | bytes 524304 | tf_op jit(solution)/shard_map/reduce_scatter | solution.py:32
  886.5 52.8 %reduce-scatter.10.cloned.1.call-done = bf16[128,2048]{1,0:T(8,128)(2,1)} async-done(((bf16[1024,2048]{1,0:T(8,128)(2,1)}), bf16[128,2048]{1,0:T(8,128)(2,1)}) %reduce-scatter.10.cloned.1.call-update) | async-done | bytes 524304 | tf_op jit(solution)/shard_map/reduce_scatter | solution.py:32
  (149 shorter events, 91.6 us)
Async XLA Ops:
  7.2 65.1 %all-gather.19.cloned.1.call-start = ((), (), s32[]{:S(2)}) async-start(), calls=%async_computation.22 | async-start | bytes 3342336 | tf_op jit(solution)/shard_map/all_gather | solution.py:41
  21.4 104.4 %all-gather.11.cloned.1.call-start = ((), (), s32[]{:S(2)}) async-start(), calls=%async_computation.11 | async-start | bytes 4718592 | tf_op jit(solution)/shard_map/all_gather | solution.py:28
  26.1 146.5 %all-gather.21.cloned.1.call-start = ((), (), s32[]{:S(2)}) async-start(), calls=%async_computation.23 | async-start | bytes 1114112 | tf_op jit(solution)/shard_map/all_gather | solution.py:71
  27.9 207.3 %reduce-scatter.8.cloned.1.call-start = ((), (), s32[]{:S(2)}) async-start(), calls=%async_computation.12 | async-start | bytes 4718592 | tf_op jit(solution)/shard_map/reduce_scatter | solution.py:32
  78.3 53.2 %copy-start.7 = (bf16[256,8,3,256]{3,1,2,0:T(8,128)(2,1)}, bf16[256,8,3,256]{3,1,2,0:T(8,128)(2,1)S(1)}, u32[]{:S(2)}) copy-start(bf16[256,8,3,256]{3,1,2,0:T(8,128)(2,1)S(1)} %copy.143) | copy-start | bytes 9437188
  177.1 58.1 %copy-start.1 = (bf16[1,128,2048]{2,1,0:T(8,128)(2,1)S(1)}, bf16[1,128,2048]{2,1,0:T(8,128)(2,1)}, u32[]{:S(2)}) copy-start(bf16[1,128,2048]{2,1,0:T(8,128)(2,1)} %param.8) | copy-start | bytes 1572868
  177.1 59.4 %copy-start.5 = (bf16[1,128,2048]{2,1,0:T(8,128)(2,1)S(1)}, bf16[1,128,2048]{2,1,0:T(8,128)(2,1)}, u32[]{:S(2)}) copy-start(bf16[1,128,2048]{2,1,0:T(8,128)(2,1)} %param.15) | copy-start | bytes 1572868
  177.2 135.1 %all-gather.23.cloned.1.call-start = ((), (), s32[]{:S(2)}) async-start(), calls=%async_computation.24 | async-start | bytes 10027008 | tf_op jit(solution)/shard_map/all_gather | solution.py:41
  177.2 61.7 %copy-start.20 = (f32[16]{0:T(128)}, f32[16]{0:T(128)S(1)}, u32[]{:S(2)}) copy-start(f32[16]{0:T(128)S(1)} %convert_element_type.161) | copy-start | bytes 196
  201.2 163.5 %all-gather.13.cloned.1.call-start = ((), (), s32[]{:S(2)}) async-start(), calls=%async_computation.13 | async-start | bytes 4718592 | tf_op jit(solution)/shard_map/all_gather | solution.py:28
  239.0 179.3 %all-gather.15.cloned.1.call-start = ((), (), s32[]{:S(2)}) async-start(), calls=%async_computation.15 | async-start | bytes 4718592 | tf_op jit(solution)/shard_map/all_gather | solution.py:28
  239.7 250.0 %reduce-scatter.12.cloned.1.call-start = ((), (), s32[]{:S(2)}) async-start(), calls=%async_computation.16 | async-start | bytes 4718592 | tf_op jit(solution)/shard_map/reduce_scatter | solution.py:32
  418.3 10.7 %copy-start.4 = (bf16[2048,2,688]{0,2,1:T(8,128)(2,1)S(1)}, bf16[2048,2,688]{0,2,1:T(8,128)(2,1)}, u32[]{:S(2)}) copy-start(bf16[2048,2,688]{0,2,1:T(8,128)(2,1)} %copy.116) | copy-start | bytes 16908292
  427.4 84.5 %copy-start.25 = (bf16[1024,688]{0,1:T(8,128)(2,1)}, bf16[1024,688]{0,1:T(8,128)(2,1)S(1)}, u32[]{:S(2)}) copy-start(bf16[1024,688]{0,1:T(8,128)(2,1)S(1)} %get-tuple-element.38) | copy-start | bytes 4227076
  437.6 52.0 %copy-start.3 = (bf16[128,2048]{1,0:T(8,128)(2,1)S(1)}, bf16[128,2048]{1,0:T(8,128)(2,1)}, u32[]{:S(2)}) copy-start(bf16[128,2048]{1,0:T(8,128)(2,1)} %reduce-scatter.8.cloned.1.call-done) | copy-start | bytes 1572868
  437.7 137.8 %all-gather.17.cloned.1.call-start = ((), (), s32[]{:S(2)}) async-start(), calls=%async_computation.17 | async-start | bytes 4718592 | tf_op jit(solution)/shard_map/all_gather | solution.py:28
  491.1 12.6 %copy-start.21 = (f32[128]{0:T(128)}, f32[128]{0:T(128)S(1)}, u32[]{:S(2)}) copy-start(f32[128]{0:T(128)S(1)} %broadcast_multiply_fusion.2) | copy-start | bytes 1540
  493.4 187.9 %reduce-scatter.20.cloned.1.call-start = ((), (), s32[]{:S(2)}) async-start(), calls=%async_computation.21 | async-start | bytes 10027008 | tf_op jit(solution)/shard_map/reduce_scatter | solution.py:50
  538.7 8.2 copy-start.2
  575.2 185.0 %reduce-scatter.16.cloned.1.call-start = ((), (), s32[]{:S(2)}) async-start(), calls=%async_computation.19 | async-start | bytes 3342336 | tf_op jit(solution)/shard_map/reduce_scatter | solution.py:50
  580.0 7.6 slice-start
  580.0 7.6 slice-start.1
  596.6 234.0 %reduce-scatter.18.cloned.1.call-start = ((), (), s32[]{:S(2)}) async-start(), calls=%async_computation.20 | async-start | bytes 1114112 | tf_op jit(solution)/shard_map/reduce_scatter | solution.py:144
  601.6 283.5 %reduce-scatter.14.cloned.1.call-start = ((), (), s32[]{:S(2)}) async-start(), calls=%async_computation.18 | async-start | bytes 4718592 | tf_op jit(solution)/shard_map/reduce_scatter | solution.py:32
  609.5 329.8 %reduce-scatter.10.cloned.1.call-start = ((), (), s32[]{:S(2)}) async-start(), calls=%async_computation.14 | async-start | bytes 4718592 | tf_op jit(solution)/shard_map/reduce_scatter | solution.py:32
  618.5 80.5 %copy-start.13 = (bf16[16,3,5504]{2,0,1:T(8,128)(2,1)S(1)}, bf16[16,3,5504]{2,0,1:T(8,128)(2,1)}, u32[]{:S(2)}) copy-start(bf16[16,3,5504]{2,0,1:T(8,128)(2,1)} %param.14) | copy-start | bytes 1585156
  696.5 135.1 %copy-start.10 = (bf16[16,4,2048]{2,1,0:T(4,128)(2,1)S(1)}, bf16[16,4,2048]{2,1,0:T(4,128)(2,1)}, u32[]{:S(2)}) copy-start(bf16[16,4,2048]{2,1,0:T(4,128)(2,1)} %param.12) | copy-start | bytes 786436
  696.5 135.1 %copy-start.19 = (f32[16]{0:T(128)S(1)}, f32[16]{0:T(128)}, u32[]{:S(2)}) copy-start(f32[16]{0:T(128)} %copy-done.18) | copy-start | bytes 196
  699.0 186.1 %copy-start.17 = (f32[128]{0:T(128)S(1)}, f32[128]{0:T(128)}, u32[]{:S(2)}) copy-start(f32[128]{0:T(128)} %copy-done.16) | copy-start | bytes 1540
  700.9 238.4 %copy-start.6 = (bf16[128,2048]{1,0:T(8,128)(2,1)S(1)}, bf16[128,2048]{1,0:T(8,128)(2,1)}, u32[]{:S(2)}) copy-start(bf16[128,2048]{1,0:T(8,128)(2,1)} %reduce-scatter.12.cloned.1.call-done) | copy-start | bytes 1572868
  700.9 238.4 %copy-start.22 = (f32[128]{0:T(128)S(1)}, f32[128]{0:T(128)}, u32[]{:S(2)}) copy-start(f32[128]{0:T(128)} %copy-done.21) | copy-start | bytes 1540
  760.2 71.3 %all-to-all-start.2 = ((bf16[8,16,3,256]{3,1,2,0:T(8,128)(2,1)}), bf16[8,16,3,256]{3,1,2,0:T(8,128)(2,1)S(1)}, u32[]{:S(2)}, u32[]{:S(2)}) async-start(bf16[8,16,3,256]{3,1,2,0:T(8,128)(2,1)} %bitcast.193), calls=%async_computation.7 | async-start | bytes 393216 | tf_op jit(solution)/shard_map/all_to_all | solution.py:51
  (15 other events, 38.9 us)
Sparse Core Ops, SparseCore 0:
  21.5 50.7 all-gather.18
  74.4 51.2 all-gather.10
  128.8 43.7 all-gather.20
  177.3 57.9 reduce-scatter.7
  237.6 74.6 all-gather.22
  314.4 50.2 all-gather.12
  366.9 51.3 all-gather.14
  437.8 51.8 reduce-scatter.11
  493.5 51.3 all-gather.16
  575.3 105.9 reduce-scatter.19
  685.9 74.2 reduce-scatter.15
  764.8 65.7 reduce-scatter.17
  833.0 52.0 reduce-scatter.13
  887.4 51.8 reduce-scatter.9

commit v2 on v1

v2 whole, which is shorter than its diff:
```python
import functools, math
import jax
import jax.numpy as jnp
from jax import lax
from jax.experimental import pallas as pl
from jax.experimental.pallas import tpu as pltpu
from jax.sharding import PartitionSpec as P

LOW = jnp.bfloat16
WIDE = jnp.float32
MESH = pl.DeviceIdType.MESH
EPS = 1e-05
HEAD_DIM = 128
ROWS = 128
MODEL = 2048
PART = 256
PROJ = 3 * PART
UNITS = 1408
SLAB = 3 * UNITS
PAIR = 2 * UNITS
FIRST = 80
MID = MODEL // 2


class Place:
    def __init__(self):
        self.seq, self.dp = lax.axis_index("seq"), lax.axis_index("dp")
        self.a, self.y = self.seq // 4, self.seq % 4
        self.b = 1 - self.a
        self.up, self.down, self.far = (self.y + 1) % 4, (self.y + 3) % 4, (self.y + 2) % 4
        self.z, self.h, self.core = self.dp // 4, self.dp // 2 % 2, self.dp % 2
        self.z_up, self.z_down, self.z_far = (self.z + 1) % 4, (self.z + 3) % 4, (self.z + 2) % 4
        self.x_dev = {"seq": self.b * 4 + self.y}
        self.up_dev = {"seq": self.a * 4 + self.up}
        self.down_dev = {"seq": self.a * 4 + self.down}
        self.h_dev = {"dp": self.member(self.z, 1 - self.h)}
        self.z_up_dev = {"dp": self.member(self.z_up, self.h)}
        self.z_down_dev = {"dp": self.member(self.z_down, self.h)}
        self.twin_dev = {"dp": self.dp + 1 - 2 * self.core}
        self.x = self.h * 2 + self.a
        self.x_up, self.x_down, self.x_far = (self.x + 1) % 4, (self.x + 3) % 4, (self.x + 2) % 4
        self.x_up_dev, self.x_down_dev = self.at_x(self.x_up), self.at_x(self.x_down)

    def member(self, z, h, twin=False):
        core = 1 - self.core if twin else self.core
        return z * 4 + h * 2 + core

    def at_x(self, x):
        return {"seq": x % 2 * 4 + self.y, "dp": self.member(self.z, x // 2)}

    def column(self, twin=False):
        return self.z * 4 + (1 - self.core if twin else self.core)

    def peers(self):
        return [{"seq": (self.seq + k) % 8} for k in range(1, 8)]


def enter(devices):
    barrier = pltpu.get_barrier_semaphore()
    for device in devices:
        pl.semaphore_signal(barrier, inc=1, device_id=device, device_id_type=MESH)
    pl.semaphore_wait(barrier, len(devices))


class Mail:
    def __init__(self, send, recv):
        self.send, self.recv = send, recv
        self.count, self.started = 0, {}

    def slots(self, n):
        first = self.count
        self.count += n
        return first

    def copy(self, slot, src, dst, device):
        return pltpu.make_async_remote_copy(
            src_ref=src, dst_ref=dst, send_sem=self.send.at[slot], recv_sem=self.recv.at[slot],
            device_id=device, device_id_type=MESH,
        )

    def go(self, slot, src, dst, device):
        copy = self.copy(slot, src, dst, device)
        copy.start()
        self.started[slot] = copy

    def arrived(self, slot, dst, device):
        self.copy(slot, dst, dst, device).wait_recv()

    def sent(self, slot):
        self.started.pop(slot).wait_send()

    def finish(self):
        for copy in self.started.values():
            copy.wait_send()


def gather_seq(me, mail, x_ref, out_ref):
    a, b, y, up, down, far = me.a, me.b, me.y, me.up, me.down, me.far
    XP, U, D = me.x_dev, me.up_dev, me.down_dev
    n = mail.slots(18)

    def cut(ref, rows, half):
        lo, hi = ((0, FIRST), (FIRST, ROWS))[rows]
        return ref.at[lo:hi] if half is None else ref.at[lo:hi, half * MID : half * MID + MID]

    def at(col, row, rows, half=None):
        return cut(out_ref.at[col * 4 + row], rows, half)

    def send(i, rows, dev):
        mail.go(n + i, cut(x_ref, rows, None), at(a, y, rows), dev)

    def fwd(i, ref, dev):
        mail.go(n + i, ref, ref, dev)

    def got(i, dst):
        mail.arrived(n + i, dst, XP)

    send(0, 0, XP)
    send(1, 0, U)
    send(2, 0, D)
    send(3, 1, U)
    send(4, 1, D)
    send(5, 1, XP)
    yield
    got(0, at(b, y, 0))
    fwd(6, at(b, y, 0), U)
    fwd(7, at(b, y, 0), D)
    yield
    got(1, at(a, down, 0))
    fwd(8, at(a, down, 0, 0), U)
    got(2, at(a, up, 0))
    fwd(9, at(a, up, 0, 1), D)
    yield
    got(3, at(a, down, 1))
    fwd(10, at(a, down, 1, 0), U)
    fwd(11, at(a, down, 1), XP)
    got(4, at(a, up, 1))
    fwd(12, at(a, up, 1, 1), D)
    fwd(13, at(a, up, 1), XP)
    yield
    got(5, at(b, y, 1))
    got(6, at(b, down, 0))
    fwd(14, at(b, down, 0, 0), U)
    got(7, at(b, up, 0))
    fwd(15, at(b, up, 0, 1), D)
    yield
    got(10, at(a, far, 1, 0))
    fwd(16, at(a, far, 1, 0), XP)
    got(12, at(a, far, 1, 1))
    fwd(17, at(a, far, 1, 1), XP)
    yield
    got(8, at(a, far, 0, 0))
    got(9, at(a, far, 0, 1))
    got(11, at(b, down, 1))
    got(13, at(b, up, 1))
    yield
    got(14, at(b, far, 0, 0))
    got(15, at(b, far, 0, 1))
    got(16, at(b, far, 1, 0))
    got(17, at(b, far, 1, 1))


def gather_y(me, mail, x_ref, out_ref):
    y, up, down, far = me.y, me.up, me.down, me.far
    U, D = me.up_dev, me.down_dev
    n = mail.slots(4)
    H = ROWS // 2
    mail.go(n, x_ref, out_ref.at[y], U)
    mail.go(n + 1, x_ref, out_ref.at[y], D)
    yield
    mail.arrived(n, out_ref.at[down], D)
    mail.go(n + 2, out_ref.at[down, 0:H], out_ref.at[down, 0:H], U)
    mail.arrived(n + 1, out_ref.at[up], U)
    mail.go(n + 3, out_ref.at[up, H:ROWS], out_ref.at[up, H:ROWS], D)
    yield
    mail.arrived(n + 2, out_ref.at[far, 0:H], D)
    mail.arrived(n + 3, out_ref.at[far, H:ROWS], U)


def scatter_y(me, mail, part, p2, p1, out):
    y, up, down, far = me.y, me.up, me.down, me.far
    U, D = me.up_dev, me.down_dev
    n = mail.slots(6)
    H = ROWS // 2
    mail.go(n + 2, part.at[up, H:ROWS], p1.at[0, H:ROWS], U)
    mail.go(n + 3, part.at[down, 0:H], p1.at[1, 0:H], D)
    yield
    mail.go(n, part.at[far, 0:H], p2.at[0], U)
    mail.go(n + 1, part.at[far, H:ROWS], p2.at[1], D)
    yield
    mail.arrived(n, p2.at[0], D)
    add(part.at[up, 0:H], p2.at[0])
    mail.go(n + 4, part.at[up, 0:H], p1.at[0, 0:H], U)
    mail.arrived(n + 1, p2.at[1], U)
    add(part.at[down, H:ROWS], p2.at[1])
    mail.go(n + 5, part.at[down, H:ROWS], p1.at[1, H:ROWS], D)
    yield
    mail.arrived(n + 2, p1.at[0, H:ROWS], D)
    mail.arrived(n + 5, p1.at[1, H:ROWS], U)
    out(H, ROWS, val(part.at[y, H:ROWS]) + val(p1.at[0, H:ROWS]) + val(p1.at[1, H:ROWS]))
    mail.arrived(n + 3, p1.at[1, 0:H], U)
    mail.arrived(n + 4, p1.at[0, 0:H], D)
    out(0, H, val(part.at[y, 0:H]) + val(p1.at[0, 0:H]) + val(p1.at[1, 0:H]))


def val(ref):
    return ref[...].astype(WIDE)


def add(dst, src):
    dst[...] = (val(dst) + val(src)).astype(LOW)


def swap_seq(me, mail, own_ref, all_ref, lo, hi):
    n = mail.slots(7)
    for k in range(1, 8):
        to = (me.seq + k) % 8
        mail.go(n + k - 1, own_ref.at[to, :, lo:hi], all_ref.at[me.seq, me.dp, :, lo:hi], {"seq": to})
    yield
    for k in range(1, 8):
        came = (me.seq + 8 - k) % 8
        mail.arrived(n + k - 1, all_ref.at[came, me.dp, :, lo:hi], me.x_dev)


def gather_dp(me, mail, ref):
    z, h = me.z, me.h
    n = mail.slots(19)
    HD, ZU, ZD, TW = me.h_dev, me.z_up_dev, me.z_down_dev, me.twin_dev

    def at(zz, hh, half=None, twin=False):
        d = me.member(zz, hh, twin)
        return ref.at[:, d] if half is None else ref.at[4 * half : 4 * half + 4, d]

    def fwd(i, r, dev):
        mail.go(n + i, r, r, dev)

    def got(i, r):
        mail.arrived(n + i, r, TW)

    hs = (h, 1 - h)
    fwd(0, at(z, h), HD)
    fwd(1, at(z, h), ZU)
    fwd(2, at(z, h), ZD)
    fwd(9, at(z, h), TW)
    yield
    got(0, at(z, 1 - h))
    fwd(3, at(z, 1 - h), ZU)
    fwd(4, at(z, 1 - h), ZD)
    fwd(10, at(z, 1 - h), TW)
    yield
    for k in range(2):
        got(1 + 2 * k, at(me.z_down, hs[k]))
        fwd(5 + 2 * k, at(me.z_down, hs[k], 0), ZU)
        fwd(11 + 2 * k, at(me.z_down, hs[k]), TW)
        yield
        got(2 + 2 * k, at(me.z_up, hs[k]))
        fwd(6 + 2 * k, at(me.z_up, hs[k], 1), ZD)
        fwd(12 + 2 * k, at(me.z_up, hs[k]), TW)
        yield
    for k in range(2):
        got(5 + 2 * k, at(me.z_far, hs[k], 0))
        fwd(15 + 2 * k, at(me.z_far, hs[k], 0), TW)
        got(6 + 2 * k, at(me.z_far, hs[k], 1))
        fwd(16 + 2 * k, at(me.z_far, hs[k], 1), TW)
        yield
    got(9, at(z, h, twin=True))
    got(10, at(z, 1 - h, twin=True))
    for k in range(2):
        got(11 + 2 * k, at(me.z_down, hs[k], twin=True))
        got(12 + 2 * k, at(me.z_up, hs[k], twin=True))
        got(15 + 2 * k, at(me.z_far, hs[k], 0, twin=True))
        got(16 + 2 * k, at(me.z_far, hs[k], 1, twin=True))


def swap_y(me, mail, own_ref, all_ref):
    n = mail.slots(3)
    for k in (2, 1, 3):
        to = (me.y + k) % 4
        mail.go(n + k - 1, own_ref.at[to], all_ref.at[me.seq, me.dp], {"seq": me.a * 4 + to})
    yield
    for k in (1, 3, 2):
        came = me.a * 4 + (me.y + 4 - k) % 4
        mail.arrived(n + k - 1, all_ref.at[came, me.dp], me.up_dev)


def slab(me, ref, x, z, half=None, twin=False):
    d = me.member(z, x // 2, twin)
    first = x % 2 * 4
    return ref.at[pl.ds(first, 4), d] if half is None else ref.at[pl.ds(first + 2 * half, 2), d]


def gather_xz(me, mail, ref):
    n = mail.slots(36)
    XU, XD, ZU, ZD, TW = me.x_up_dev, me.x_down_dev, me.z_up_dev, me.z_down_dev, me.twin_dev
    z, zu, zd, zf = me.z, me.z_up, me.z_down, me.z_far
    xs = (me.x, me.x_down, me.x_up, me.x_far)

    def at(x, zz, half=None, twin=False):
        return slab(me, ref, x, zz, half, twin)

    def fwd(i, r, dev):
        mail.go(n + i, r, r, dev)

    def got(i, r):
        mail.arrived(n + i, r, TW)

    def z_first(k):
        fwd(4 + 4 * k, at(xs[k], z), ZU)
        fwd(5 + 4 * k, at(xs[k], z), ZD)
        fwd(20 + 4 * k, at(xs[k], z), TW)

    def z_second(k):
        got(4 + 4 * k, at(xs[k], zd))
        fwd(6 + 4 * k, at(xs[k], zd, 0), ZU)
        fwd(21 + 4 * k, at(xs[k], zd), TW)
        got(5 + 4 * k, at(xs[k], zu))
        fwd(7 + 4 * k, at(xs[k], zu, 1), ZD)
        fwd(22 + 4 * k, at(xs[k], zu), TW)

    def z_third(k):
        got(6 + 4 * k, at(xs[k], zf, 0))
        got(7 + 4 * k, at(xs[k], zf, 1))
        fwd(23 + 4 * k, at(xs[k], zf), TW)

    fwd(0, at(me.x, z), XU)
    fwd(1, at(me.x, z), XD)
    z_first(0)
    yield
    got(0, at(me.x_down, z))
    fwd(2, at(me.x_down, z, 0), XU)
    got(1, at(me.x_up, z))
    fwd(3, at(me.x_up, z, 1), XD)
    z_first(1)
    z_first(2)
    yield
    z_second(0)
    yield
    got(2, at(me.x_far, z, 0))
    got(3, at(me.x_far, z, 1))
    z_first(3)
    yield
    z_second(1)
    yield
    z_third(0)
    z_second(2)
    yield
    z_third(1)
    yield
    z_second(3)
    z_third(2)
    yield
    z_third(3)
    yield
    for k in range(4):
        for i, zz in enumerate((z, zd, zu, zf)):
            got(20 + 4 * k + i, at(xs[k], zz, twin=True))


def add_slabs(dst, *sources):
    def one(i, carry):
        total = val(dst.at[i])
        for source in sources:
            total = total + val(source.at[i])
        dst[i] = total.astype(LOW)
        return carry

    lax.fori_loop(0, dst.shape[0], one, 0)


def halved(ref, half):
    k = ref.shape[0] // 2
    return ref.at[half * k : half * k + k]


class RingSum:
    def __init__(self, mail, at, places, devices, over, near):
        self.mail, self.at, self.places, self.devices = mail, at, places, devices
        self.over, self.near = over, near
        self.n = mail.slots(6)

    def first(self):
        own, up, down, far = self.places
        U, D = self.devices
        go, n = self.mail.go, self.n
        go(n, halved(self.at(far), 0), self.over.at[0], U)
        go(n + 1, halved(self.at(far), 1), self.over.at[1], D)
        go(n + 2, halved(self.at(up), 1), halved(self.near.at[0], 1), U)
        go(n + 3, halved(self.at(down), 0), halved(self.near.at[1], 0), D)

    def second(self):
        own, up, down, far = self.places
        U, D = self.devices
        go, got, n = self.mail.go, self.mail.arrived, self.n
        got(n, self.over.at[0], D)
        add_slabs(halved(self.at(up), 0), self.over.at[0])
        go(n + 4, halved(self.at(up), 0), halved(self.near.at[0], 0), U)
        got(n + 1, self.over.at[1], U)
        add_slabs(halved(self.at(down), 1), self.over.at[1])
        go(n + 5, halved(self.at(down), 1), halved(self.near.at[1], 1), D)

    def third(self):
        own = self.places[0]
        U, D = self.devices
        got, n = self.mail.arrived, self.n
        got(n + 2, halved(self.near.at[0], 1), D)
        got(n + 3, halved(self.near.at[1], 0), U)
        got(n + 4, halved(self.near.at[0], 0), D)
        got(n + 5, halved(self.near.at[1], 1), U)
        add_slabs(self.at(own), self.near.at[0], self.near.at[1])


def twin_sum(me, mail, stage, acc, order, product):
    slots = stage.shape[0]
    n = mail.slots(len(order))

    def settle(i):
        mail.arrived(n + i, acc.at[order[i]], me.twin_dev)
        add_slabs(acc.at[order[i]], stage.at[i % slots, :, me.core])

    for i, s in enumerate(order):
        if i >= slots:
            mail.sent(n + i - slots)
        product(s, stage.at[i % slots])
        mail.go(n + i, stage.at[i % slots, :, 1 - me.core], acc.at[s], me.twin_dev)
        if i > 0:
            settle(i - 1)
        yield
    settle(len(order) - 1)
    for i in range(max(0, len(order) - slots), len(order)):
        mail.sent(n + i)


def scatter_xz(me, mail, acc, z_over, z_near, x_over, x_near):
    xs = (me.x_far, me.x, me.x_up, me.x_down)
    zs = (me.z, me.z_up, me.z_down, me.z_far)
    XU, XD, ZU, ZD = me.x_up_dev, me.x_down_dev, me.z_up_dev, me.z_down_dev

    def at(x):
        return lambda z: acc.at[pl.ds(x % 2 * 4, 4), z * 2 + x // 2]

    rings = [RingSum(mail, at(x), zs, (ZU, ZD), z_over.at[k], z_near.at[k]) for k, x in enumerate(xs)]
    ring = RingSum(mail, lambda x: at(x)(me.z), (me.x, me.x_up, me.x_down, me.x_far), (XU, XD), x_over, x_near)
    rings[0].first()
    yield
    rings[2].first()
    rings[3].first()
    rings[1].first()
    yield
    for k in (0, 2, 3, 1):
        rings[k].second()
        yield
    for k in (0, 2, 3):
        rings[k].third()
        yield
    ring.first()
    yield
    rings[1].third()
    yield
    ring.second()
    yield
    ring.third()


def scatter_hz(me, mail, acc, z_over, z_near, h_near):
    hs = (1 - me.h, me.h)
    zs = (me.z, me.z_up, me.z_down, me.z_far)

    def at(h):
        return lambda z: acc.at[:, z * 2 + h]

    rings = [RingSum(mail, at(h), zs, (me.z_up_dev, me.z_down_dev), z_over.at[k], z_near.at[k]) for k, h in enumerate(hs)]
    n = mail.slots(1)
    rings[0].first()
    rings[1].first()
    yield
    for k in range(2):
        rings[k].second()
        yield
    rings[0].third()
    mail.go(n, at(1 - me.h)(me.z), h_near, me.h_dev)
    yield
    rings[1].third()
    yield
    mail.arrived(n, h_near, me.h_dev)
    add_slabs(at(me.h)(me.z), h_near)


def send_y(me, mail, slab, result):
    n = mail.slots(3)
    for k in (2, 1, 3):
        to = (me.y + k) % 4
        mail.go(n + k - 1, slab.at[to], result.at[me.y], {"seq": me.a * 4 + to})
    result[me.y] = slab[me.y]
    yield
    for k in (1, 3, 2):
        mail.arrived(n + k - 1, result.at[(me.y + 4 - k) % 4], me.up_dev)


def send_seq(me, mail, slab, result, lo, hi):
    n = mail.slots(7)
    for k in range(1, 8):
        to = (me.seq + k) % 8
        mail.go(n + k - 1, slab.at[to, :, lo:hi], result.at[me.seq], {"seq": to})
    result[me.seq] = slab[me.seq, :, lo:hi]
    yield
    for k in range(1, 8):
        mail.arrived(n + k - 1, result.at[(me.seq + 8 - k) % 8], me.x_dev)


def scatter_bufs():
    late = ROWS - FIRST
    shapes = ((4, late, MODEL), (2, late, MID), (2, late, MODEL), (4, FIRST, MID), (4, FIRST, MODEL), (1, FIRST, MODEL))
    return [pltpu.VMEM(shape, LOW) for shape in shapes]


def scatter_seq(me, mail, part, bufs, out):
    a, b, y, up, down, far = me.a, me.b, me.y, me.up, me.down, me.far
    XP, U, D = me.x_dev, me.up_dev, me.down_dev
    qx, q2, q1, p2, p1, px = bufs
    n = mail.slots(23)
    halves = (pl.ds(0, MID), pl.ds(MID, MID))

    def go(i, src, dst, dev):
        mail.go(n + i, src, dst, dev)

    def got(i, dst):
        mail.arrived(n + i, dst, XP)

    def at(col, row, rows, half=None):
        lo, hi = ((0, FIRST), (FIRST, ROWS))[rows]
        ref = part.at[col * 4 + row]
        return ref.at[lo:hi] if half is None else ref.at[lo:hi, halves[half]]

    def lane(ref, k, half):
        return ref.at[k, :, halves[half]]

    for k, row in enumerate((far, down, up, y)):
        go(k, at(b, row, 1), qx.at[row], XP)
    cols = (b, a)

    def p_first(k):
        c, s = cols[k], 10 + 6 * k
        go(s, at(c, far, 0, 0), p2.at[2 * k], U)
        go(s + 1, at(c, far, 0, 1), p2.at[2 * k + 1], D)
        go(s + 2, at(c, up, 0, 1), lane(p1, 2 * k, 1), U)
        go(s + 3, at(c, down, 0, 0), lane(p1, 2 * k + 1, 0), D)

    def p_second(k):
        c, s = cols[k], 10 + 6 * k
        got(s, p2.at[2 * k])
        add(at(c, up, 0, 0), p2.at[2 * k])
        go(s + 4, at(c, up, 0, 0), lane(p1, 2 * k, 0), U)
        got(s + 1, p2.at[2 * k + 1])
        add(at(c, down, 0, 1), p2.at[2 * k + 1])
        go(s + 5, at(c, down, 0, 1), lane(p1, 2 * k + 1, 1), D)

    def p_third(k):
        s = 10 + 6 * k
        got(s + 2, lane(p1, 2 * k, 1))
        got(s + 3, lane(p1, 2 * k + 1, 0))
        got(s + 4, lane(p1, 2 * k, 0))
        got(s + 5, lane(p1, 2 * k + 1, 1))
        return val(at(cols[k], y, 0)) + val(p1.at[2 * k]) + val(p1.at[2 * k + 1])

    p_first(0)
    yield
    p_first(1)
    yield
    got(0, qx.at[far])
    add(at(a, far, 1), qx.at[far])
    go(4, at(a, far, 1, 0), q2.at[0], U)
    go(5, at(a, far, 1, 1), q2.at[1], D)
    yield
    p_second(0)
    yield
    got(1, qx.at[down])
    add(at(a, down, 1), qx.at[down])
    go(6, at(a, down, 1, 0), lane(q1, 1, 0), D)
    got(2, qx.at[up])
    add(at(a, up, 1), qx.at[up])
    go(7, at(a, up, 1, 1), lane(q1, 0, 1), U)
    yield
    p_second(1)
    yield
    rows = p_third(0)
    own = at(b, y, 0)
    own[...] = rows.astype(LOW)
    go(22, own, px.at[0], XP)
    yield
    got(4, q2.at[0])
    add(at(a, up, 1, 0), q2.at[0])
    go(8, at(a, up, 1, 0), lane(q1, 0, 0), U)
    got(5, q2.at[1])
    add(at(a, down, 1, 1), q2.at[1])
    go(9, at(a, down, 1, 1), lane(q1, 1, 1), D)
    yield
    rows = p_third(1)
    got(22, px.at[0])
    out(0, FIRST, rows + val(px.at[0]))
    yield
    got(3, qx.at[y])
    got(6, lane(q1, 1, 0))
    got(7, lane(q1, 0, 1))
    got(8, lane(q1, 0, 0))
    got(9, lane(q1, 1, 1))
    out(FIRST, ROWS, val(at(a, y, 1)) + val(qx.at[y]) + val(q1.at[0]) + val(q1.at[1]))


def run(*tasks):
    tasks = list(tasks)
    while tasks:
        for task in list(tasks):
            if next(task, tasks) is tasks:
                tasks.remove(task)


def step(task):
    return next(task, None)
def dot(a, b, dims=((1,), (0,))):
    return lax.dot_general(a, b, (dims, ((), ())), preferred_element_type=WIDE)


def row_scale(values):
    return lax.rsqrt(jnp.mean(values * values, axis=-1, keepdims=True) + EPS)


def front_kernel(
    x_ref, live_ref, cot_ref, wa_own, wm_own, pos_q, pos_k,
    one_out, wa_out, grad_all, wm, qkv_out, probs_out, att_out, resid, two,
    one_all, wa, grad_own, qkv, probs, att, part, qx, q2, q1, p2, p1, px, send, recv, local_sem,
):
    me = Place()
    mail = Mail(send, recv)
    saves = []

    def save(src, dst):
        copy = pltpu.make_async_copy(src, dst, local_sem.at[len(saves)])
        copy.start()
        saves.append(copy)
        return copy

    enter(me.peers() + [me.h_dev, me.z_up_dev, me.z_down_dev, me.twin_dev, me.x_up_dev, me.x_down_dev])
    swap_a = swap_seq(me, mail, wa_own, wa, 0, PROJ)
    step(swap_a)
    x = x_ref[...].astype(WIDE)
    one_all[me.seq] = (x * row_scale(x) * live_ref[...]).astype(LOW)
    gather_one = gather_seq(me, mail, one_all.at[me.seq], one_all)
    step(gather_one)
    wa[pl.ds(me.seq, 1), pl.ds(me.dp, 1), :, 0:PROJ] = wa_own[pl.ds(me.seq, 1), :, 0:PROJ][None]
    for k in range(8):
        wa[k, pl.ds(me.dp, 1), :, PROJ:] = wa_own[k, :, PROJ:][None]
    step(swap_a)
    gather_wa = gather_dp(me, mail, wa)
    step(gather_wa)
    swap_m = swap_y(me, mail, wm_own, wm)
    step(swap_m)
    keep_m = save(wm_own.at[me.y], wm.at[me.seq, me.dp])
    grad_own[...] = (cot_ref[...].astype(WIDE) * live_ref[...]).astype(LOW)
    save(grad_own, grad_all.at[me.y])
    for i in range(3):
        step(gather_one)
        step(gather_wa)
    step(swap_m)
    keep_m.wait()
    gather_wm = gather_xz(me, mail, wm)
    step(gather_wm)
    run(gather_one, gather_wa)
    gather_g = gather_y(me, mail, grad_own, grad_all)
    step(gather_g)
    save(one_all, one_out)
    save(wa, wa_out)

    def project(i, carry):
        rows = one_all[pl.ds(i * 2, 2)].reshape(2 * ROWS, MODEL)
        weight = wa[:, :, :, 0:PROJ].reshape(MODEL, PROJ)
        qkv[pl.ds(pl.multiple_of(i * 256, 256), 256), :] = dot(rows, weight).astype(LOW)
        return carry

    def attend(i, carry):
        first = pl.multiple_of(i * ROWS, ROWS)
        rows = pl.ds(first, ROWS)
        allowed = pos_k[...] <= pos_q[rows, :]
        for head in range(2):
            lo, hi = head * HEAD_DIM, (head + 1) * HEAD_DIM
            q = qkv[rows, lo:hi]
            k = qkv[:, PART + lo : PART + hi]
            v = qkv[:, 2 * PART + lo : 2 * PART + hi]
            scores = dot(q, k, ((1,), (1,))) * (1.0 / math.sqrt(HEAD_DIM)) - math.log(8 * ROWS)
            p = jnp.where(allowed, 1.0 / (1.0 + jnp.exp(-scores)), 0.0).astype(LOW)
            probs[head, rows, :] = p
            att[rows, lo:hi] = dot(p, v).astype(LOW)
        return carry

    def out_project(col):
        rows = att[pl.ds(pl.multiple_of(col * 512, 512), 512), :]

        def piece(k, carry):
            weight = wa[k, :, :, PROJ:].reshape(PART, PART)
            columns = pl.ds(pl.multiple_of(k * PART, PART), PART)
            part[pl.ds(col * 4, 4), :, columns] = dot(rows, weight).reshape(4, ROWS, PART).astype(LOW)
            return carry

        lax.fori_loop(0, 8, piece, 0)

    for i in range(2):
        lax.fori_loop(2 * i, 2 * i + 2, project, 0)
        step(gather_g)
        step(gather_wm)
    save(qkv, qkv_out)

    def write(lo, hi, rows):
        total = x_ref[lo:hi].astype(WIDE) + rows
        resid[lo:hi] = total
        two[lo:hi] = (total * row_scale(total) * live_ref[lo:hi]).astype(LOW)

    scatter = scatter_seq(me, mail, part, (qx, q2, q1, p2, p1, px), write)
    for col in (me.b, me.a):
        for i in range(2):
            lax.fori_loop(col * 4 + 2 * i, col * 4 + 2 * i + 2, attend, 0)
            step(gather_wm)
            step(gather_g)
        out_project(col)
        step(scatter)
    save(probs, probs_out)
    save(att, att_out)
    run(scatter, gather_wm, gather_g)
    for copy in saves:
        if copy is not keep_m:
            copy.wait()
    mail.finish()


def front(x, live, cot, wa_own, wm_own, pos):
    vmem, anywhere = pl.BlockSpec(memory_space=pltpu.VMEM), pl.BlockSpec(memory_space=pl.ANY)
    shape = jax.ShapeDtypeStruct
    count = 7 + 18 + 19 + 3 + 36 + 4 + 23
    return pl.pallas_call(
        front_kernel,
        out_shape=(
            shape((8, ROWS, MODEL), LOW), shape((8, 16, 16, 1024), LOW), shape((4, ROWS, MODEL), LOW),
            shape((8, 16, 16, SLAB), LOW), shape((1024, PROJ), LOW), shape((2, 1024, 1024), LOW),
            shape((1024, PART), LOW), shape((ROWS, MODEL), WIDE), shape((ROWS, MODEL), LOW),
        ),
        in_specs=[vmem] * 4 + [anywhere] + [vmem] * 2,
        out_specs=(anywhere,) * 7 + (vmem, vmem),
        scratch_shapes=[
            pltpu.VMEM((8, ROWS, MODEL), LOW), pltpu.VMEM((8, 16, 16, 1024), LOW), pltpu.VMEM((ROWS, MODEL), LOW),
            pltpu.VMEM((1024, PROJ), LOW), pltpu.VMEM((2, 1024, 1024), LOW), pltpu.VMEM((1024, PART), LOW),
            pltpu.VMEM((8, ROWS, MODEL), LOW),
        ]
        + scatter_bufs()
        + [pltpu.SemaphoreType.DMA((count,)), pltpu.SemaphoreType.DMA((count,)), pltpu.SemaphoreType.DMA((8,))],
        compiler_params=pltpu.CompilerParams(collective_id=1, has_side_effects=True, vmem_limit_bytes=56 * 2**20),
        name="front",
    )(x, live, cot, wa_own, wm_own, pos[:, None], pos[None, :])
def mlp_kernel(
    two_ref, resid, cot_ref, live_ref, grad_all, wm_all,
    two_out, hidden_out, pair_out, branch_out, grad_resid, grad_branch,
    down_own,
    wm, grads, twos, hidden, pair, part, branch, p2, p1,
    stage, acc, z_over, z_near, x_over, x_near, send, recv, local_sem,
):
    me = Place()
    mail = Mail(send, recv)
    saves = []

    def save(src, dst):
        copy = pltpu.make_async_copy(src, dst, local_sem.at[len(saves)])
        copy.start()
        saves.append(copy)
        return copy

    load_w = save(wm_all, wm)
    load_g = save(grad_all, grads)
    others = [{"seq": me.a * 4 + (me.y + k) % 4} for k in (1, 2, 3)]
    enter(others + [me.x_up_dev, me.x_down_dev, me.z_up_dev, me.z_down_dev, me.twin_dev])
    twos[me.y] = two_ref[...]
    gather = gather_y(me, mail, twos.at[me.y], twos)
    step(gather)
    load_w.wait()
    load_g.wait()

    def rows_of(ref, blocks):
        return jnp.concatenate([ref[k] for k in blocks], axis=0)

    def put(ref, blocks, columns, values):
        for i, k in enumerate(blocks):
            ref[k, :, columns] = values[i * ROWS : (i + 1) * ROWS].astype(LOW)

    def hidden_tile(blocks, j, wide):
        start = j * 128
        if not isinstance(j, int):
            start = pl.multiple_of(start, 128)
        width = wide * 128
        weight = wm[:, :, :, pl.ds(2 * start, 2 * width)].reshape(MODEL, 2 * width)
        gate_up = dot(rows_of(twos, blocks), weight)
        down = wm[:, :, :, pl.ds(PAIR + start, width)].reshape(MODEL, width)
        grad_hidden = dot(rows_of(grads, blocks), down)
        low, pairs = [], []
        for i in range(wide):
            gate = gate_up[:, i * 256 : i * 256 + 128]
            up = gate_up[:, i * 256 + 128 : i * 256 + 256]
            back = grad_hidden[:, i * 128 : i * 128 + 128]
            squashed = 1.0 / (1.0 + jnp.exp(-gate))
            active = gate * squashed
            low.append(active * up)
            pairs.append(back * up * (squashed * (1.0 + gate * (1.0 - squashed))))
            pairs.append(back * active)
        put(hidden, blocks, pl.ds(start, width), jnp.concatenate(low, axis=1))
        put(pair, blocks, pl.ds(2 * start, 2 * width), jnp.concatenate(pairs, axis=1))

    def ahead(blocks):
        def tile(j, carry):
            hidden_tile(blocks, 2 * j, 2)
            return carry

        lax.fori_loop(0, 5, tile, 0)
        hidden_tile(blocks, 10, 1)

    def back(blocks):
        def tile(s, carry):
            columns = pl.ds(pl.multiple_of(s * 256, 256), 256)
            weight = wm[s, :, :, 0:PAIR].reshape(256, PAIR)
            put(part, blocks, columns, dot(rows_of(pair, blocks), weight, ((1,), (1,))))
            return carry

        lax.fori_loop(0, 8, tile, 0)

    def down_back(blocks):
        def tile(s, carry):
            columns = pl.ds(pl.multiple_of(s * 256, 256), 256)
            weight = wm[s, :, :, PAIR:].reshape(256, UNITS)
            put(branch, blocks, columns, dot(rows_of(hidden, blocks), weight, ((1,), (1,))))
            return carry

        lax.fori_loop(0, 8, tile, 0)

    def write(lo, hi, rows):
        x = resid[lo:hi]
        scale = row_scale(x)
        hat = x * scale
        inner = jnp.mean(rows * hat, axis=-1, keepdims=True)
        total = cot_ref[lo:hi].astype(WIDE) * live_ref[lo:hi] + scale * (rows - hat * inner)
        grad_resid[lo:hi] = total
        grad_branch[lo:hi] = total.astype(LOW)

    scatter = scatter_y(me, mail, part, p2, p1, write)
    ahead([me.y])
    step(gather)
    ahead([me.up, me.down])
    back([me.up, me.down])
    step(scatter)
    step(gather)
    ahead([me.far])
    back([me.far])
    step(scatter)
    save(twos, two_out)
    save(hidden, hidden_out)
    save(pair, pair_out)
    back([me.y])
    step(scatter)
    order = [me.a * 4 + i for i in range(4)] + [me.b * 4 + i for i in range(4)]

    def down_product(s, out):
        rows = grads[:, :, pl.ds(pl.multiple_of(s * 256, 256), 256)].reshape(4 * ROWS, 256)

        def tile(j, carry):
            columns = pl.ds(pl.multiple_of(j * 128, 128), 128)
            terms = dot(rows, hidden[:, :, columns].reshape(4 * ROWS, 128), ((0,), (0,)))
            out[:, :, :, columns] = terms.reshape(8, 2, 16, 128).astype(LOW)
            return carry

        lax.fori_loop(0, UNITS // 128, tile, 0)

    twin = twin_sum(me, mail, stage, acc, order, down_product)
    for i in range(4):
        step(twin)
    step(scatter)
    step(twin)
    sums = scatter_xz(me, mail, acc, z_over, z_near, x_over, x_near)
    step(sums)
    run(twin)
    step(sums)
    step(scatter)
    every = [me.y, me.up, me.down, me.far]
    down_back(every)
    save(branch, branch_out)
    run(scatter, gather, sums)
    run(send_y(me, mail, acc.at[pl.ds(me.a * 4, 4), me.z * 2 + me.h], down_own))
    for copy in saves[2:]:
        copy.wait()
    mail.finish()


def mlp(two, resid, cot, live, grad_all, wm):
    vmem, anywhere = pl.BlockSpec(memory_space=pltpu.VMEM), pl.BlockSpec(memory_space=pl.ANY)
    shape = jax.ShapeDtypeStruct
    blocks = (4, ROWS, MODEL)
    return pl.pallas_call(
        mlp_kernel,
        out_shape=(
            shape(blocks, LOW), shape((4, ROWS, UNITS), LOW), shape((4, ROWS, PAIR), LOW), shape(blocks, LOW),
            shape((ROWS, MODEL), WIDE), shape((ROWS, MODEL), LOW), shape((4, 16, UNITS), LOW),
        ),
        in_specs=[vmem] * 4 + [anywhere] * 2,
        out_specs=(anywhere,) * 4 + (vmem,) * 3,
        scratch_shapes=[
            pltpu.VMEM((8, 16, 16, SLAB), LOW), pltpu.VMEM(blocks, LOW), pltpu.VMEM(blocks, LOW),
            pltpu.VMEM((4, ROWS, UNITS), LOW), pltpu.VMEM((4, ROWS, PAIR), LOW), pltpu.VMEM(blocks, LOW),
            pltpu.VMEM(blocks, LOW), pltpu.VMEM((2, ROWS // 2, MODEL), LOW), pltpu.VMEM((2, ROWS, MODEL), LOW),
            pltpu.VMEM((3, 8, 2, 16, UNITS), LOW), pltpu.VMEM((8, 8, 16, UNITS), LOW),
            pltpu.VMEM((4, 2, 2, 16, UNITS), LOW), pltpu.VMEM((4, 2, 4, 16, UNITS), LOW),
            pltpu.VMEM((2, 2, 16, UNITS), LOW), pltpu.VMEM((2, 4, 16, UNITS), LOW),
            pltpu.SemaphoreType.DMA((51,)), pltpu.SemaphoreType.DMA((51,)), pltpu.SemaphoreType.DMA((6,)),
        ],
        compiler_params=pltpu.CompilerParams(collective_id=2, has_side_effects=True, vmem_limit_bytes=56 * 2**20),
        name="mlp",
    )(two, resid, cot, live, grad_all, wm)
def back_kernel(
    branch_grad, grad_resid, x_ref, live_ref, resid, branch_all, two_all, pair_all, one_all, wa_all, qkv_all, probs_all, att_all,
    layer_out, input_grad, pair_own, in_own, out_own,
    acc, z_over, z_near, x_over, x_near, grads, part, qx, q2, q1, p2, p1, px,
    wa, acc_a, az_over, az_near, h_near, twos, pair, stage, ones, qkv, probs, att, grad_att, grad_proj, grad_k, grad_v, stage_a,
    send, recv, local_sem,
):
    me = Place()
    mail = Mail(send, recv)
    loads = []

    def load(src, dst):
        copy = pltpu.make_async_copy(src, dst, local_sem.at[len(loads)])
        copy.start()
        loads.append(copy)
        return copy

    load_wa = load(wa_all, wa)
    load_branch = load(branch_all, part.at[0:4])
    enter(me.peers() + [me.h_dev, me.z_up_dev, me.z_down_dev, me.x_up_dev, me.x_down_dev, me.twin_dev])
    grads[me.seq] = branch_grad[...]
    gather = gather_seq(me, mail, grads.at[me.seq], grads)
    step(gather)
    order = [me.a * 4 + i for i in range(4)] + [me.b * 4 + i for i in range(4)]

    def columns_of(s, width=256):
        return pl.ds(pl.multiple_of(s * width, width), width)

    def pair_sums():
        yield from scatter_xz(me, mail, acc, z_over, z_near, x_over, x_near)
        yield from send_y(me, mail, acc.at[pl.ds(me.a * 4, 4), me.z * 2 + me.h], pair_own)

    sums = pair_sums()

    first, second = load(two_all, twos), load(pair_all, pair)
    waits = [load(*both) for both in ((qkv_all, qkv), (att_all, att), (one_all.at[4:8], ones))]
    first.wait()
    second.wait()

    def pair_product(s, out):
        rows = twos[:, :, columns_of(s)].reshape(4 * ROWS, 256)

        def tile(j, carry):
            columns = columns_of(j)
            terms = dot(rows, pair[:, :, columns].reshape(4 * ROWS, 256), ((0,), (0,)))
            out[:, :, :, columns] = terms.reshape(8, 2, 16, 256).astype(LOW)
            return carry

        lax.fori_loop(0, PAIR // 256, tile, 0)

    twin = twin_sum(me, mail, stage, acc, order, pair_product)
    for i in range(5):
        step(twin)
        step(gather)
    step(sums)
    for i in range(4):
        step(twin)
        step(gather)
    step(sums)

    def write_out(lo, hi, rows):
        layer_out[lo:hi] = (live_ref[lo:hi] * (resid[lo:hi] + rows)).astype(LOW)

    def write_grad(lo, hi, rows):
        x = x_ref[lo:hi].astype(WIDE)
        scale = row_scale(x)
        hat = x * scale
        inner = jnp.mean(rows * hat, axis=-1, keepdims=True)
        input_grad[lo:hi] = grad_resid[lo:hi] + live_ref[lo:hi] * scale * (rows - hat * inner)

    class Lower:
        at = {0: part.at[6, 0 : ROWS // 2], 1: part.at[6, ROWS // 2 : ROWS]}

    out_sum = scatter_y(me, mail, part.at[0:4], Lower, part.at[4:6], write_out)
    grad_sum = scatter_seq(me, mail, part, (qx, q2, q1, p2, p1, px), write_grad)

    run(gather)
    waits.append(load(one_all.at[0:4], twos))
    fetch = [load(probs_all.at[:, 256 * i : 256 * i + 256], probs.at[i]) for i in range(2)]
    load_branch.wait()
    out_slots = range(mail.count, mail.count + 6)
    step(out_sum)
    load_wa.wait()
    for wait in waits:
        wait.wait()
    head_scale = 1.0 / math.sqrt(HEAD_DIM)

    def attended_grad(i, carry):
        total = jnp.zeros((256, PART), WIDE)
        for k in range(8):
            rows = grads[pl.ds(i * 2, 2), :, k * PART : k * PART + PART].reshape(256, PART)
            total = total + dot(rows, wa[k, :, :, PROJ:].reshape(PART, PART), ((1,), (1,)))
        grad_att[columns_of(i), :] = total.astype(LOW)
        return carry

    lax.fori_loop(0, 4, attended_grad, 0)
    step(out_sum)
    step(sums)
    grad_k[...] = jnp.zeros_like(grad_k)
    grad_v[...] = jnp.zeros_like(grad_v)

    def attend_back(i):
        rows = pl.ds(256 * i, 256)
        for head in range(2):
            lo, hi = head * HEAD_DIM, (head + 1) * HEAD_DIM
            low = probs[i % 2, head]
            p = low.astype(WIDE)
            g = grad_att[rows, lo:hi]
            back = dot(g, qkv[:, 2 * PART + lo : 2 * PART + hi], ((1,), (1,)))
            grad_s = (back * (p * (1.0 - p))).astype(LOW)
            grad_q = dot(grad_s, qkv[:, PART + lo : PART + hi]) * head_scale
            grad_proj[rows, lo:hi] = grad_q.astype(LOW)
            grad_v[:, lo:hi] += dot(low, g, ((0,), (0,)))
            grad_k[:, lo:hi] += dot(grad_s, qkv[rows, lo:hi], ((0,), (0,)))

    for i in range(4):
        fetch[i].wait()
        attend_back(i)
        if i < 2:
            fetch.append(load(probs_all.at[:, 256 * i + 512 : 256 * i + 768], probs.at[i]))
        step(sums)
        step(out_sum)
    run(out_sum)
    for slot in out_slots:
        mail.sent(slot)
    grad_proj[:, PART : 2 * PART] = (grad_k[...] * head_scale).astype(LOW)
    grad_proj[:, 2 * PART :] = grad_v[...].astype(LOW)

    def norm_terms(col):
        rows = grad_proj[columns_of(col, 512), :]

        def piece(s, carry):
            weight = wa[s, :, :, 0:PROJ].reshape(256, PROJ)
            terms = dot(rows, weight, ((1,), (1,)))
            part[pl.ds(col * 4, 4), :, columns_of(s)] = terms.reshape(4, ROWS, 256).astype(LOW)
            return carry

        lax.fori_loop(0, 8, piece, 0)

    norm_terms(me.b)
    step(grad_sum)
    norm_terms(me.a)
    step(grad_sum)
    step(sums)

    def product(s, out):
        terms = jnp.zeros((256, PROJ), WIDE)
        for half, tokens in enumerate((twos, ones)):
            rows = tokens[:, :, columns_of(s)].reshape(4 * ROWS, 256)
            terms = terms + dot(rows, grad_proj[512 * half : 512 * half + 512, :], ((0,), (0,)))
        out[:, :, :, 0:PROJ] = terms.reshape(8, 2, 16, PROJ).astype(LOW)
        rows = grads[:, :, columns_of(s)].reshape(8 * ROWS, 256)
        terms = dot(att[...], rows, ((0,), (0,)))
        out[:, :, :, PROJ:] = terms.reshape(8, 2, 16, PART).astype(LOW)

    twin = twin_sum(me, mail, stage_a, acc_a, order, product)
    for i in range(9):
        step(twin)
        step(grad_sum)
        if i % 2 == 0:
            step(sums)

    def proj_sums():
        yield from scatter_hz(me, mail, acc_a, az_over, az_near, h_near)
        own = acc_a.at[:, me.z * 2 + me.h]
        out_own[...] = own[:, :, PROJ:]
        yield from send_seq(me, mail, own, in_own, 0, PROJ)

    run(proj_sums(), grad_sum, sums)

    mail.finish()


def back(branch_grad, grad_resid, x, live, resid, branch, twos, pair, ones, wa, qkv, probs, att):
    vmem, anywhere = pl.BlockSpec(memory_space=pltpu.VMEM), pl.BlockSpec(memory_space=pl.ANY)
    shape = jax.ShapeDtypeStruct
    blocks = (4, ROWS, MODEL)
    count = 18 + 8 + 30 + 3 + 6 + 23 + 8 + 13 + 7
    return pl.pallas_call(
        back_kernel,
        out_shape=(
            shape((ROWS, MODEL), LOW), shape((ROWS, MODEL), WIDE), shape((4, 16, PAIR), LOW),
            shape((8, 16, PROJ), LOW), shape((8, 16, PART), LOW),
        ),
        in_specs=[vmem] * 5 + [anywhere] * 8,
        out_specs=(vmem,) * 5,
        scratch_shapes=[
            pltpu.VMEM((8, 8, 16, PAIR), LOW), pltpu.VMEM((4, 2, 2, 16, PAIR), LOW), pltpu.VMEM((4, 2, 4, 16, PAIR), LOW),
            pltpu.VMEM((2, 2, 16, PAIR), LOW), pltpu.VMEM((2, 4, 16, PAIR), LOW), pltpu.VMEM((8, ROWS, MODEL), LOW),
            pltpu.VMEM((8, ROWS, MODEL), LOW),
        ]
        + scatter_bufs()
        + [
            pltpu.VMEM((8, 16, 16, 1024), LOW), pltpu.VMEM((8, 8, 16, 1024), LOW), pltpu.VMEM((2, 2, 4, 16, 1024), LOW),
            pltpu.VMEM((2, 2, 8, 16, 1024), LOW), pltpu.VMEM((8, 16, 1024), LOW),
            pltpu.VMEM(blocks, LOW), pltpu.VMEM((4, ROWS, PAIR), LOW), pltpu.VMEM((2, 8, 2, 16, PAIR), LOW), pltpu.VMEM(blocks, LOW),
            pltpu.VMEM((1024, PROJ), LOW), pltpu.VMEM((2, 2, 256, 1024), LOW), pltpu.VMEM((1024, PART), LOW),
            pltpu.VMEM((1024, PART), LOW), pltpu.VMEM((1024, PROJ), LOW),
            pltpu.VMEM((1024, PART), WIDE), pltpu.VMEM((1024, PART), WIDE), pltpu.VMEM((2, 8, 2, 16, 1024), LOW),
            pltpu.SemaphoreType.DMA((count,)), pltpu.SemaphoreType.DMA((count,)), pltpu.SemaphoreType.DMA((12,)),
        ],
        compiler_params=pltpu.CompilerParams(collective_id=3, has_side_effects=True, vmem_limit_bytes=62 * 2**20),
        name="back",
    )(branch_grad, grad_resid, x, live, resid, branch, twos, pair, ones, wa, qkv, probs, att)
def weights_out(attn_weight, mlp_weight, gain_one, gain_two):
    proj = (attn_weight[:, :3].astype(WIDE) * gain_one).astype(LOW).reshape(16, 3, 8, PART)
    proj = proj.transpose(2, 0, 1, 3).reshape(8, 16, PROJ)
    out = attn_weight[:, 3].reshape(16, 8, PART).transpose(1, 0, 2)
    units = mlp_weight.shape[2] // 4
    spare = UNITS - units
    pair = (mlp_weight[:, :2].astype(WIDE) * gain_two).astype(LOW).reshape(16, 2, 4, units)
    pair = jnp.pad(pair, ((0, 0), (0, 0), (0, 0), (0, spare))).reshape(16, 2, 4, UNITS // 128, 128)
    pair = pair.transpose(2, 0, 3, 1, 4).reshape(4, 16, PAIR)
    down = jnp.pad(mlp_weight[:, 2].reshape(16, 4, units), ((0, 0), (0, 0), (0, spare))).transpose(1, 0, 2)
    return jnp.concatenate([proj, out], axis=2), jnp.concatenate([pair, down], axis=2)


def weights_back(pair, down, proj, out, units):
    proj = proj.reshape(8, 16, 3, PART).transpose(1, 2, 0, 3).reshape(16, 3, MODEL).astype(WIDE)
    out = out.transpose(1, 0, 2).reshape(16, MODEL).astype(WIDE)
    pair = pair.reshape(4, 16, UNITS // 128, 2, 128).transpose(1, 3, 0, 2, 4).reshape(16, 2, 4, UNITS)
    pair = pair[..., : units // 4].reshape(16, 2, units).astype(WIDE)
    down = down[..., : units // 4].transpose(1, 0, 2).reshape(16, units).astype(WIDE)
    return proj, out, pair, down


def local(
    tokens, valid_counts, block_owner, norm1_gain, attn_weight, norm2_gain, mlp_weight, cotangent
):
    row_index = jnp.arange(ROWS, dtype=jnp.int32)
    live = (row_index < valid_counts[0, 0]).astype(WIDE)[:, None]
    pos = (block_owner[0][:, None] * ROWS + row_index[None]).reshape(-1)
    x, cot = tokens[0], cotangent[0]
    gain_one = norm1_gain.astype(WIDE)[:, None, None]
    gain_two = norm2_gain.astype(WIDE)[:, None, None]
    wa_own, wm_own = weights_out(attn_weight, mlp_weight, gain_one, gain_two)
    ones, wa, grads, wm, qkv, probs, att, resid, two = front(x, live, cot, wa_own, wm_own, pos)
    twos, hidden, pair, branch, grad_resid, branch_grad, down_own = mlp(two, resid, cot, live, grads, wm)
    layer_out, input_grad, pair_own, in_own, out_own = back(
        branch_grad, grad_resid, x, live, resid, branch, twos, pair, ones, wa, qkv, probs, att
    )
    in_sum, out_sum, pair_sum, down_sum = weights_back(pair_own, down_own, in_own, out_own, mlp_weight.shape[2])
    attn_grad = jnp.concatenate([in_sum * gain_one, out_sum[:, None]], axis=1)
    mlp_grad = jnp.concatenate([pair_sum * gain_two, down_sum[:, None]], axis=1)
    gain_one_grad = jnp.sum(in_sum * attn_weight[:, :3].astype(WIDE), axis=(1, 2))
    gain_two_grad = jnp.sum(pair_sum * mlp_weight[:, :2].astype(WIDE), axis=(1, 2))
    return (layer_out[None], input_grad[None], gain_one_grad, attn_grad, gain_two_grad, mlp_grad)


def solution(mesh):
    token_spec = P("dp", "seq", None)
    row_spec = P(("seq", "dp"), None, None)
    gain_spec = P(("seq", "dp"))
    in_specs = (
        token_spec, P("dp", "seq"), P("dp", None), gain_spec, row_spec, gain_spec, row_spec, token_spec
    )
    out_specs = (token_spec, token_spec, gain_spec, row_spec, gain_spec, row_spec)
    return jax.shard_map(local, mesh=mesh, in_specs=in_specs, out_specs=out_specs, check_vma=False)
```

time: 962 us -> 430 us (0.45)
  waiting for transfers between devices: 646 us -> 0 us
  Pallas kernels: 0 us -> 402 us
  matrix products: 96.5 us -> 0 us
  local copies, waits for them, and re-layouts: 95.9 us -> 11.2 us
  blocking collectives: 48.4 us -> 0 us
  other arithmetic: 42.2 us -> 8.07 us
  between operations: 15.5 us -> 2.05 us
    pallas_call x0 -> x3, Pallas kernels: none -> 402 us  [the longest x1 148 us: front(): pl.pallas_call(front_kernel, out_shape=(shape((8, ROWS, MODEL), LOW), sha...]
    reduce_scatter x7 -> x0, waiting for transfers between devices: 377 us -> none  [the longest x4 190 us: scatter_tokens(): lax.psum_scatter(partial.astype(LOW), 'seq', scatter_dimension=0, tiled=T...]
    all_gather x7 -> x0, waiting for transfers between devices: 267 us -> none  [the longest x4 120 us: gather_tokens(): return lax.all_gather(rows, 'seq', axis=0, tiled=True)]
    dot_general x18 -> x0, matrix products: 96.5 us -> none  [the longest x12 83.4 us: dot(): return lax.dot_general(a, b, (dims, ((), ())), preferred_element_type=WIDE)]
    all_to_all x3 -> x0, blocking collectives: 48.4 us -> none  [the longest x2 34 us: columns_in(): lax.all_to_all(cut, 'seq', split_axis=2, concat_axis=0, tiled=True)[:, :, 0]]
    concatenate x2 -> x0, local copies, waits for them, and re-layouts: 23.6 us -> none  [local(): jnp.concatenate([dot(all_two, grad_pair, ((0,), (0,))).reshape(model, 2,...]
    transpose x2 -> x3, local copies, waits for them, and re-layouts: 19.1 us -> 0.58 us  [the longest x1 0.39 us: weights_out(): pair = pair.transpose(2, 0, 3, 1, 4).reshape(4, 16, PAIR)]
    transpose x1 -> x0, other arithmetic: 17.6 us -> none  [columns_out(): grads.astype(LOW).reshape(seq, dp, count, slots, part)]
  transfers between devices with their start and end apart: 15 -> 0, of which waited for: 13 -> 0; matrix products, arithmetic and copies ran while one was open for 20% -> 0% of each run, Pallas kernels for 0% -> 0%
where the time goes in v2:
time: 430 us; the launch traced here: 423 us
  Pallas kernels  402 us (93%)
  local copies, waits for them, and re-layouts  11.2 us (3%)
  other arithmetic  8.07 us (2%)
    pallas_call x1, Pallas kernels, front(): pl.pallas_call(front_kernel, out_shape=(shape((8, ROWS, MODEL), LOW), sha...  148 us
    pallas_call x1, Pallas kernels, back(): pl.pallas_call(back_kernel, out_shape=(shape((ROWS, MODEL), LOW), shape((...  148 us
    pallas_call x1, Pallas kernels, mlp(): pl.pallas_call(mlp_kernel, out_shape=(shape(blocks, LOW), shape((4, ROWS,...  106 us

profile of v2, /device:TPU:0, one launch (start us, length us, event | category | flops | bytes accessed | tf_op | source)
XLA Modules:
  0.0 423.4 jit_solution(15047407918019743371)
XLA Ops:
  1.3 0.7 convert_element_type.86
  2.0 0.7 convert_element_type.89
  2.6 0.7 multiply_bitcast_fusion
  3.4 0.6 fusion.4.live_ref
  4.0 1.3 slice_reduce_fusion
  5.4 0.9 slice.23
  6.3 0.2 reshape_squeeze.7
  6.8 0.2 copy.29
  7.0 0.2 reshape.134
  7.2 0.7 pad_maximum_fusion.3.wa_own
  8.1 0.4 reshape.135
  8.6 0.2 reshape.136
  8.8 0.4 copy.32
  9.4 0.8 pad_maximum_fusion.1.wm_own
  10.2 1.0 copy.34.pos_q
  11.3 148.1 %front.1 = (bf16[8,128,2048]{2,1,0:T(8,128)(2,1)}, bf16[8,16,16,1024]{3,2,1,0:T(8,128)(2,1)}, bf16[4,128,2048]{2,1,0:T(8,128)(2,1)}, bf16[8,16,16,4224]{3,2,1,0:...) custom-call(bf16[128,2048]{1,0:T(8,128)(2,1)} %bitcast.53, ...), custom_call_target="tpu_custom_call" | custom-call | tf_op jit(solution)/shard_map/front/pallas_call | solution.py:737
  159.3 106.4 %mlp.1 = (bf16[4,128,2048]{2,1,0:T(8,128)(2,1)}, bf16[4,128,1408]{2,1,0:T(8,128)(2,1)}, bf16[4,128,2816]{2,1,0:T(8,128)(2,1)}, bf16[4,128,2048]{2,1,0:T(8,128)(2...) custom-call(bf16[128,2048]{1,0:T(8,128)(2,1)} %get-tuple-element.26.two_ref, ...), custom_call_target="tpu_custom_call" | custom-call | tf_op jit(solution)/shard_map/mlp/pallas_call | solution.py:899
  265.8 147.6 %back.1 = (bf16[128,2048]{1,0:T(8,128)(2,1)}, f32[128,2048]{1,0:T(8,128)}, bf16[4,16,2816]{2,1,0:T(8,128)(2,1)}, bf16[8,16,768]{2,1,0:T(8,128)(2,1)}, bf16[8,16,256]{2,1,0:T(8,128)(2,1)}) custom-call(bf16[128,2048]{1,0:T(8,128)(2,1)} %get-tuple-element.30.branch_grad, f32[128,2048]{1,0:T(8,128)} %get-tuple-element.31.grad_resid, bf16[128,2048]{1,0:T(8,128)(2,1)} %bitcast.54, ...), custom_call_target="tpu_custom_call" | custom-call | tf_op jit(solution)/shard_map/back/pallas_call | solution.py:1097
  413.4 0.9 convert_bitcast_fusion.1
  414.4 1.1 reshape.138
  415.5 0.2 reshape.139
  415.8 0.3 copy.38
  416.1 0.4 reshape.142
  416.5 0.7 broadcast_multiply_fusion
  417.4 0.2 reshape.143
  417.6 1.0 pad_maximum_fusion
  418.7 0.2 reshape.144
  418.9 0.2 copy.35
  419.2 0.8 broadcast_multiply_fusion.1
  420.0 1.1 copy.40
  421.2 0.8 copy.53
  422.0 1.0 copy.54
  (32 shorter events, 1.2 us)
Async XLA Ops:
  0.6 6.0 %copy-start = (bf16[16,4,2048]{2,1,0:T(4,128)(2,1)S(1)}, bf16[16,4,2048]{2,1,0:T(4,128)(2,1)}, u32[]{:S(2)}) copy-start(bf16[16,4,2048]{2,1,0:T(4,128)(2,1)} %param.12) | copy-start | bytes 786436
  3.4 6.8 %copy-start.6 = (s32[8,128]{1,0:T(8,128)}, s32[8,128]{1,0:T(8,128)S(1)}, u32[]{:S(2)}) copy-start(s32[8,128]{1,0:T(8,128)S(1)} %iota_add_fusion) | copy-start | bytes 12292
  6.6 1.4 copy-start.1
  416.1 1.1 copy-start.5
  417.4 1.3 copy-start.4
  419.2 2.0 copy-start.3
  420.0 2.0 copy-start.2

commit v3 on v2

--- a/solution.py
+++ b/solution.py
@@ -409,13 +409,15 @@
         add_slabs(self.at(own), self.near.at[0], self.near.at[1])
 
 
-def twin_sum(me, mail, stage, acc, order, product):
+def twin_sum(me, mail, stage, acc, order, product, kept=None):
     slots = stage.shape[0]
     n = mail.slots(len(order))
 
     def settle(i):
         mail.arrived(n + i, acc.at[order[i]], me.twin_dev)
         add_slabs(acc.at[order[i]], stage.at[i % slots, :, me.core])
+        if kept is not None:
+            kept(i)
 
     for i, s in enumerate(order):
         if i >= slots:
@@ -642,6 +644,9 @@
     enter(me.peers() + [me.h_dev, me.z_up_dev, me.z_down_dev, me.twin_dev, me.x_up_dev, me.x_down_dev])
     swap_a = swap_seq(me, mail, wa_own, wa, 0, PROJ)
     step(swap_a)
+    swap_m = swap_y(me, mail, wm_own, wm)
+    step(swap_m)
+    keep_m = save(wm_own.at[me.y], wm.at[me.seq, me.dp])
     x = x_ref[...].astype(WIDE)
     one_all[me.seq] = (x * row_scale(x) * live_ref[...]).astype(LOW)
     gather_one = gather_seq(me, mail, one_all.at[me.seq], one_all)
@@ -652,18 +657,17 @@
     step(swap_a)
     gather_wa = gather_dp(me, mail, wa)
     step(gather_wa)
-    swap_m = swap_y(me, mail, wm_own, wm)
-    step(swap_m)
-    keep_m = save(wm_own.at[me.y], wm.at[me.seq, me.dp])
-    grad_own[...] = (cot_ref[...].astype(WIDE) * live_ref[...]).astype(LOW)
-    save(grad_own, grad_all.at[me.y])
-    for i in range(3):
-        step(gather_one)
-        step(gather_wa)
     step(swap_m)
     keep_m.wait()
     gather_wm = gather_xz(me, mail, wm)
     step(gather_wm)
+    grad_own[...] = (cot_ref[...].astype(WIDE) * live_ref[...]).astype(LOW)
+    save(grad_own, grad_all.at[me.y])
+    for i in range(8):
+        step(gather_one)
+        step(gather_wa)
+        if i in (2, 4, 6):
+            step(gather_wm)
     run(gather_one, gather_wa)
     gather_g = gather_y(me, mail, grad_own, grad_all)
     step(gather_g)
@@ -755,10 +759,9 @@
     )(x, live, cot, wa_own, wm_own, pos[:, None], pos[None, :])
 def mlp_kernel(
     two_ref, resid, cot_ref, live_ref, grad_all, wm_all,
-    two_out, hidden_out, pair_out, branch_out, grad_resid, grad_branch,
-    down_own,
+    acc_out, branch_out, grad_resid, grad_branch,
     wm, grads, twos, hidden, pair, part, branch, p2, p1,
-    stage, acc, z_over, z_near, x_over, x_near, send, recv, local_sem,
+    stage, acc, send, recv, local_sem,
 ):
     me = Place()
     mail = Mail(send, recv)
@@ -772,8 +775,7 @@
 
     load_w = save(wm_all, wm)
     load_g = save(grad_all, grads)
-    others = [{"seq": me.a * 4 + (me.y + k) % 4} for k in (1, 2, 3)]
-    enter(others + [me.x_up_dev, me.x_down_dev, me.z_up_dev, me.z_down_dev, me.twin_dev])
+    enter([me.up_dev, me.down_dev, me.twin_dev])
     twos[me.y] = two_ref[...]
     gather = gather_y(me, mail, twos.at[me.y], twos)
     step(gather)
@@ -854,39 +856,33 @@
     ahead([me.far])
     back([me.far])
     step(scatter)
-    save(twos, two_out)
-    save(hidden, hidden_out)
-    save(pair, pair_out)
     back([me.y])
     step(scatter)
     order = [me.a * 4 + i for i in range(4)] + [me.b * 4 + i for i in range(4)]
 
-    def down_product(s, out):
-        rows = grads[:, :, pl.ds(pl.multiple_of(s * 256, 256), 256)].reshape(4 * ROWS, 256)
-
-        def tile(j, carry):
-            columns = pl.ds(pl.multiple_of(j * 128, 128), 128)
-            terms = dot(rows, hidden[:, :, columns].reshape(4 * ROWS, 128), ((0,), (0,)))
-            out[:, :, :, columns] = terms.reshape(8, 2, 16, 128).astype(LOW)
-            return carry
-
-        lax.fori_loop(0, UNITS // 128, tile, 0)
-
-    twin = twin_sum(me, mail, stage, acc, order, down_product)
-    for i in range(4):
+    def product(s, out):
+        columns = pl.ds(pl.multiple_of(s * 256, 256), 256)
+        rows = twos[:, :, columns].reshape(4 * ROWS, 256).T
+        terms = dot(rows, pair[...].reshape(4 * ROWS, PAIR))
+        out[:, :, :, 0:PAIR] = terms.reshape(8, 2, 16, PAIR).astype(LOW)
+        rows = grads[:, :, columns].reshape(4 * ROWS, 256).T
+        terms = dot(rows, hidden[...].reshape(4 * ROWS, UNITS))
+        out[:, :, :, PAIR:] = terms.reshape(8, 2, 16, UNITS).astype(LOW)
+
+    def kept(i):
+        save(acc.at[order[i]], acc_out.at[order[i]])
+
+    twin = twin_sum(me, mail, stage, acc, order, product, kept)
+    for i in range(3):
         step(twin)
     step(scatter)
-    step(twin)
-    sums = scatter_xz(me, mail, acc, z_over, z_near, x_over, x_near)
-    step(sums)
+    for i in range(3):
+        step(twin)
+    step(scatter)
     run(twin)
-    step(sums)
-    step(scatter)
-    every = [me.y, me.up, me.down, me.far]
-    down_back(every)
+    down_back([me.y, me.up, me.down, me.far])
     save(branch, branch_out)
-    run(scatter, gather, sums)
-    run(send_y(me, mail, acc.at[pl.ds(me.a * 4, 4), me.z * 2 + me.h], down_own))
+    run(scatter, gather)
     for copy in saves[2:]:
         copy.wait()
     mail.finish()
@@ -899,28 +895,25 @@
     return pl.pallas_call(
         mlp_kernel,
         out_shape=(
-            shape(blocks, LOW), shape((4, ROWS, UNITS), LOW), shape((4, ROWS, PAIR), LOW), shape(blocks, LOW),
-            shape((ROWS, MODEL), WIDE), shape((ROWS, MODEL), LOW), shape((4, 16, UNITS), LOW),
+            shape((8, 8, 16, SLAB), LOW), shape(blocks, LOW), shape((ROWS, MODEL), WIDE), shape((ROWS, MODEL), LOW),
         ),
         in_specs=[vmem] * 4 + [anywhere] * 2,
-        out_specs=(anywhere,) * 4 + (vmem,) * 3,
+        out_specs=(anywhere,) * 2 + (vmem,) * 2,
         scratch_shapes=[
             pltpu.VMEM((8, 16, 16, SLAB), LOW), pltpu.VMEM(blocks, LOW), pltpu.VMEM(blocks, LOW),
             pltpu.VMEM((4, ROWS, UNITS), LOW), pltpu.VMEM((4, ROWS, PAIR), LOW), pltpu.VMEM(blocks, LOW),
             pltpu.VMEM(blocks, LOW), pltpu.VMEM((2, ROWS // 2, MODEL), LOW), pltpu.VMEM((2, ROWS, MODEL), LOW),
-            pltpu.VMEM((3, 8, 2, 16, UNITS), LOW), pltpu.VMEM((8, 8, 16, UNITS), LOW),
-            pltpu.VMEM((4, 2, 2, 16, UNITS), LOW), pltpu.VMEM((4, 2, 4, 16, UNITS), LOW),
-            pltpu.VMEM((2, 2, 16, UNITS), LOW), pltpu.VMEM((2, 4, 16, UNITS), LOW),
-            pltpu.SemaphoreType.DMA((51,)), pltpu.SemaphoreType.DMA((51,)), pltpu.SemaphoreType.DMA((6,)),
+            pltpu.VMEM((2, 8, 2, 16, SLAB), LOW), pltpu.VMEM((8, 8, 16, SLAB), LOW),
+            pltpu.SemaphoreType.DMA((18,)), pltpu.SemaphoreType.DMA((18,)), pltpu.SemaphoreType.DMA((11,)),
         ],
-        compiler_params=pltpu.CompilerParams(collective_id=2, has_side_effects=True, vmem_limit_bytes=56 * 2**20),
+        compiler_params=pltpu.CompilerParams(collective_id=2, has_side_effects=True, vmem_limit_bytes=62 * 2**20),
         name="mlp",
     )(two, resid, cot, live, grad_all, wm)
 def back_kernel(
-    branch_grad, grad_resid, x_ref, live_ref, resid, branch_all, two_all, pair_all, one_all, wa_all, qkv_all, probs_all, att_all,
-    layer_out, input_grad, pair_own, in_own, out_own,
+    branch_grad, grad_resid, x_ref, live_ref, resid, branch_all, acc_all, one_all, wa_all, qkv_all, probs_all, att_all,
+    layer_out, input_grad, slab_own, in_own, out_own,
     acc, z_over, z_near, x_over, x_near, grads, part, qx, q2, q1, p2, p1, px,
-    wa, acc_a, az_over, az_near, h_near, twos, pair, stage, ones, qkv, probs, att, grad_att, grad_proj, grad_k, grad_v, stage_a,
+    wa, acc_a, az_over, az_near, h_near, ones, qkv, probs, att, grad_att, grad_proj, grad_k, grad_v, stage_a,
     send, recv, local_sem,
 ):
     me = Place()
@@ -933,48 +926,33 @@
         loads.append(copy)
         return copy
 
-    load_wa = load(wa_all, wa)
-    load_branch = load(branch_all, part.at[0:4])
+    load_acc = [load(acc_all.at[pl.ds(col * 4, 4)], acc.at[pl.ds(col * 4, 4)]) for col in (me.a, me.b)]
     enter(me.peers() + [me.h_dev, me.z_up_dev, me.z_down_dev, me.x_up_dev, me.x_down_dev, me.twin_dev])
     grads[me.seq] = branch_grad[...]
     gather = gather_seq(me, mail, grads.at[me.seq], grads)
     step(gather)
+    load_wa = load(wa_all, wa)
+    load_branch = load(branch_all, part.at[0:4])
+    waits = [load(*both) for both in ((qkv_all, qkv), (att_all, att), (one_all, ones))]
+    fetch = [load(probs_all.at[:, 256 * i : 256 * i + 256], probs.at[i]) for i in range(2)]
     order = [me.a * 4 + i for i in range(4)] + [me.b * 4 + i for i in range(4)]
 
     def columns_of(s, width=256):
         return pl.ds(pl.multiple_of(s * width, width), width)
 
-    def pair_sums():
+    def slab_sums():
         yield from scatter_xz(me, mail, acc, z_over, z_near, x_over, x_near)
-        yield from send_y(me, mail, acc.at[pl.ds(me.a * 4, 4), me.z * 2 + me.h], pair_own)
-
-    sums = pair_sums()
-
-    first, second = load(two_all, twos), load(pair_all, pair)
-    waits = [load(*both) for both in ((qkv_all, qkv), (att_all, att), (one_all.at[4:8], ones))]
-    first.wait()
-    second.wait()
-
-    def pair_product(s, out):
-        rows = twos[:, :, columns_of(s)].reshape(4 * ROWS, 256)
-
-        def tile(j, carry):
-            columns = columns_of(j)
-            terms = dot(rows, pair[:, :, columns].reshape(4 * ROWS, 256), ((0,), (0,)))
-            out[:, :, :, columns] = terms.reshape(8, 2, 16, 256).astype(LOW)
-            return carry
-
-        lax.fori_loop(0, PAIR // 256, tile, 0)
-
-    twin = twin_sum(me, mail, stage, acc, order, pair_product)
-    for i in range(5):
-        step(twin)
+        yield from send_y(me, mail, acc.at[pl.ds(me.a * 4, 4), me.z * 2 + me.h], slab_own)
+
+    sums = slab_sums()
+
+    load_acc[0].wait()
+    step(sums)
+    load_acc[1].wait()
+    step(sums)
+    for i in range(3):
         step(gather)
-    step(sums)
-    for i in range(4):
-        step(twin)
-        step(gather)
-    step(sums)
+        step(sums)
 
     def write_out(lo, hi, rows):
         layer_out[lo:hi] = (live_ref[lo:hi] * (resid[lo:hi] + rows)).astype(LOW)
@@ -993,8 +971,6 @@
     grad_sum = scatter_seq(me, mail, part, (qx, q2, q1, p2, p1, px), write_grad)
 
     run(gather)
-    waits.append(load(one_all.at[0:4], twos))
-    fetch = [load(probs_all.at[:, 256 * i : 256 * i + 256], probs.at[i]) for i in range(2)]
     load_branch.wait()
     out_slots = range(mail.count, mail.count + 6)
     step(out_sum)
@@ -1055,28 +1031,22 @@
 
         lax.fori_loop(0, 8, piece, 0)
 
-    norm_terms(me.b)
-    step(grad_sum)
-    norm_terms(me.a)
-    step(grad_sum)
-    step(sums)
-
     def product(s, out):
-        terms = jnp.zeros((256, PROJ), WIDE)
-        for half, tokens in enumerate((twos, ones)):
-            rows = tokens[:, :, columns_of(s)].reshape(4 * ROWS, 256)
-            terms = terms + dot(rows, grad_proj[512 * half : 512 * half + 512, :], ((0,), (0,)))
+        rows = ones[:, :, columns_of(s)].reshape(8 * ROWS, 256).T
+        terms = dot(rows, grad_proj[...])
         out[:, :, :, 0:PROJ] = terms.reshape(8, 2, 16, PROJ).astype(LOW)
         rows = grads[:, :, columns_of(s)].reshape(8 * ROWS, 256)
         terms = dot(att[...], rows, ((0,), (0,)))
         out[:, :, :, PROJ:] = terms.reshape(8, 2, 16, PART).astype(LOW)
 
     twin = twin_sum(me, mail, stage_a, acc_a, order, product)
+    norm_terms(me.b)
+    step(grad_sum)
     for i in range(9):
         step(twin)
-        step(grad_sum)
-        if i % 2 == 0:
-            step(sums)
+    norm_terms(me.a)
+    step(grad_sum)
+    step(sums)
 
     def proj_sums():
         yield from scatter_hz(me, mail, acc_a, az_over, az_near, h_near)
@@ -1089,29 +1059,28 @@
     mail.finish()
 
 
-def back(branch_grad, grad_resid, x, live, resid, branch, twos, pair, ones, wa, qkv, probs, att):
+def back(branch_grad, grad_resid, x, live, resid, branch, acc, ones, wa, qkv, probs, att):
     vmem, anywhere = pl.BlockSpec(memory_space=pltpu.VMEM), pl.BlockSpec(memory_space=pl.ANY)
     shape = jax.ShapeDtypeStruct
-    blocks = (4, ROWS, MODEL)
-    count = 18 + 8 + 30 + 3 + 6 + 23 + 8 + 13 + 7
+    count = 18 + 30 + 3 + 6 + 23 + 8 + 13 + 7
     return pl.pallas_call(
         back_kernel,
         out_shape=(
-            shape((ROWS, MODEL), LOW), shape((ROWS, MODEL), WIDE), shape((4, 16, PAIR), LOW),
+            shape((ROWS, MODEL), LOW), shape((ROWS, MODEL), WIDE), shape((4, 16, SLAB), LOW),
             shape((8, 16, PROJ), LOW), shape((8, 16, PART), LOW),
         ),
-        in_specs=[vmem] * 5 + [anywhere] * 8,
+        in_specs=[vmem] * 5 + [anywhere] * 7,
         out_specs=(vmem,) * 5,
         scratch_shapes=[
-            pltpu.VMEM((8, 8, 16, PAIR), LOW), pltpu.VMEM((4, 2, 2, 16, PAIR), LOW), pltpu.VMEM((4, 2, 4, 16, PAIR), LOW),
-            pltpu.VMEM((2, 2, 16, PAIR), LOW), pltpu.VMEM((2, 4, 16, PAIR), LOW), pltpu.VMEM((8, ROWS, MODEL), LOW),
+            pltpu.VMEM((8, 8, 16, SLAB), LOW), pltpu.VMEM((4, 2, 2, 16, SLAB), LOW), pltpu.VMEM((4, 2, 4, 16, SLAB), LOW),
+            pltpu.VMEM((2, 2, 16, SLAB), LOW), pltpu.VMEM((2, 4, 16, SLAB), LOW), pltpu.VMEM((8, ROWS, MODEL), LOW),
             pltpu.VMEM((8, ROWS, MODEL), LOW),
         ]
         + scatter_bufs()
         + [
             pltpu.VMEM((8, 16, 16, 1024), LOW), pltpu.VMEM((8, 8, 16, 1024), LOW), pltpu.VMEM((2, 2, 4, 16, 1024), LOW),
             pltpu.VMEM((2, 2, 8, 16, 1024), LOW), pltpu.VMEM((8, 16, 1024), LOW),
-            pltpu.VMEM(blocks, LOW), pltpu.VMEM((4, ROWS, PAIR), LOW), pltpu.VMEM((2, 8, 2, 16, PAIR), LOW), pltpu.VMEM(blocks, LOW),
+            pltpu.VMEM((8, ROWS, MODEL), LOW),
             pltpu.VMEM((1024, PROJ), LOW), pltpu.VMEM((2, 2, 256, 1024), LOW), pltpu.VMEM((1024, PART), LOW),
             pltpu.VMEM((1024, PART), LOW), pltpu.VMEM((1024, PROJ), LOW),
             pltpu.VMEM((1024, PART), WIDE), pltpu.VMEM((1024, PART), WIDE), pltpu.VMEM((2, 8, 2, 16, 1024), LOW),
@@ -1119,7 +1088,7 @@
         ],
         compiler_params=pltpu.CompilerParams(collective_id=3, has_side_effects=True, vmem_limit_bytes=62 * 2**20),
         name="back",
-    )(branch_grad, grad_resid, x, live, resid, branch, twos, pair, ones, wa, qkv, probs, att)
+    )(branch_grad, grad_resid, x, live, resid, branch, acc, ones, wa, qkv, probs, att)
 def weights_out(attn_weight, mlp_weight, gain_one, gain_two):
     proj = (attn_weight[:, :3].astype(WIDE) * gain_one).astype(LOW).reshape(16, 3, 8, PART)
     proj = proj.transpose(2, 0, 1, 3).reshape(8, 16, PROJ)
@@ -1133,7 +1102,8 @@
     return jnp.concatenate([proj, out], axis=2), jnp.concatenate([pair, down], axis=2)
 
 
-def weights_back(pair, down, proj, out, units):
+def weights_back(slab, proj, out, units):
+    pair, down = slab[..., :PAIR], slab[..., PAIR:]
     proj = proj.reshape(8, 16, 3, PART).transpose(1, 2, 0, 3).reshape(16, 3, MODEL).astype(WIDE)
     out = out.transpose(1, 0, 2).reshape(16, MODEL).astype(WIDE)
     pair = pair.reshape(4, 16, UNITS // 128, 2, 128).transpose(1, 3, 0, 2, 4).reshape(16, 2, 4, UNITS)
@@ -1153,11 +1123,11 @@
     gain_two = norm2_gain.astype(WIDE)[:, None, None]
     wa_own, wm_own = weights_out(attn_weight, mlp_weight, gain_one, gain_two)
     ones, wa, grads, wm, qkv, probs, att, resid, two = front(x, live, cot, wa_own, wm_own, pos)
-    twos, hidden, pair, branch, grad_resid, branch_grad, down_own = mlp(two, resid, cot, live, grads, wm)
-    layer_out, input_grad, pair_own, in_own, out_own = back(
-        branch_grad, grad_resid, x, live, resid, branch, twos, pair, ones, wa, qkv, probs, att
+    acc, branch, grad_resid, branch_grad = mlp(two, resid, cot, live, grads, wm)
+    layer_out, input_grad, slab_own, in_own, out_own = back(
+        branch_grad, grad_resid, x, live, resid, branch, acc, ones, wa, qkv, probs, att
     )
-    in_sum, out_sum, pair_sum, down_sum = weights_back(pair_own, down_own, in_own, out_own, mlp_weight.shape[2])
+    in_sum, out_sum, pair_sum, down_sum = weights_back(slab_own, in_own, out_own, mlp_weight.shape[2])
     attn_grad = jnp.concatenate([in_sum * gain_one, out_sum[:, None]], axis=1)
     mlp_grad = jnp.concatenate([pair_sum * gain_two, down_sum[:, None]], axis=1)
     gain_one_grad = jnp.sum(in_sum * attn_weight[:, :3].astype(WIDE), axis=(1, 2))

time: 430 us -> 375 us (0.87)
  Pallas kernels: 402 us -> 346 us
    pallas_call x1, Pallas kernels: 106 us -> 69.7 us  [mlp(): pl.pallas_call(mlp_kernel, out_shape=(shape((8, 8, 16, SLAB), LOW), shape...]
    pallas_call x1, Pallas kernels: 148 us -> 138 us  [back(): pl.pallas_call(back_kernel, out_shape=(shape((ROWS, MODEL), LOW), shape((...]
    pallas_call x1, Pallas kernels: 148 us -> 139 us  [front(): pl.pallas_call(front_kernel, out_shape=(shape((8, ROWS, MODEL), LOW), sha...]
where the time goes in v3:
time: 375 us; the launch traced here: 369 us
  Pallas kernels  346 us (92%)
  local copies, waits for them, and re-layouts  11.2 us (3%)
  other arithmetic  8.99 us (2%)
    pallas_call x1, Pallas kernels, front(): pl.pallas_call(front_kernel, out_shape=(shape((8, ROWS, MODEL), LOW), sha...  139 us
    pallas_call x1, Pallas kernels, back(): pl.pallas_call(back_kernel, out_shape=(shape((ROWS, MODEL), LOW), shape((...  138 us
    pallas_call x1, Pallas kernels, mlp(): pl.pallas_call(mlp_kernel, out_shape=(shape((8, 8, 16, SLAB), LOW), shape...  69.7 us

profile of v3, /device:TPU:0, one launch (start us, length us, event | category | flops | bytes accessed | tf_op | source)
XLA Modules:
  0.0 368.7 jit_solution(17396296501161305194)
XLA Ops:
  1.3 0.7 convert_element_type.86
  2.0 0.7 convert_element_type.89
  2.6 0.7 multiply_bitcast_fusion
  3.4 0.6 fusion.4.live_ref
  4.0 1.3 slice_reduce_fusion
  5.4 0.9 slice.28
  6.3 0.2 reshape_squeeze.7
  7.0 0.2 reshape.134
  7.2 0.7 pad_maximum_fusion.3.wa_own
  8.1 0.4 reshape.135
  8.6 0.2 reshape.136
  8.8 0.4 copy.32
  9.4 0.8 pad_maximum_fusion.1.wm_own
  10.2 1.0 copy.34.pos_q
  11.3 138.9 %front.1 = (bf16[8,128,2048]{2,1,0:T(8,128)(2,1)}, bf16[8,16,16,1024]{3,2,1,0:T(8,128)(2,1)}, bf16[4,128,2048]{2,1,0:T(8,128)(2,1)}, bf16[8,16,16,4224]{3,2,1,0:...) custom-call(bf16[128,2048]{1,0:T(8,128)(2,1)} %bitcast.53, ...), custom_call_target="tpu_custom_call" | custom-call | tf_op jit(solution)/shard_map/front/pallas_call | solution.py:741
  150.2 69.7 %mlp.1 = (bf16[8,8,16,4224]{3,2,1,0:T(8,128)(2,1)}, bf16[4,128,2048]{2,1,0:T(8,128)(2,1)}, f32[128,2048]{1,0:T(8,128)}, bf16[128,2048]{1,0:T(8,128)(2,1)}) custom-call(bf16[128,2048]{1,0:T(8,128)(2,1)} %get-tuple-element.24.two_ref, f32[128,2048]{1,0:T(8,128)} %get-tuple-element.25.resid, bf16[128,2048]{1,0:T(8,128)(2,1)} %bitcast.59, ...), custom_call_target="tpu_custom_call" | custom-call | tf_op jit(solution)/shard_map/mlp/pallas_call | solution.py:895
  219.9 137.8 %back.1 = (bf16[128,2048]{1,0:T(8,128)(2,1)}, f32[128,2048]{1,0:T(8,128)}, bf16[4,16,4224]{2,1,0:T(8,128)(2,1)}, bf16[8,16,768]{2,1,0:T(8,128)(2,1)}, bf16[8,16,256]{2,1,0:T(8,128)(2,1)}) custom-call(bf16[128,2048]{1,0:T(8,128)(2,1)} %get-tuple-element.28.branch_grad, f32[128,2048]{1,0:T(8,128)} %get-tuple-element.29.grad_resid, bf16[128,2048]{1,0:T(8,128)(2,1)} %bitcast.54, ...), custom_call_target="tpu_custom_call" | custom-call | tf_op jit(solution)/shard_map/back/pallas_call | solution.py:1066
  357.7 0.9 convert_bitcast_fusion.1
  358.7 0.9 convert_bitcast_fusion
  359.7 1.0 slice.29
  360.9 0.2 reshape.143
  361.2 0.2 reshape.139
  361.5 0.3 copy.38
  361.8 0.4 reshape.142
  362.2 0.7 broadcast_multiply_fusion
  362.9 1.0 pad_maximum_fusion
  364.0 0.2 reshape.144
  364.2 0.2 copy.35
  364.5 0.8 broadcast_multiply_fusion.1
  365.3 1.1 copy.40
  366.5 0.8 copy.53
  367.3 1.0 copy.54
  (31 shorter events, 1.4 us)
Async XLA Ops:
  0.6 6.0 %copy-start = (bf16[16,4,2048]{2,1,0:T(4,128)(2,1)S(1)}, bf16[16,4,2048]{2,1,0:T(4,128)(2,1)}, u32[]{:S(2)}) copy-start(bf16[16,4,2048]{2,1,0:T(4,128)(2,1)} %param.12) | copy-start | bytes 786436
  3.4 6.8 %copy-start.5 = (s32[8,128]{1,0:T(8,128)}, s32[8,128]{1,0:T(8,128)S(1)}, u32[]{:S(2)}) copy-start(s32[8,128]{1,0:T(8,128)S(1)} %iota_add_fusion) | copy-start | bytes 12292
  6.6 1.4 copy-start.1
  362.2 1.8 copy-start.4
  364.5 2.0 copy-start.3
  365.3 2.0 copy-start.2

commit v4 on v3

--- a/solution.py
+++ b/solution.py
@@ -322,9 +322,10 @@
         got(7 + 4 * k, at(xs[k], zf, 1))
         fwd(23 + 4 * k, at(xs[k], zf), TW)
 
+    z_first(0)
+    yield
     fwd(0, at(me.x, z), XU)
     fwd(1, at(me.x, z), XD)
-    z_first(0)
     yield
     got(0, at(me.x_down, z))
     fwd(2, at(me.x_down, z, 0), XU)
@@ -333,24 +334,16 @@
     z_first(1)
     z_first(2)
     yield
-    z_second(0)
-    yield
     got(2, at(me.x_far, z, 0))
     got(3, at(me.x_far, z, 1))
     z_first(3)
     yield
-    z_second(1)
-    yield
-    z_third(0)
-    z_second(2)
-    yield
-    z_third(1)
-    yield
-    z_second(3)
-    z_third(2)
-    yield
-    z_third(3)
-    yield
+    for k in range(4):
+        z_second(k)
+        yield
+    for k in range(4):
+        z_third(k)
+        yield
     for k in range(4):
         for i, zz in enumerate((z, zd, zu, zf)):
             got(20 + 4 * k + i, at(xs[k], zz, twin=True))
@@ -616,8 +609,17 @@
                 tasks.remove(task)
 
 
-def step(task):
-    return next(task, None)
+def step(task, count=1):
+    for _ in range(count):
+        next(task, None)
+
+
+def finish(task, *others):
+    k = 0
+    while next(task, others) is not others:
+        k += 1
+        if k % 2 == 0 and others:
+            step(others[k // 2 % len(others)])
 def dot(a, b, dims=((1,), (0,))):
     return lax.dot_general(a, b, (dims, ((), ())), preferred_element_type=WIDE)
 
@@ -629,7 +631,7 @@
 def front_kernel(
     x_ref, live_ref, cot_ref, wa_own, wm_own, pos_q, pos_k,
     one_out, wa_out, grad_all, wm, qkv_out, probs_out, att_out, resid, two,
-    one_all, wa, grad_own, qkv, probs, att, part, qx, q2, q1, p2, p1, px, send, recv, local_sem,
+    one_all, wa, grad_own, qkv, probs, att, ones_t, att_t, part, qx, q2, q1, p2, p1, px, send, recv, local_sem,
 ):
     me = Place()
     mail = Mail(send, recv)
@@ -657,21 +659,23 @@
     step(swap_a)
     gather_wa = gather_dp(me, mail, wa)
     step(gather_wa)
+    grad_own[...] = (cot_ref[...].astype(WIDE) * live_ref[...]).astype(LOW)
+    save(grad_own, grad_all.at[me.y])
+    step(gather_one)
+    step(gather_wa)
+    step(gather_one)
+    step(gather_wa, 2)
+    step(gather_one)
+    step(gather_wa, 2)
     step(swap_m)
     keep_m.wait()
     gather_wm = gather_xz(me, mail, wm)
-    step(gather_wm)
-    grad_own[...] = (cot_ref[...].astype(WIDE) * live_ref[...]).astype(LOW)
-    save(grad_own, grad_all.at[me.y])
-    for i in range(8):
-        step(gather_one)
-        step(gather_wa)
-        if i in (2, 4, 6):
-            step(gather_wm)
-    run(gather_one, gather_wa)
+    step(gather_wm, 2)
+    step(gather_one, 2)
     gather_g = gather_y(me, mail, grad_own, grad_all)
     step(gather_g)
-    save(one_all, one_out)
+    run(gather_one, gather_wa)
+    step(gather_wm)
     save(wa, wa_out)
 
     def project(i, carry):
@@ -706,10 +710,8 @@
 
         lax.fori_loop(0, 8, piece, 0)
 
-    for i in range(2):
-        lax.fori_loop(2 * i, 2 * i + 2, project, 0)
-        step(gather_g)
-        step(gather_wm)
+    lax.fori_loop(0, 4, project, 0)
+    step(gather_g)
     save(qkv, qkv_out)
 
     def write(lo, hi, rows):
@@ -718,16 +720,29 @@
         two[lo:hi] = (total * row_scale(total) * live_ref[lo:hi]).astype(LOW)
 
     scatter = scatter_seq(me, mail, part, (qx, q2, q1, p2, p1, px), write)
-    for col in (me.b, me.a):
-        for i in range(2):
-            lax.fori_loop(col * 4 + 2 * i, col * 4 + 2 * i + 2, attend, 0)
-            step(gather_wm)
-            step(gather_g)
-        out_project(col)
-        step(scatter)
+    lax.fori_loop(me.b * 4, me.b * 4 + 4, attend, 0)
+    out_project(me.b)
+    step(scatter)
+    step(gather_wm)
+    lax.fori_loop(me.a * 4, me.a * 4 + 4, attend, 0)
+    out_project(me.a)
+    step(scatter)
     save(probs, probs_out)
-    save(att, att_out)
-    run(scatter, gather_wm, gather_g)
+    finish(scatter, gather_wm)
+    step(gather_wm)
+
+    def turn(s, carry):
+        columns = pl.ds(pl.multiple_of(s * 256, 256), 256)
+        ones_t[s] = one_all[:, :, columns].reshape(8 * ROWS, 256).T
+        return carry
+
+    att_t[...] = att[...].T
+    save(att_t, att_out)
+    for i in range(4):
+        lax.fori_loop(2 * i, 2 * i + 2, turn, 0)
+        step(gather_wm)
+    save(ones_t, one_out)
+    run(gather_wm, gather_g)
     for copy in saves:
         if copy is not keep_m:
             copy.wait()
@@ -741,15 +756,16 @@
     return pl.pallas_call(
         front_kernel,
         out_shape=(
-            shape((8, ROWS, MODEL), LOW), shape((8, 16, 16, 1024), LOW), shape((4, ROWS, MODEL), LOW),
+            shape((8, 256, 1024), LOW), shape((8, 16, 16, 1024), LOW), shape((4, ROWS, MODEL), LOW),
             shape((8, 16, 16, SLAB), LOW), shape((1024, PROJ), LOW), shape((2, 1024, 1024), LOW),
-            shape((1024, PART), LOW), shape((ROWS, MODEL), WIDE), shape((ROWS, MODEL), LOW),
+            shape((PART, 1024), LOW), shape((ROWS, MODEL), WIDE), shape((ROWS, MODEL), LOW),
         ),
         in_specs=[vmem] * 4 + [anywhere] + [vmem] * 2,
         out_specs=(anywhere,) * 7 + (vmem, vmem),
         scratch_shapes=[
             pltpu.VMEM((8, ROWS, MODEL), LOW), pltpu.VMEM((8, 16, 16, 1024), LOW), pltpu.VMEM((ROWS, MODEL), LOW),
             pltpu.VMEM((1024, PROJ), LOW), pltpu.VMEM((2, 1024, 1024), LOW), pltpu.VMEM((1024, PART), LOW),
+            pltpu.VMEM((8, 256, 1024), LOW), pltpu.VMEM((PART, 1024), LOW),
             pltpu.VMEM((8, ROWS, MODEL), LOW),
         ]
         + scatter_bufs()
@@ -760,7 +776,7 @@
 def mlp_kernel(
     two_ref, resid, cot_ref, live_ref, grad_all, wm_all,
     acc_out, branch_out, grad_resid, grad_branch,
-    wm, grads, twos, hidden, pair, part, branch, p2, p1,
+    wm, grads, twos, hidden, pair, grads_t, part, branch, p2, p1,
     stage, acc, send, recv, local_sem,
 ):
     me = Place()
@@ -848,6 +864,13 @@
 
     scatter = scatter_y(me, mail, part, p2, p1, write)
     ahead([me.y])
+
+    def turn(s, carry):
+        columns = pl.ds(pl.multiple_of(s * 256, 256), 256)
+        grads_t[s] = grads[:, :, columns].reshape(4 * ROWS, 256).T
+        return carry
+
+    lax.fori_loop(0, 8, turn, 0)
     step(gather)
     ahead([me.up, me.down])
     back([me.up, me.down])
@@ -857,7 +880,10 @@
     back([me.far])
     step(scatter)
     back([me.y])
+    down_back([me.y, me.up, me.down, me.far])
     step(scatter)
+
+    save(branch, branch_out)
     order = [me.a * 4 + i for i in range(4)] + [me.b * 4 + i for i in range(4)]
 
     def product(s, out):
@@ -865,24 +891,17 @@
         rows = twos[:, :, columns].reshape(4 * ROWS, 256).T
         terms = dot(rows, pair[...].reshape(4 * ROWS, PAIR))
         out[:, :, :, 0:PAIR] = terms.reshape(8, 2, 16, PAIR).astype(LOW)
-        rows = grads[:, :, columns].reshape(4 * ROWS, 256).T
-        terms = dot(rows, hidden[...].reshape(4 * ROWS, UNITS))
+        terms = dot(grads_t[s], hidden[...].reshape(4 * ROWS, UNITS))
         out[:, :, :, PAIR:] = terms.reshape(8, 2, 16, UNITS).astype(LOW)
 
     def kept(i):
         save(acc.at[order[i]], acc_out.at[order[i]])
 
     twin = twin_sum(me, mail, stage, acc, order, product, kept)
-    for i in range(3):
-        step(twin)
-    step(scatter)
-    for i in range(3):
-        step(twin)
+    step(twin, 3)
     step(scatter)
     run(twin)
-    down_back([me.y, me.up, me.down, me.far])
-    save(branch, branch_out)
-    run(scatter, gather)
+    run(scatter)
     for copy in saves[2:]:
         copy.wait()
     mail.finish()
@@ -901,10 +920,10 @@
         out_specs=(anywhere,) * 2 + (vmem,) * 2,
         scratch_shapes=[
             pltpu.VMEM((8, 16, 16, SLAB), LOW), pltpu.VMEM(blocks, LOW), pltpu.VMEM(blocks, LOW),
-            pltpu.VMEM((4, ROWS, UNITS), LOW), pltpu.VMEM((4, ROWS, PAIR), LOW), pltpu.VMEM(blocks, LOW),
+            pltpu.VMEM((4, ROWS, UNITS), LOW), pltpu.VMEM((4, ROWS, PAIR), LOW), pltpu.VMEM((8, 256, 4 * ROWS), LOW), pltpu.VMEM(blocks, LOW),
             pltpu.VMEM(blocks, LOW), pltpu.VMEM((2, ROWS // 2, MODEL), LOW), pltpu.VMEM((2, ROWS, MODEL), LOW),
             pltpu.VMEM((2, 8, 2, 16, SLAB), LOW), pltpu.VMEM((8, 8, 16, SLAB), LOW),
-            pltpu.SemaphoreType.DMA((18,)), pltpu.SemaphoreType.DMA((18,)), pltpu.SemaphoreType.DMA((11,)),
+            pltpu.SemaphoreType.DMA((24,)), pltpu.SemaphoreType.DMA((24,)), pltpu.SemaphoreType.DMA((11,)),
         ],
         compiler_params=pltpu.CompilerParams(collective_id=2, has_side_effects=True, vmem_limit_bytes=62 * 2**20),
         name="mlp",
@@ -912,8 +931,8 @@
 def back_kernel(
     branch_grad, grad_resid, x_ref, live_ref, resid, branch_all, acc_all, one_all, wa_all, qkv_all, probs_all, att_all,
     layer_out, input_grad, slab_own, in_own, out_own,
-    acc, z_over, z_near, x_over, x_near, grads, part, qx, q2, q1, p2, p1, px,
-    wa, acc_a, az_over, az_near, h_near, ones, qkv, probs, att, grad_att, grad_proj, grad_k, grad_v, stage_a,
+    acc, z_over, z_near, x_over, x_near, grads, branch, b2, b1, part, qx, q2, q1, p2, p1, px,
+    wa, acc_a, az_over, az_near, h_near, ones_t, qkv, probs, att_t, grad_att, grad_proj, grad_k, grad_v, stage_a,
     send, recv, local_sem,
 ):
     me = Place()
@@ -932,8 +951,8 @@
     gather = gather_seq(me, mail, grads.at[me.seq], grads)
     step(gather)
     load_wa = load(wa_all, wa)
-    load_branch = load(branch_all, part.at[0:4])
-    waits = [load(*both) for both in ((qkv_all, qkv), (att_all, att), (one_all, ones))]
+    load_branch = load(branch_all, branch)
+    waits = [load(*both) for both in ((qkv_all, qkv), (att_all, att_t), (one_all, ones_t))]
     fetch = [load(probs_all.at[:, 256 * i : 256 * i + 256], probs.at[i]) for i in range(2)]
     order = [me.a * 4 + i for i in range(4)] + [me.b * 4 + i for i in range(4)]
 
@@ -950,13 +969,15 @@
     step(sums)
     load_acc[1].wait()
     step(sums)
-    for i in range(3):
-        step(gather)
-        step(sums)
+    step(gather, 4)
 
     def write_out(lo, hi, rows):
         layer_out[lo:hi] = (live_ref[lo:hi] * (resid[lo:hi] + rows)).astype(LOW)
 
+    out_sum = scatter_y(me, mail, branch, b2, b1, write_out)
+    load_branch.wait()
+    step(out_sum, 2)
+    run(gather)
     def write_grad(lo, hi, rows):
         x = x_ref[lo:hi].astype(WIDE)
         scale = row_scale(x)
@@ -964,16 +985,8 @@
         inner = jnp.mean(rows * hat, axis=-1, keepdims=True)
         input_grad[lo:hi] = grad_resid[lo:hi] + live_ref[lo:hi] * scale * (rows - hat * inner)
 
-    class Lower:
-        at = {0: part.at[6, 0 : ROWS // 2], 1: part.at[6, ROWS // 2 : ROWS]}
-
-    out_sum = scatter_y(me, mail, part.at[0:4], Lower, part.at[4:6], write_out)
     grad_sum = scatter_seq(me, mail, part, (qx, q2, q1, p2, p1, px), write_grad)
 
-    run(gather)
-    load_branch.wait()
-    out_slots = range(mail.count, mail.count + 6)
-    step(out_sum)
     load_wa.wait()
     for wait in waits:
         wait.wait()
@@ -988,8 +1001,6 @@
         return carry
 
     lax.fori_loop(0, 4, attended_grad, 0)
-    step(out_sum)
-    step(sums)
     grad_k[...] = jnp.zeros_like(grad_k)
     grad_v[...] = jnp.zeros_like(grad_v)
 
@@ -1010,13 +1021,11 @@
     for i in range(4):
         fetch[i].wait()
         attend_back(i)
+        if i == 1:
+            step(out_sum)
         if i < 2:
             fetch.append(load(probs_all.at[:, 256 * i + 512 : 256 * i + 768], probs.at[i]))
         step(sums)
-        step(out_sum)
-    run(out_sum)
-    for slot in out_slots:
-        mail.sent(slot)
     grad_proj[:, PART : 2 * PART] = (grad_k[...] * head_scale).astype(LOW)
     grad_proj[:, 2 * PART :] = grad_v[...].astype(LOW)
 
@@ -1032,21 +1041,17 @@
         lax.fori_loop(0, 8, piece, 0)
 
     def product(s, out):
-        rows = ones[:, :, columns_of(s)].reshape(8 * ROWS, 256).T
-        terms = dot(rows, grad_proj[...])
+        terms = dot(ones_t[s], grad_proj[...])
         out[:, :, :, 0:PROJ] = terms.reshape(8, 2, 16, PROJ).astype(LOW)
         rows = grads[:, :, columns_of(s)].reshape(8 * ROWS, 256)
-        terms = dot(att[...], rows, ((0,), (0,)))
-        out[:, :, :, PROJ:] = terms.reshape(8, 2, 16, PART).astype(LOW)
+        out[:, :, :, PROJ:] = dot(att_t[...], rows).reshape(8, 2, 16, PART).astype(LOW)
 
     twin = twin_sum(me, mail, stage_a, acc_a, order, product)
     norm_terms(me.b)
     step(grad_sum)
-    for i in range(9):
-        step(twin)
+    step(twin, 9)
     norm_terms(me.a)
     step(grad_sum)
-    step(sums)
 
     def proj_sums():
         yield from scatter_hz(me, mail, acc_a, az_over, az_near, h_near)
@@ -1054,8 +1059,10 @@
         out_own[...] = own[:, :, PROJ:]
         yield from send_seq(me, mail, own, in_own, 0, PROJ)
 
-    run(proj_sums(), grad_sum, sums)
-
+    rest = proj_sums()
+    step(rest)
+    finish(grad_sum, sums)
+    run(rest, sums, out_sum)
     mail.finish()
 
 
@@ -1074,14 +1081,15 @@
         scratch_shapes=[
             pltpu.VMEM((8, 8, 16, SLAB), LOW), pltpu.VMEM((4, 2, 2, 16, SLAB), LOW), pltpu.VMEM((4, 2, 4, 16, SLAB), LOW),
             pltpu.VMEM((2, 2, 16, SLAB), LOW), pltpu.VMEM((2, 4, 16, SLAB), LOW), pltpu.VMEM((8, ROWS, MODEL), LOW),
+            pltpu.VMEM((4, ROWS, MODEL), LOW), pltpu.VMEM((2, ROWS // 2, MODEL), LOW), pltpu.VMEM((2, ROWS, MODEL), LOW),
             pltpu.VMEM((8, ROWS, MODEL), LOW),
         ]
         + scatter_bufs()
         + [
             pltpu.VMEM((8, 16, 16, 1024), LOW), pltpu.VMEM((8, 8, 16, 1024), LOW), pltpu.VMEM((2, 2, 4, 16, 1024), LOW),
             pltpu.VMEM((2, 2, 8, 16, 1024), LOW), pltpu.VMEM((8, 16, 1024), LOW),
-            pltpu.VMEM((8, ROWS, MODEL), LOW),
-            pltpu.VMEM((1024, PROJ), LOW), pltpu.VMEM((2, 2, 256, 1024), LOW), pltpu.VMEM((1024, PART), LOW),
+            pltpu.VMEM((8, 256, 1024), LOW),
+            pltpu.VMEM((1024, PROJ), LOW), pltpu.VMEM((2, 2, 256, 1024), LOW), pltpu.VMEM((PART, 1024), LOW),
             pltpu.VMEM((1024, PART), LOW), pltpu.VMEM((1024, PROJ), LOW),
             pltpu.VMEM((1024, PART), WIDE), pltpu.VMEM((1024, PART), WIDE), pltpu.VMEM((2, 8, 2, 16, 1024), LOW),
             pltpu.SemaphoreType.DMA((count,)), pltpu.SemaphoreType.DMA((count,)), pltpu.SemaphoreType.DMA((12,)),

time: 375 us -> 343 us (0.915)
  Pallas kernels: 346 us -> 315 us
    pallas_call x1, Pallas kernels: 139 us -> 121 us  [front(): pl.pallas_call(front_kernel, out_shape=(shape((8, 256, 1024), LOW), shape...]
    pallas_call x1, Pallas kernels: 138 us -> 126 us  [back(): pl.pallas_call(back_kernel, out_shape=(shape((ROWS, MODEL), LOW), shape((...]
where the time goes in v4:
time: 343 us; the launch traced here: 337 us
  Pallas kernels  315 us (92%)
  local copies, waits for them, and re-layouts  11.2 us (3%)
  other arithmetic  8.99 us (3%)
    pallas_call x1, Pallas kernels, back(): pl.pallas_call(back_kernel, out_shape=(shape((ROWS, MODEL), LOW), shape((...  126 us
    pallas_call x1, Pallas kernels, front(): pl.pallas_call(front_kernel, out_shape=(shape((8, 256, 1024), LOW), shape...  121 us
    pallas_call x1, Pallas kernels, mlp(): pl.pallas_call(mlp_kernel, out_shape=(shape((8, 8, 16, SLAB), LOW), shape...  67.8 us

profile of v4, /device:TPU:0, one launch (start us, length us, event | category | flops | bytes accessed | tf_op | source)
XLA Modules:
  0.0 337.5 jit_solution(16006248707867309643)
XLA Ops:
  1.3 0.7 convert_element_type.86
  2.0 0.7 convert_element_type.89
  2.6 0.7 multiply_bitcast_fusion
  3.4 0.6 fusion.4.live_ref
  4.0 1.3 slice_reduce_fusion
  5.4 0.9 slice.28
  6.3 0.2 reshape_squeeze.7
  7.0 0.2 reshape.134
  7.2 0.7 pad_maximum_fusion.3.wa_own
  8.1 0.4 reshape.135
  8.6 0.2 reshape.136
  8.8 0.4 copy.32
  9.4 0.8 pad_maximum_fusion.1.wm_own
  10.2 1.0 copy.34.pos_q
  11.3 121.2 %front.1 = (bf16[8,256,1024]{2,1,0:T(8,128)(2,1)}, bf16[8,16,16,1024]{3,2,1,0:T(8,128)(2,1)}, bf16[4,128,2048]{2,1,0:T(8,128)(2,1)}, bf16[8,16,16,4224]{3,2,1,0:...) custom-call(bf16[128,2048]{1,0:T(8,128)(2,1)} %bitcast.53, ...), custom_call_target="tpu_custom_call" | custom-call | tf_op jit(solution)/shard_map/front/pallas_call | solution.py:756
  132.5 67.8 %mlp.1 = (bf16[8,8,16,4224]{3,2,1,0:T(8,128)(2,1)}, bf16[4,128,2048]{2,1,0:T(8,128)(2,1)}, f32[128,2048]{1,0:T(8,128)}, bf16[128,2048]{1,0:T(8,128)(2,1)}) custom-call(bf16[128,2048]{1,0:T(8,128)(2,1)} %get-tuple-element.24.two_ref, f32[128,2048]{1,0:T(8,128)} %get-tuple-element.25.resid, bf16[128,2048]{1,0:T(8,128)(2,1)} %bitcast.59, ...), custom_call_target="tpu_custom_call" | custom-call | tf_op jit(solution)/shard_map/mlp/pallas_call | solution.py:914
  200.3 126.2 %back.1 = (bf16[128,2048]{1,0:T(8,128)(2,1)}, f32[128,2048]{1,0:T(8,128)}, bf16[4,16,4224]{2,1,0:T(8,128)(2,1)}, bf16[8,16,768]{2,1,0:T(8,128)(2,1)}, bf16[8,16,256]{2,1,0:T(8,128)(2,1)}) custom-call(bf16[128,2048]{1,0:T(8,128)(2,1)} %get-tuple-element.28.branch_grad, f32[128,2048]{1,0:T(8,128)} %get-tuple-element.29.grad_resid, bf16[128,2048]{1,0:T(8,128)(2,1)} %bitcast.54, ...), custom_call_target="tpu_custom_call" | custom-call | tf_op jit(solution)/shard_map/back/pallas_call | solution.py:1073
  326.5 0.9 convert_bitcast_fusion.1
  327.4 0.9 convert_bitcast_fusion
  328.4 1.0 slice.29
  329.6 0.2 reshape.143
  329.9 0.2 reshape.139
  330.2 0.3 copy.38
  330.5 0.4 reshape.142
  330.9 0.7 broadcast_multiply_fusion
  331.6 1.0 pad_maximum_fusion
  332.7 0.2 reshape.144
  332.9 0.2 copy.35
  333.2 0.8 broadcast_multiply_fusion.1
  334.1 1.1 copy.40
  335.2 0.8 copy.53
  336.0 1.0 copy.54
  (31 shorter events, 1.4 us)
Async XLA Ops:
  0.6 6.0 %copy-start = (bf16[16,4,2048]{2,1,0:T(4,128)(2,1)S(1)}, bf16[16,4,2048]{2,1,0:T(4,128)(2,1)}, u32[]{:S(2)}) copy-start(bf16[16,4,2048]{2,1,0:T(4,128)(2,1)} %param.12) | copy-start | bytes 786436
  3.4 6.8 %copy-start.5 = (s32[8,128]{1,0:T(8,128)}, s32[8,128]{1,0:T(8,128)S(1)}, u32[]{:S(2)}) copy-start(s32[8,128]{1,0:T(8,128)S(1)} %iota_add_fusion) | copy-start | bytes 12292
  6.6 1.4 copy-start.1
  330.9 1.8 copy-start.4
  333.2 2.0 copy-start.3
  334.0 2.0 copy-start.2

commit v5 on v4

--- a/solution.py
+++ b/solution.py
@@ -18,7 +18,7 @@
 UNITS = 1408
 SLAB = 3 * UNITS
 PAIR = 2 * UNITS
-FIRST = 80
+FIRST = 96
 MID = MODEL // 2
 
 
@@ -55,11 +55,11 @@
         return [{"seq": (self.seq + k) % 8} for k in range(1, 8)]
 
 
-def enter(devices):
+def greet(devices):
     barrier = pltpu.get_barrier_semaphore()
     for device in devices:
         pl.semaphore_signal(barrier, inc=1, device_id=device, device_id_type=MESH)
-    pl.semaphore_wait(barrier, len(devices))
+    return lambda: pl.semaphore_wait(barrier, len(devices))
 
 
 class Mail:
@@ -181,26 +181,25 @@
     y, up, down, far = me.y, me.up, me.down, me.far
     U, D = me.up_dev, me.down_dev
     n = mail.slots(6)
-    H = ROWS // 2
-    mail.go(n + 2, part.at[up, H:ROWS], p1.at[0, H:ROWS], U)
-    mail.go(n + 3, part.at[down, 0:H], p1.at[1, 0:H], D)
-    yield
-    mail.go(n, part.at[far, 0:H], p2.at[0], U)
-    mail.go(n + 1, part.at[far, H:ROWS], p2.at[1], D)
+    left, right = pl.ds(0, MID), pl.ds(MID, MID)
+    mail.go(n, part.at[far, :, left], p2.at[0], U)
+    mail.go(n + 3, part.at[down, :, left], p1.at[1, :, left], D)
+    yield
+    mail.go(n + 1, part.at[far, :, right], p2.at[1], D)
+    mail.go(n + 2, part.at[up, :, right], p1.at[0, :, right], U)
     yield
     mail.arrived(n, p2.at[0], D)
-    add(part.at[up, 0:H], p2.at[0])
-    mail.go(n + 4, part.at[up, 0:H], p1.at[0, 0:H], U)
+    add(part.at[up, :, left], p2.at[0])
+    mail.go(n + 4, part.at[up, :, left], p1.at[0, :, left], U)
     mail.arrived(n + 1, p2.at[1], U)
-    add(part.at[down, H:ROWS], p2.at[1])
-    mail.go(n + 5, part.at[down, H:ROWS], p1.at[1, H:ROWS], D)
-    yield
-    mail.arrived(n + 2, p1.at[0, H:ROWS], D)
-    mail.arrived(n + 5, p1.at[1, H:ROWS], U)
-    out(H, ROWS, val(part.at[y, H:ROWS]) + val(p1.at[0, H:ROWS]) + val(p1.at[1, H:ROWS]))
-    mail.arrived(n + 3, p1.at[1, 0:H], U)
-    mail.arrived(n + 4, p1.at[0, 0:H], D)
-    out(0, H, val(part.at[y, 0:H]) + val(p1.at[0, 0:H]) + val(p1.at[1, 0:H]))
+    add(part.at[down, :, right], p2.at[1])
+    mail.go(n + 5, part.at[down, :, right], p1.at[1, :, right], D)
+    yield
+    mail.arrived(n + 2, p1.at[0, :, right], D)
+    mail.arrived(n + 3, p1.at[1, :, left], U)
+    mail.arrived(n + 4, p1.at[0, :, left], D)
+    mail.arrived(n + 5, p1.at[1, :, right], U)
+    out(0, ROWS, val(part.at[y]) + val(p1.at[0]) + val(p1.at[1]))
 
 
 def val(ref):
@@ -425,16 +424,14 @@
         mail.sent(n + i)
 
 
-def scatter_xz(me, mail, acc, z_over, z_near, x_over, x_near):
+def scatter_z(me, mail, acc, z_over, z_near):
     xs = (me.x_far, me.x, me.x_up, me.x_down)
     zs = (me.z, me.z_up, me.z_down, me.z_far)
-    XU, XD, ZU, ZD = me.x_up_dev, me.x_down_dev, me.z_up_dev, me.z_down_dev
 
     def at(x):
         return lambda z: acc.at[pl.ds(x % 2 * 4, 4), z * 2 + x // 2]
 
-    rings = [RingSum(mail, at(x), zs, (ZU, ZD), z_over.at[k], z_near.at[k]) for k, x in enumerate(xs)]
-    ring = RingSum(mail, lambda x: at(x)(me.z), (me.x, me.x_up, me.x_down, me.x_far), (XU, XD), x_over, x_near)
+    rings = [RingSum(mail, at(x), zs, (me.z_up_dev, me.z_down_dev), z_over.at[k], z_near.at[k]) for k, x in enumerate(xs)]
     rings[0].first()
     yield
     rings[2].first()
@@ -447,9 +444,13 @@
     for k in (0, 2, 3):
         rings[k].third()
         yield
+    rings[1].third()
+
+
+def scatter_x(me, mail, at, x_over, x_near):
+    places = (me.x, me.x_up, me.x_down, me.x_far)
+    ring = RingSum(mail, at, places, (me.x_up_dev, me.x_down_dev), x_over, x_near)
     ring.first()
-    yield
-    rings[1].third()
     yield
     ring.second()
     yield
@@ -628,10 +629,20 @@
     return lax.rsqrt(jnp.mean(values * values, axis=-1, keepdims=True) + EPS)
 
 
+def column(row_ref):
+    shape = (16, 16)
+    here = lax.broadcasted_iota(jnp.int32, shape, 0) == lax.broadcasted_iota(jnp.int32, shape, 1)
+    return jnp.sum(jnp.where(here, row_ref[...].astype(WIDE), 0.0), axis=1, keepdims=True)
+
+
+def live_rows(count_ref):
+    return jnp.where(lax.broadcasted_iota(jnp.int32, (ROWS, 1), 0) < count_ref[0, 0], 1.0, 0.0).astype(WIDE)
+
+
 def front_kernel(
-    x_ref, live_ref, cot_ref, wa_own, wm_own, pos_q, pos_k,
-    one_out, wa_out, grad_all, wm, qkv_out, probs_out, att_out, resid, two,
-    one_all, wa, grad_own, qkv, probs, att, ones_t, att_t, part, qx, q2, q1, p2, p1, px, send, recv, local_sem,
+    x_ref, count_ref, owner_ref, cot_ref, attn_ref, mlp_ref, gain_one, gain_two,
+    one_out, wa_out, grad_all, wm, qkv_out, probs_out, att_out, two_all, resid,
+    one_all, wa, grad_own, qkv, probs, att, ones_t, att_t, two, wa_own, wm_own, pos_k, part, qx, q2, q1, p2, p1, px, send, recv, local_sem,
 ):
     me = Place()
     mail = Mail(send, recv)
@@ -643,23 +654,48 @@
         saves.append(copy)
         return copy
 
-    enter(me.peers() + [me.h_dev, me.z_up_dev, me.z_down_dev, me.twin_dev, me.x_up_dev, me.x_down_dev])
+    ready = greet(me.peers() + [me.h_dev, me.z_up_dev, me.z_down_dev, me.twin_dev, me.x_up_dev, me.x_down_dev])
+    live = live_rows(count_ref)
+    x = x_ref[...].astype(WIDE)
+    one_all[me.seq] = (x * row_scale(x) * live).astype(LOW)
+    ready()
+    gather_one = gather_seq(me, mail, one_all.at[me.seq], one_all)
+    step(gather_one)
+    gain = column(gain_one)
+    for slot in range(4):
+        weight = attn_ref[:, slot, :].astype(WIDE)
+        if slot < 3:
+            weight = weight * gain
+        for to in range(8):
+            wa_own[to, :, slot * PART : slot * PART + PART] = weight[:, to * PART : to * PART + PART].astype(LOW)
     swap_a = swap_seq(me, mail, wa_own, wa, 0, PROJ)
     step(swap_a)
+    gain = column(gain_two)
+    units = mlp_ref.shape[2] // 4
+    for slot in range(3):
+        weight = mlp_ref[:, slot, :].astype(WIDE)
+        if slot < 2:
+            weight = weight * gain
+        for to in range(4):
+            piece = weight if to == 0 else pltpu.roll(weight, (4 - to) * units, 1)
+            piece = piece[:, 0:UNITS]
+            piece = jnp.where(lax.broadcasted_iota(jnp.int32, piece.shape, 1) < units, piece, 0.0).astype(LOW)
+            for tile in range(UNITS // 128):
+                first = PAIR + tile * 128 if slot == 2 else (2 * tile + slot) * 128
+                wm_own[to, :, first : first + 128] = piece[:, tile * 128 : tile * 128 + 128]
     swap_m = swap_y(me, mail, wm_own, wm)
     step(swap_m)
     keep_m = save(wm_own.at[me.y], wm.at[me.seq, me.dp])
-    x = x_ref[...].astype(WIDE)
-    one_all[me.seq] = (x * row_scale(x) * live_ref[...]).astype(LOW)
-    gather_one = gather_seq(me, mail, one_all.at[me.seq], one_all)
-    step(gather_one)
+    for block in range(8):
+        columns = lax.broadcasted_iota(jnp.int32, (1, ROWS), 1)
+        pos_k[:, block * ROWS : block * ROWS + ROWS] = columns + owner_ref[0, block] * ROWS
     wa[pl.ds(me.seq, 1), pl.ds(me.dp, 1), :, 0:PROJ] = wa_own[pl.ds(me.seq, 1), :, 0:PROJ][None]
     for k in range(8):
         wa[k, pl.ds(me.dp, 1), :, PROJ:] = wa_own[k, :, PROJ:][None]
     step(swap_a)
     gather_wa = gather_dp(me, mail, wa)
     step(gather_wa)
-    grad_own[...] = (cot_ref[...].astype(WIDE) * live_ref[...]).astype(LOW)
+    grad_own[...] = (cot_ref[...].astype(WIDE) * live).astype(LOW)
     save(grad_own, grad_all.at[me.y])
     step(gather_one)
     step(gather_wa)
@@ -674,9 +710,8 @@
     step(gather_one, 2)
     gather_g = gather_y(me, mail, grad_own, grad_all)
     step(gather_g)
-    run(gather_one, gather_wa)
-    step(gather_wm)
-    save(wa, wa_out)
+    step(gather_one)
+    run(gather_wa)
 
     def project(i, carry):
         rows = one_all[pl.ds(i * 2, 2)].reshape(2 * ROWS, MODEL)
@@ -684,17 +719,22 @@
         qkv[pl.ds(pl.multiple_of(i * 256, 256), 256), :] = dot(rows, weight).astype(LOW)
         return carry
 
+    lax.fori_loop(me.a * 2, me.a * 2 + 2, project, 0)
+    run(gather_one)
+    step(gather_wm)
+    save(wa, wa_out)
+
     def attend(i, carry):
         first = pl.multiple_of(i * ROWS, ROWS)
         rows = pl.ds(first, ROWS)
-        allowed = pos_k[...] <= pos_q[rows, :]
+        allowed = pos_k[...] <= lax.broadcasted_iota(jnp.int32, (ROWS, 1), 0) + owner_ref[0, i] * ROWS
         for head in range(2):
             lo, hi = head * HEAD_DIM, (head + 1) * HEAD_DIM
             q = qkv[rows, lo:hi]
             k = qkv[:, PART + lo : PART + hi]
             v = qkv[:, 2 * PART + lo : 2 * PART + hi]
-            scores = dot(q, k, ((1,), (1,))) * (1.0 / math.sqrt(HEAD_DIM)) - math.log(8 * ROWS)
-            p = jnp.where(allowed, 1.0 / (1.0 + jnp.exp(-scores)), 0.0).astype(LOW)
+            odds = jnp.exp2(math.log2(8 * ROWS) - dot(q, k, ((1,), (1,))) * (math.log2(math.e) / math.sqrt(HEAD_DIM)))
+            p = jnp.where(allowed, 1.0 / (1.0 + odds), 0.0).astype(LOW)
             probs[head, rows, :] = p
             att[rows, lo:hi] = dot(p, v).astype(LOW)
         return carry
@@ -710,14 +750,14 @@
 
         lax.fori_loop(0, 8, piece, 0)
 
-    lax.fori_loop(0, 4, project, 0)
+    lax.fori_loop(me.b * 2, me.b * 2 + 2, project, 0)
     step(gather_g)
     save(qkv, qkv_out)
 
     def write(lo, hi, rows):
         total = x_ref[lo:hi].astype(WIDE) + rows
         resid[lo:hi] = total
-        two[lo:hi] = (total * row_scale(total) * live_ref[lo:hi]).astype(LOW)
+        two[lo:hi] = (total * row_scale(total) * live[lo:hi]).astype(LOW)
 
     scatter = scatter_seq(me, mail, part, (qx, q2, q1, p2, p1, px), write)
     lax.fori_loop(me.b * 4, me.b * 4 + 4, attend, 0)
@@ -729,6 +769,9 @@
     step(scatter)
     save(probs, probs_out)
     finish(scatter, gather_wm)
+    gather_two = gather_y(me, mail, two, two_all)
+    step(gather_two)
+    save(two, two_all.at[me.y])
     step(gather_wm)
 
     def turn(s, carry):
@@ -741,43 +784,46 @@
     for i in range(4):
         lax.fori_loop(2 * i, 2 * i + 2, turn, 0)
         step(gather_wm)
+        if i == 1:
+            step(gather_two)
     save(ones_t, one_out)
-    run(gather_wm, gather_g)
+    run(gather_wm, gather_g, gather_two)
     for copy in saves:
         if copy is not keep_m:
             copy.wait()
     mail.finish()
 
 
-def front(x, live, cot, wa_own, wm_own, pos):
+def front(x, counts, owners, cot, attn_weight, mlp_weight, gain_one, gain_two):
     vmem, anywhere = pl.BlockSpec(memory_space=pltpu.VMEM), pl.BlockSpec(memory_space=pl.ANY)
     shape = jax.ShapeDtypeStruct
-    count = 7 + 18 + 19 + 3 + 36 + 4 + 23
+    count = 7 + 18 + 19 + 3 + 36 + 4 + 23 + 4
     return pl.pallas_call(
         front_kernel,
         out_shape=(
             shape((8, 256, 1024), LOW), shape((8, 16, 16, 1024), LOW), shape((4, ROWS, MODEL), LOW),
             shape((8, 16, 16, SLAB), LOW), shape((1024, PROJ), LOW), shape((2, 1024, 1024), LOW),
-            shape((PART, 1024), LOW), shape((ROWS, MODEL), WIDE), shape((ROWS, MODEL), LOW),
+            shape((PART, 1024), LOW), shape((4, ROWS, MODEL), LOW), shape((ROWS, MODEL), WIDE),
         ),
-        in_specs=[vmem] * 4 + [anywhere] + [vmem] * 2,
-        out_specs=(anywhere,) * 7 + (vmem, vmem),
+        in_specs=[vmem] + [pl.BlockSpec(memory_space=pltpu.SMEM)] * 2 + [vmem] * 5,
+        out_specs=(anywhere,) * 8 + (vmem,),
         scratch_shapes=[
             pltpu.VMEM((8, ROWS, MODEL), LOW), pltpu.VMEM((8, 16, 16, 1024), LOW), pltpu.VMEM((ROWS, MODEL), LOW),
             pltpu.VMEM((1024, PROJ), LOW), pltpu.VMEM((2, 1024, 1024), LOW), pltpu.VMEM((1024, PART), LOW),
-            pltpu.VMEM((8, 256, 1024), LOW), pltpu.VMEM((PART, 1024), LOW),
+            pltpu.VMEM((8, 256, 1024), LOW), pltpu.VMEM((PART, 1024), LOW), pltpu.VMEM((ROWS, MODEL), LOW),
+            pltpu.VMEM((8, 16, 1024), LOW), pltpu.VMEM((4, 16, SLAB), LOW), pltpu.VMEM((1, 1024), jnp.int32),
             pltpu.VMEM((8, ROWS, MODEL), LOW),
         ]
         + scatter_bufs()
-        + [pltpu.SemaphoreType.DMA((count,)), pltpu.SemaphoreType.DMA((count,)), pltpu.SemaphoreType.DMA((8,))],
+        + [pltpu.SemaphoreType.DMA((count,)), pltpu.SemaphoreType.DMA((count,)), pltpu.SemaphoreType.DMA((9,))],
         compiler_params=pltpu.CompilerParams(collective_id=1, has_side_effects=True, vmem_limit_bytes=56 * 2**20),
         name="front",
-    )(x, live, cot, wa_own, wm_own, pos[:, None], pos[None, :])
+    )(x, counts, owners, cot, attn_weight, mlp_weight, gain_one, gain_two)
 def mlp_kernel(
-    two_ref, resid, cot_ref, live_ref, grad_all, wm_all,
-    acc_out, branch_out, grad_resid, grad_branch,
-    wm, grads, twos, hidden, pair, grads_t, part, branch, p2, p1,
-    stage, acc, send, recv, local_sem,
+    resid, cot_ref, count_ref, two_all, grad_all, wm_all,
+    acc_out, branch_out, branch_grads, grad_resid, down_out,
+    wm, grads, twos, hidden, pair, part, branch, p2, p1, grad_branch,
+    stage_d, acc_d, z_over, z_near, stage, acc, send, recv, local_sem, wm_sem,
 ):
     me = Place()
     mail = Mail(send, recv)
@@ -789,155 +835,169 @@
         saves.append(copy)
         return copy
 
-    load_w = save(wm_all, wm)
-    load_g = save(grad_all, grads)
-    enter([me.up_dev, me.down_dev, me.twin_dev])
-    twos[me.y] = two_ref[...]
-    gather = gather_y(me, mail, twos.at[me.y], twos)
-    step(gather)
-    load_w.wait()
-    load_g.wait()
-
-    def rows_of(ref, blocks):
-        return jnp.concatenate([ref[k] for k in blocks], axis=0)
-
-    def put(ref, blocks, columns, values):
-        for i, k in enumerate(blocks):
-            ref[k, :, columns] = values[i * ROWS : (i + 1) * ROWS].astype(LOW)
-
-    def hidden_tile(blocks, j, wide):
-        start = j * 128
-        if not isinstance(j, int):
-            start = pl.multiple_of(start, 128)
+    live = live_rows(count_ref)
+    loads = [save(two_all, twos), save(grad_all, grads)]
+
+    def weights(j, wide):
+        for first, each, sem in ((0, 256, 0), (PAIR, 128, 6)):
+            columns = pl.ds(pl.multiple_of(first + j * each, 128), wide * each)
+            yield pltpu.make_async_copy(
+                wm_all.at[:, :, :, columns], wm.at[:, :, :, columns], wm_sem.at[sem + j // 2]
+            )
+
+    for j in range(0, UNITS // 128, 2):
+        for copy in weights(j, min(2, UNITS // 128 - j)):
+            copy.start()
+    ready = greet([me.x_dev, me.up_dev, me.down_dev, me.z_up_dev, me.z_down_dev, me.twin_dev])
+    for load in loads:
+        load.wait()
+
+    def tall(ref, columns=slice(None)):
+        values = ref[:, :, columns]
+        return values.reshape(4 * ROWS, values.shape[2])
+
+    def put(ref, columns, values):
+        ref[:, :, columns] = values.reshape(4, ROWS, values.shape[1]).astype(LOW)
+
+    def ahead(j, wide):
+        for copy in weights(j, wide):
+            copy.wait()
+        start = pl.multiple_of(j * 128, 128)
         width = wide * 128
         weight = wm[:, :, :, pl.ds(2 * start, 2 * width)].reshape(MODEL, 2 * width)
-        gate_up = dot(rows_of(twos, blocks), weight)
+        gate_up = dot(tall(twos), weight)
         down = wm[:, :, :, pl.ds(PAIR + start, width)].reshape(MODEL, width)
-        grad_hidden = dot(rows_of(grads, blocks), down)
+        grad_hidden = dot(tall(grads), down)
         low, pairs = [], []
         for i in range(wide):
             gate = gate_up[:, i * 256 : i * 256 + 128]
             up = gate_up[:, i * 256 + 128 : i * 256 + 256]
-            back = grad_hidden[:, i * 128 : i * 128 + 128]
+            grad = grad_hidden[:, i * 128 : i * 128 + 128]
             squashed = 1.0 / (1.0 + jnp.exp(-gate))
             active = gate * squashed
             low.append(active * up)
-            pairs.append(back * up * (squashed * (1.0 + gate * (1.0 - squashed))))
-            pairs.append(back * active)
-        put(hidden, blocks, pl.ds(start, width), jnp.concatenate(low, axis=1))
-        put(pair, blocks, pl.ds(2 * start, 2 * width), jnp.concatenate(pairs, axis=1))
-
-    def ahead(blocks):
-        def tile(j, carry):
-            hidden_tile(blocks, 2 * j, 2)
-            return carry
-
-        lax.fori_loop(0, 5, tile, 0)
-        hidden_tile(blocks, 10, 1)
-
-    def back(blocks):
-        def tile(s, carry):
-            columns = pl.ds(pl.multiple_of(s * 256, 256), 256)
-            weight = wm[s, :, :, 0:PAIR].reshape(256, PAIR)
-            put(part, blocks, columns, dot(rows_of(pair, blocks), weight, ((1,), (1,))))
-            return carry
-
-        lax.fori_loop(0, 8, tile, 0)
-
-    def down_back(blocks):
-        def tile(s, carry):
-            columns = pl.ds(pl.multiple_of(s * 256, 256), 256)
-            weight = wm[s, :, :, PAIR:].reshape(256, UNITS)
-            put(branch, blocks, columns, dot(rows_of(hidden, blocks), weight, ((1,), (1,))))
-            return carry
-
-        lax.fori_loop(0, 8, tile, 0)
+            pairs.append(grad * up * (squashed * (1.0 + gate * (1.0 - squashed))))
+            pairs.append(grad * active)
+        put(hidden, pl.ds(start, width), jnp.concatenate(low, axis=1))
+        put(pair, pl.ds(2 * start, 2 * width), jnp.concatenate(pairs, axis=1))
+
+    def ahead_tile(j, carry):
+        ahead(2 * j, 2)
+        return carry
+
+    def back(s, carry):
+        columns = pl.ds(pl.multiple_of(s * 256, 256), 256)
+        weight = wm[s, :, :, 0:PAIR].reshape(256, PAIR)
+        put(part, columns, dot(tall(pair), weight, ((1,), (1,))))
+        return carry
+
+    def down_back(s, carry):
+        columns = pl.ds(pl.multiple_of(s * 256, 256), 256)
+        weight = wm[s, :, :, PAIR:].reshape(256, UNITS)
+        put(branch, columns, dot(tall(hidden), weight, ((1,), (1,))))
+        return carry
 
     def write(lo, hi, rows):
         x = resid[lo:hi]
         scale = row_scale(x)
         hat = x * scale
         inner = jnp.mean(rows * hat, axis=-1, keepdims=True)
-        total = cot_ref[lo:hi].astype(WIDE) * live_ref[lo:hi] + scale * (rows - hat * inner)
+        total = cot_ref[lo:hi].astype(WIDE) * live[lo:hi] + scale * (rows - hat * inner)
         grad_resid[lo:hi] = total
         grad_branch[lo:hi] = total.astype(LOW)
 
+    order = [me.a * 4 + i for i in range(4)] + [me.b * 4 + i for i in range(4)]
+
+    def columns_t(ref, s):
+        return ref[:, :, pl.ds(pl.multiple_of(s * 256, 256), 256)].reshape(4 * ROWS, 256).T
+
+    def down_product(s, out):
+        terms = dot(columns_t(grads, s), hidden[...].reshape(4 * ROWS, UNITS))
+        out[...] = terms.reshape(8, 2, 16, UNITS).astype(LOW)
+
+    def pair_product(s, out):
+        terms = dot(columns_t(twos, s), pair[...].reshape(4 * ROWS, PAIR))
+        out[...] = terms.reshape(8, 2, 16, PAIR).astype(LOW)
+
+    def kept(i):
+        save(acc.at[order[i]], acc_out.at[order[i]])
+
     scatter = scatter_y(me, mail, part, p2, p1, write)
-    ahead([me.y])
-
-    def turn(s, carry):
-        columns = pl.ds(pl.multiple_of(s * 256, 256), 256)
-        grads_t[s] = grads[:, :, columns].reshape(4 * ROWS, 256).T
-        return carry
-
-    lax.fori_loop(0, 8, turn, 0)
-    step(gather)
-    ahead([me.up, me.down])
-    back([me.up, me.down])
+    twin_d = twin_sum(me, mail, stage_d, acc_d, order, down_product)
+    twin = twin_sum(me, mail, stage, acc, order, pair_product, kept)
+    sums = scatter_z(me, mail, acc_d, z_over, z_near)
+    gather = gather_seq(me, mail, grad_branch, branch_grads)
+    lax.fori_loop(0, 5, ahead_tile, 0)
+    ahead(10, 1)
+    lax.fori_loop(0, 4, back, 0)
+    ready()
+    step(scatter)
+    lax.fori_loop(4, 8, back, 0)
+    step(scatter)
+    run(twin_d)
+    step(sums, 2)
+    step(scatter)
+    step(twin, 3)
+    step(sums, 2)
+    step(twin, 3)
     step(scatter)
     step(gather)
-    ahead([me.far])
-    back([me.far])
-    step(scatter)
-    back([me.y])
-    down_back([me.y, me.up, me.down, me.far])
-    step(scatter)
-
+    keep = save(grad_branch, branch_grads.at[me.seq])
+    step(sums, 2)
+    run(twin)
+    step(gather)
+    for i in range(5):
+        if i < 4:
+            lax.fori_loop(2 * i, 2 * i + 2, down_back, 0)
+        step(sums)
+        step(gather)
     save(branch, branch_out)
-    order = [me.a * 4 + i for i in range(4)] + [me.b * 4 + i for i in range(4)]
-
-    def product(s, out):
-        columns = pl.ds(pl.multiple_of(s * 256, 256), 256)
-        rows = twos[:, :, columns].reshape(4 * ROWS, 256).T
-        terms = dot(rows, pair[...].reshape(4 * ROWS, PAIR))
-        out[:, :, :, 0:PAIR] = terms.reshape(8, 2, 16, PAIR).astype(LOW)
-        terms = dot(grads_t[s], hidden[...].reshape(4 * ROWS, UNITS))
-        out[:, :, :, PAIR:] = terms.reshape(8, 2, 16, UNITS).astype(LOW)
-
-    def kept(i):
-        save(acc.at[order[i]], acc_out.at[order[i]])
-
-    twin = twin_sum(me, mail, stage, acc, order, product, kept)
-    step(twin, 3)
-    step(scatter)
-    run(twin)
-    run(scatter)
+    run(sums)
+    for x in range(4):
+        save(acc_d.at[x % 2 * 4 : x % 2 * 4 + 4, me.z * 2 + x // 2], down_out.at[x])
+    run(gather)
     for copy in saves[2:]:
         copy.wait()
     mail.finish()
 
 
-def mlp(two, resid, cot, live, grad_all, wm):
+def mlp(resid, cot, counts, twos, grads, wm):
     vmem, anywhere = pl.BlockSpec(memory_space=pltpu.VMEM), pl.BlockSpec(memory_space=pl.ANY)
     shape = jax.ShapeDtypeStruct
     blocks = (4, ROWS, MODEL)
+    count = 6 + 8 + 8 + 24 + 18
     return pl.pallas_call(
         mlp_kernel,
         out_shape=(
-            shape((8, 8, 16, SLAB), LOW), shape(blocks, LOW), shape((ROWS, MODEL), WIDE), shape((ROWS, MODEL), LOW),
+            shape((8, 8, 16, PAIR), LOW), shape(blocks, LOW), shape((8, ROWS, MODEL), LOW), shape((ROWS, MODEL), WIDE),
+            shape((4, 4, 16, UNITS), LOW),
         ),
-        in_specs=[vmem] * 4 + [anywhere] * 2,
-        out_specs=(anywhere,) * 2 + (vmem,) * 2,
+        in_specs=[vmem] * 2 + [pl.BlockSpec(memory_space=pltpu.SMEM)] + [anywhere] * 3,
+        out_specs=(anywhere,) * 3 + (vmem, anywhere),
         scratch_shapes=[
             pltpu.VMEM((8, 16, 16, SLAB), LOW), pltpu.VMEM(blocks, LOW), pltpu.VMEM(blocks, LOW),
-            pltpu.VMEM((4, ROWS, UNITS), LOW), pltpu.VMEM((4, ROWS, PAIR), LOW), pltpu.VMEM((8, 256, 4 * ROWS), LOW), pltpu.VMEM(blocks, LOW),
-            pltpu.VMEM(blocks, LOW), pltpu.VMEM((2, ROWS // 2, MODEL), LOW), pltpu.VMEM((2, ROWS, MODEL), LOW),
-            pltpu.VMEM((2, 8, 2, 16, SLAB), LOW), pltpu.VMEM((8, 8, 16, SLAB), LOW),
-            pltpu.SemaphoreType.DMA((24,)), pltpu.SemaphoreType.DMA((24,)), pltpu.SemaphoreType.DMA((11,)),
+            pltpu.VMEM((4, ROWS, UNITS), LOW), pltpu.VMEM((4, ROWS, PAIR), LOW), pltpu.VMEM(blocks, LOW),
+            pltpu.VMEM(blocks, LOW), pltpu.VMEM((2, ROWS, MID), LOW), pltpu.VMEM((2, ROWS, MODEL), LOW),
+            pltpu.VMEM((ROWS, MODEL), LOW),
+            pltpu.VMEM((2, 8, 2, 16, UNITS), LOW), pltpu.VMEM((8, 8, 16, UNITS), LOW),
+            pltpu.VMEM((4, 2, 2, 16, UNITS), LOW), pltpu.VMEM((4, 2, 4, 16, UNITS), LOW),
+            pltpu.VMEM((2, 8, 2, 16, PAIR), LOW), pltpu.VMEM((8, 8, 16, PAIR), LOW),
+            pltpu.SemaphoreType.DMA((count,)), pltpu.SemaphoreType.DMA((count,)), pltpu.SemaphoreType.DMA((16,)), pltpu.SemaphoreType.DMA((12,)),
         ],
         compiler_params=pltpu.CompilerParams(collective_id=2, has_side_effects=True, vmem_limit_bytes=62 * 2**20),
         name="mlp",
-    )(two, resid, cot, live, grad_all, wm)
+    )(resid, cot, counts, twos, grads, wm)
 def back_kernel(
-    branch_grad, grad_resid, x_ref, live_ref, resid, branch_all, acc_all, one_all, wa_all, qkv_all, probs_all, att_all,
-    layer_out, input_grad, slab_own, in_own, out_own,
-    acc, z_over, z_near, x_over, x_near, grads, branch, b2, b1, part, qx, q2, q1, p2, p1, px,
+    grad_resid, x_ref, count_ref, resid, attn_ref, mlp_ref, gain_one, gain_two, down_all, branch_grads, branch_all, acc_all, one_all, wa_all, qkv_all, probs_all, att_all,
+    layer_out, input_grad, attn_grad, mlp_grad, gain_grads,
+    down, dx_over, dx_near, down_own, pair_own, in_own, acc, z_over, z_near, x_over, x_near, grads, branch, b2, b1, part, qx, q2, q1, p2, p1, px,
     wa, acc_a, az_over, az_near, h_near, ones_t, qkv, probs, att_t, grad_att, grad_proj, grad_k, grad_v, stage_a,
     send, recv, local_sem,
 ):
     me = Place()
     mail = Mail(send, recv)
     loads = []
+    live = live_rows(count_ref)
 
     def load(src, dst):
         copy = pltpu.make_async_copy(src, dst, local_sem.at[len(loads)])
@@ -946,12 +1006,11 @@
         return copy
 
     load_acc = [load(acc_all.at[pl.ds(col * 4, 4)], acc.at[pl.ds(col * 4, 4)]) for col in (me.a, me.b)]
-    enter(me.peers() + [me.h_dev, me.z_up_dev, me.z_down_dev, me.x_up_dev, me.x_down_dev, me.twin_dev])
-    grads[me.seq] = branch_grad[...]
-    gather = gather_seq(me, mail, grads.at[me.seq], grads)
-    step(gather)
+    load_down = load(down_all, down)
+    load_branch = load(branch_all, branch)
+    ready = greet(me.peers() + [me.h_dev, me.z_up_dev, me.z_down_dev, me.x_up_dev, me.x_down_dev, me.twin_dev])
+    load_grads = load(branch_grads, grads)
     load_wa = load(wa_all, wa)
-    load_branch = load(branch_all, branch)
     waits = [load(*both) for both in ((qkv_all, qkv), (att_all, att_t), (one_all, ones_t))]
     fetch = [load(probs_all.at[:, 256 * i : 256 * i + 256], probs.at[i]) for i in range(2)]
     order = [me.a * 4 + i for i in range(4)] + [me.b * 4 + i for i in range(4)]
@@ -959,31 +1018,38 @@
     def columns_of(s, width=256):
         return pl.ds(pl.multiple_of(s * width, width), width)
 
-    def slab_sums():
-        yield from scatter_xz(me, mail, acc, z_over, z_near, x_over, x_near)
-        yield from send_y(me, mail, acc.at[pl.ds(me.a * 4, 4), me.z * 2 + me.h], slab_own)
-
-    sums = slab_sums()
+    def down_sums():
+        yield from scatter_x(me, mail, lambda x: down.at[x], dx_over, dx_near)
+        yield from send_y(me, mail, down.at[me.x], down_own)
+
+    def pair_sums():
+        yield from scatter_z(me, mail, acc, z_over, z_near)
+        yield from scatter_x(me, mail, lambda x: acc.at[pl.ds(x % 2 * 4, 4), me.z * 2 + x // 2], x_over, x_near)
+        yield from send_y(me, mail, acc.at[pl.ds(me.a * 4, 4), me.z * 2 + me.h], pair_own)
+
+    downs = down_sums()
+    sums = pair_sums()
 
     load_acc[0].wait()
+    ready()
     step(sums)
     load_acc[1].wait()
     step(sums)
-    step(gather, 4)
-
+    load_down.wait()
+    step(downs)
     def write_out(lo, hi, rows):
-        layer_out[lo:hi] = (live_ref[lo:hi] * (resid[lo:hi] + rows)).astype(LOW)
+        layer_out[lo:hi] = (live[lo:hi] * (resid[lo:hi] + rows)).astype(LOW)
 
     out_sum = scatter_y(me, mail, branch, b2, b1, write_out)
     load_branch.wait()
     step(out_sum, 2)
-    run(gather)
+    load_grads.wait()
     def write_grad(lo, hi, rows):
         x = x_ref[lo:hi].astype(WIDE)
         scale = row_scale(x)
         hat = x * scale
         inner = jnp.mean(rows * hat, axis=-1, keepdims=True)
-        input_grad[lo:hi] = grad_resid[lo:hi] + live_ref[lo:hi] * scale * (rows - hat * inner)
+        input_grad[lo:hi] = grad_resid[lo:hi] + live[lo:hi] * scale * (rows - hat * inner)
 
     grad_sum = scatter_seq(me, mail, part, (qx, q2, q1, p2, p1, px), write_grad)
 
@@ -1021,11 +1087,14 @@
     for i in range(4):
         fetch[i].wait()
         attend_back(i)
-        if i == 1:
-            step(out_sum)
         if i < 2:
             fetch.append(load(probs_all.at[:, 256 * i + 512 : 256 * i + 768], probs.at[i]))
-        step(sums)
+        if i == 1:
+            step(sums)
+        if i == 2:
+            step(downs)
+        if i == 3:
+            step(out_sum)
     grad_proj[:, PART : 2 * PART] = (grad_k[...] * head_scale).astype(LOW)
     grad_proj[:, 2 * PART :] = grad_v[...].astype(LOW)
 
@@ -1049,39 +1118,79 @@
     twin = twin_sum(me, mail, stage_a, acc_a, order, product)
     norm_terms(me.b)
     step(grad_sum)
-    step(twin, 9)
     norm_terms(me.a)
     step(grad_sum)
+    step(twin, 3)
+    step(grad_sum)
+    step(downs)
+    step(twin, 3)
+    step(grad_sum)
+    step(sums)
+    step(twin, 3)
 
     def proj_sums():
         yield from scatter_hz(me, mail, acc_a, az_over, az_near, h_near)
         own = acc_a.at[:, me.z * 2 + me.h]
-        out_own[...] = own[:, :, PROJ:]
         yield from send_seq(me, mail, own, in_own, 0, PROJ)
 
     rest = proj_sums()
     step(rest)
-    finish(grad_sum, sums)
-    run(rest, sums, out_sum)
+    finish(grad_sum, sums, rest)
+    own = acc_a.at[:, me.z * 2 + me.h]
+    gain = column(gain_one)
+    sum_one = jnp.zeros((16, 1), WIDE)
+    run(sums, out_sum, downs)
+    units = mlp_ref.shape[2] // 4
+    spare = jnp.zeros((16, mlp_ref.shape[2] - UNITS), WIDE)
+    gain_mlp = column(gain_two)
+    sum_two = jnp.zeros((16, 1), WIDE)
+    for slot in range(3):
+        whole = None
+        for src in range(4):
+            if slot == 2:
+                piece = down_own[src].astype(WIDE)
+            else:
+                firsts = [(2 * tile + slot) * 128 for tile in range(UNITS // 128)]
+                piece = jnp.concatenate([pair_own[src, :, f : f + 128].astype(WIDE) for f in firsts], axis=1)
+            piece = jnp.concatenate([piece, spare], axis=1)
+            whole = piece if src == 0 else whole + pltpu.roll(piece, src * units, 1)
+        if slot < 2:
+            sum_two = sum_two + jnp.sum(whole * mlp_ref[:, slot, :].astype(WIDE), axis=1, keepdims=True)
+            whole = whole * gain_mlp
+        mlp_grad[:, slot, :] = whole
+    run(rest)
+    for slot in range(4):
+        if slot < 3:
+            pieces = [in_own[src, :, slot * PART : slot * PART + PART] for src in range(8)]
+        else:
+            pieces = [own[k, :, PROJ:] for k in range(8)]
+        whole = jnp.concatenate([piece.astype(WIDE) for piece in pieces], axis=1)
+        if slot < 3:
+            sum_one = sum_one + jnp.sum(whole * attn_ref[:, slot, :].astype(WIDE), axis=1, keepdims=True)
+            whole = whole * gain
+        attn_grad[:, slot, :] = whole
+    gain_grads[:, 0:128] = jnp.broadcast_to(sum_one, (16, 128))
+    gain_grads[:, 128:256] = jnp.broadcast_to(sum_two, (16, 128))
     mail.finish()
 
 
-def back(branch_grad, grad_resid, x, live, resid, branch, acc, ones, wa, qkv, probs, att):
+def back(grad_resid, x, counts, resid, attn_weight, mlp_weight, gain_one, gain_two, down, grads, branch, acc, ones, wa, qkv, probs, att):
     vmem, anywhere = pl.BlockSpec(memory_space=pltpu.VMEM), pl.BlockSpec(memory_space=pl.ANY)
     shape = jax.ShapeDtypeStruct
-    count = 18 + 30 + 3 + 6 + 23 + 8 + 13 + 7
+    count = 9 + 30 + 3 + 6 + 23 + 8 + 13 + 7
     return pl.pallas_call(
         back_kernel,
         out_shape=(
-            shape((ROWS, MODEL), LOW), shape((ROWS, MODEL), WIDE), shape((4, 16, SLAB), LOW),
-            shape((8, 16, PROJ), LOW), shape((8, 16, PART), LOW),
+            shape((ROWS, MODEL), LOW), shape((ROWS, MODEL), WIDE), shape(attn_weight.shape, WIDE),
+            shape(mlp_weight.shape, WIDE), shape((16, 256), WIDE),
         ),
-        in_specs=[vmem] * 5 + [anywhere] * 7,
+        in_specs=[vmem] * 2 + [pl.BlockSpec(memory_space=pltpu.SMEM)] + [vmem] * 5 + [anywhere] * 9,
         out_specs=(vmem,) * 5,
         scratch_shapes=[
-            pltpu.VMEM((8, 8, 16, SLAB), LOW), pltpu.VMEM((4, 2, 2, 16, SLAB), LOW), pltpu.VMEM((4, 2, 4, 16, SLAB), LOW),
-            pltpu.VMEM((2, 2, 16, SLAB), LOW), pltpu.VMEM((2, 4, 16, SLAB), LOW), pltpu.VMEM((8, ROWS, MODEL), LOW),
-            pltpu.VMEM((4, ROWS, MODEL), LOW), pltpu.VMEM((2, ROWS // 2, MODEL), LOW), pltpu.VMEM((2, ROWS, MODEL), LOW),
+            pltpu.VMEM((4, 4, 16, UNITS), LOW), pltpu.VMEM((2, 2, 16, UNITS), LOW), pltpu.VMEM((2, 4, 16, UNITS), LOW),
+            pltpu.VMEM((4, 16, UNITS), LOW), pltpu.VMEM((4, 16, PAIR), LOW), pltpu.VMEM((8, 16, PROJ), LOW), pltpu.VMEM((8, 8, 16, PAIR), LOW), pltpu.VMEM((4, 2, 2, 16, PAIR), LOW), pltpu.VMEM((4, 2, 4, 16, PAIR), LOW),
+            pltpu.VMEM((2, 2, 16, PAIR), LOW), pltpu.VMEM((2, 4, 16, PAIR), LOW), pltpu.VMEM((8, ROWS, MODEL), LOW),
+            pltpu.VMEM((4, ROWS, MODEL), LOW), pltpu.VMEM((2, ROWS, MID), LOW), pltpu.VMEM((2, ROWS, MODEL), LOW),
             pltpu.VMEM((8, ROWS, MODEL), LOW),
         ]
         + scatter_bufs()
@@ -1092,55 +1201,25 @@
             pltpu.VMEM((1024, PROJ), LOW), pltpu.VMEM((2, 2, 256, 1024), LOW), pltpu.VMEM((PART, 1024), LOW),
             pltpu.VMEM((1024, PART), LOW), pltpu.VMEM((1024, PROJ), LOW),
             pltpu.VMEM((1024, PART), WIDE), pltpu.VMEM((1024, PART), WIDE), pltpu.VMEM((2, 8, 2, 16, 1024), LOW),
-            pltpu.SemaphoreType.DMA((count,)), pltpu.SemaphoreType.DMA((count,)), pltpu.SemaphoreType.DMA((12,)),
+            pltpu.SemaphoreType.DMA((count,)), pltpu.SemaphoreType.DMA((count,)), pltpu.SemaphoreType.DMA((14,)),
         ],
         compiler_params=pltpu.CompilerParams(collective_id=3, has_side_effects=True, vmem_limit_bytes=62 * 2**20),
         name="back",
-    )(branch_grad, grad_resid, x, live, resid, branch, acc, ones, wa, qkv, probs, att)
-def weights_out(attn_weight, mlp_weight, gain_one, gain_two):
-    proj = (attn_weight[:, :3].astype(WIDE) * gain_one).astype(LOW).reshape(16, 3, 8, PART)
-    proj = proj.transpose(2, 0, 1, 3).reshape(8, 16, PROJ)
-    out = attn_weight[:, 3].reshape(16, 8, PART).transpose(1, 0, 2)
-    units = mlp_weight.shape[2] // 4
-    spare = UNITS - units
-    pair = (mlp_weight[:, :2].astype(WIDE) * gain_two).astype(LOW).reshape(16, 2, 4, units)
-    pair = jnp.pad(pair, ((0, 0), (0, 0), (0, 0), (0, spare))).reshape(16, 2, 4, UNITS // 128, 128)
-    pair = pair.transpose(2, 0, 3, 1, 4).reshape(4, 16, PAIR)
-    down = jnp.pad(mlp_weight[:, 2].reshape(16, 4, units), ((0, 0), (0, 0), (0, spare))).transpose(1, 0, 2)
-    return jnp.concatenate([proj, out], axis=2), jnp.concatenate([pair, down], axis=2)
-
-
-def weights_back(slab, proj, out, units):
-    pair, down = slab[..., :PAIR], slab[..., PAIR:]
-    proj = proj.reshape(8, 16, 3, PART).transpose(1, 2, 0, 3).reshape(16, 3, MODEL).astype(WIDE)
-    out = out.transpose(1, 0, 2).reshape(16, MODEL).astype(WIDE)
-    pair = pair.reshape(4, 16, UNITS // 128, 2, 128).transpose(1, 3, 0, 2, 4).reshape(16, 2, 4, UNITS)
-    pair = pair[..., : units // 4].reshape(16, 2, units).astype(WIDE)
-    down = down[..., : units // 4].transpose(1, 0, 2).reshape(16, units).astype(WIDE)
-    return proj, out, pair, down
-
-
+    )(grad_resid, x, counts, resid, attn_weight, mlp_weight, gain_one, gain_two, down, grads, branch, acc, ones, wa, qkv, probs, att)
 def local(
     tokens, valid_counts, block_owner, norm1_gain, attn_weight, norm2_gain, mlp_weight, cotangent
 ):
-    row_index = jnp.arange(ROWS, dtype=jnp.int32)
-    live = (row_index < valid_counts[0, 0]).astype(WIDE)[:, None]
-    pos = (block_owner[0][:, None] * ROWS + row_index[None]).reshape(-1)
     x, cot = tokens[0], cotangent[0]
-    gain_one = norm1_gain.astype(WIDE)[:, None, None]
-    gain_two = norm2_gain.astype(WIDE)[:, None, None]
-    wa_own, wm_own = weights_out(attn_weight, mlp_weight, gain_one, gain_two)
-    ones, wa, grads, wm, qkv, probs, att, resid, two = front(x, live, cot, wa_own, wm_own, pos)
-    acc, branch, grad_resid, branch_grad = mlp(two, resid, cot, live, grads, wm)
-    layer_out, input_grad, slab_own, in_own, out_own = back(
-        branch_grad, grad_resid, x, live, resid, branch, acc, ones, wa, qkv, probs, att
+    gain_one, gain_two = norm1_gain[None], norm2_gain[None]
+    ones, wa, grads, wm, qkv, probs, att, twos, resid = front(
+        x, valid_counts, block_owner, cot, attn_weight, mlp_weight, gain_one, gain_two
     )
-    in_sum, out_sum, pair_sum, down_sum = weights_back(slab_own, in_own, out_own, mlp_weight.shape[2])
-    attn_grad = jnp.concatenate([in_sum * gain_one, out_sum[:, None]], axis=1)
-    mlp_grad = jnp.concatenate([pair_sum * gain_two, down_sum[:, None]], axis=1)
-    gain_one_grad = jnp.sum(in_sum * attn_weight[:, :3].astype(WIDE), axis=(1, 2))
-    gain_two_grad = jnp.sum(pair_sum * mlp_weight[:, :2].astype(WIDE), axis=(1, 2))
-    return (layer_out[None], input_grad[None], gain_one_grad, attn_grad, gain_two_grad, mlp_grad)
+    acc, branch, branch_grads, grad_resid, down = mlp(resid, cot, valid_counts, twos, grads, wm)
+    layer_out, input_grad, attn_grad, mlp_grad, gain_grads = back(
+        grad_resid, x, valid_counts, resid, attn_weight, mlp_weight, gain_one, gain_two, down,
+        branch_grads, branch, acc, ones, wa, qkv, probs, att,
+    )
+    return (layer_out[None], input_grad[None], gain_grads[:, 0], attn_grad, gain_grads[:, 128], mlp_grad)
 
 
 def solution(mesh):

time: 343 us -> 322 us (0.939)
  Pallas kernels: 315 us -> 306 us
  other arithmetic: 8.99 us -> 0 us
    pallas_call x1, Pallas kernels: 126 us -> 99.8 us  [back(): pl.pallas_call(back_kernel, out_shape=(shape((ROWS, MODEL), LOW), shape((...]
    pallas_call x1, Pallas kernels: 67.8 us -> 86.5 us  [mlp(): pl.pallas_call(mlp_kernel, out_shape=(shape((8, 8, 16, PAIR), LOW), shape...]
    unnamed x16 -> x9, local copies, waits for them, and re-layouts: 2.96 us -> 8.21 us
    convert_element_type x8 -> x0, other arithmetic: 4.09 us -> none  [the longest x1 0.95 us: weights_back(): down[..., :units // 4].transpose(1, 0, 2).reshape(16, units).astype(WIDE)]
where the time goes in v5:
time: 322 us; the launch traced here: 318 us
  Pallas kernels  306 us (95%)
  local copies, waits for them, and re-layouts  9.67 us (3%)
    pallas_call x1, Pallas kernels, front(): pl.pallas_call(front_kernel, out_shape=(shape((8, 256, 1024), LOW), shape...  120 us
    pallas_call x1, Pallas kernels, back(): pl.pallas_call(back_kernel, out_shape=(shape((ROWS, MODEL), LOW), shape((...  99.8 us
    pallas_call x1, Pallas kernels, mlp(): pl.pallas_call(mlp_kernel, out_shape=(shape((8, 8, 16, PAIR), LOW), shape...  86.5 us
    unnamed x9, local copies, waits for them, and re-layouts  8.21 us

profile of v5, /device:TPU:0, one launch (start us, length us, event | category | flops | bytes accessed | tf_op | source)
XLA Modules:
  0.0 317.8 jit_solution(18166738103661387881)
XLA Ops:
  1.3 2.2 copy.17.mlp_ref
  3.4 120.0 %front.1 = (bf16[8,256,1024]{2,1,0:T(8,128)(2,1)}, bf16[8,16,16,1024]{3,2,1,0:T(8,128)(2,1)}, bf16[4,128,2048]{2,1,0:T(8,128)(2,1)}, bf16[8,16,16,4224]{3,2,1,0:...) custom-call(bf16[128,2048]{1,0:T(8,128)(2,1)} %bitcast.6, ...), custom_call_target="tpu_custom_call" | custom-call | tf_op jit(solution)/shard_map/front/pallas_call | solution.py:801
  123.4 86.5 %mlp.1 = (bf16[8,8,16,2816]{3,2,1,0:T(8,128)(2,1)}, bf16[4,128,2048]{2,1,0:T(8,128)(2,1)}, bf16[8,128,2048]{2,1,0:T(8,128)(2,1)}, f32[128,2048]{1,0:T(8,128)}, bf16[4,4,16,1408]{3,2,1,0:T(8,128)(2,1)}) custom-call(f32[128,2048]{1,0:T(8,128)} %get-tuple-element.25.resid, bf16[128,2048]{1,0:T(8,128)(2,1)} %bitcast.9, s32[1,1]{1,0:T(1,128)S(6)} %copy.23.count_ref, ...), custom_call_target="tpu_custom_call" | custom-call | tf_op jit(solution)/shard_map/mlp/pallas_call | solution.py:969
  210.0 99.8 %back.1 = (bf16[128,2048]{1,0:T(8,128)(2,1)}, f32[128,2048]{1,0:T(8,128)}, f32[16,4,2048]{2,1,0:T(4,128)}, f32[16,3,5504]{2,1,0:T(4,128)}, f32[16,256]{1,0:T(8,128)}) custom-call(f32[128,2048]{1,0:T(8,128)} %get-tuple-element.29.grad_resid, bf16[128,2048]{1,0:T(8,128)(2,1)} %bitcast.7, s32[1,1]{1,0:T(1,128)S(6)} %copy.23.count_ref, ...), custom_call_target="tpu_custom_call" | custom-call | tf_op jit(solution)/shard_map/back/pallas_call | solution.py:1181
  309.8 0.0 copy-start
  309.8 0.0 copy-start.1
  309.8 1.5 slice_reduce_fusion
  311.3 2.4 copy.19
  313.7 1.9 copy.24
  315.5 0.0 copy-done
  315.5 1.0 copy.25
  316.5 0.0 copy-done.1
  316.5 0.8 copy.26
Async XLA Ops:
  309.8 5.8 %copy-start = (f32[128,2048]{1,0:T(8,128)S(1)}, f32[128,2048]{1,0:T(8,128)}, u32[]{:S(2)}) copy-start(f32[128,2048]{1,0:T(8,128)} %get-tuple-element.40) | copy-start | bytes 3145732
  309.8 6.7 %copy-start.1 = (f32[16,4,2048]{2,1,0:T(4,128)S(1)}, f32[16,4,2048]{2,1,0:T(4,128)}, u32[]{:S(2)}) copy-start(f32[16,4,2048]{2,1,0:T(4,128)} %get-tuple-element.67) | copy-start | bytes 1572868

commit v6 on v5

--- a/solution.py
+++ b/solution.py
@@ -424,8 +424,7 @@
         mail.sent(n + i)
 
 
-def scatter_z(me, mail, acc, z_over, z_near):
-    xs = (me.x_far, me.x, me.x_up, me.x_down)
+def scatter_z(me, mail, acc, xs, z_over, z_near):
     zs = (me.z, me.z_up, me.z_down, me.z_far)
 
     def at(x):
@@ -434,17 +433,16 @@
     rings = [RingSum(mail, at(x), zs, (me.z_up_dev, me.z_down_dev), z_over.at[k], z_near.at[k]) for k, x in enumerate(xs)]
     rings[0].first()
     yield
-    rings[2].first()
-    rings[3].first()
-    rings[1].first()
-    yield
-    for k in (0, 2, 3, 1):
-        rings[k].second()
+    for ring in rings[1:]:
+        ring.first()
+    yield
+    for ring in rings:
+        ring.second()
         yield
-    for k in (0, 2, 3):
-        rings[k].third()
+    for ring in rings[:-1]:
+        ring.third()
         yield
-    rings[1].third()
+    rings[-1].third()
 
 
 def scatter_x(me, mail, at, x_over, x_near):
@@ -613,6 +611,12 @@
 def step(task, count=1):
     for _ in range(count):
         next(task, None)
+
+
+def beside(task, other):
+    for _ in task:
+        step(other)
+        yield
 
 
 def finish(task, *others):
@@ -823,11 +827,11 @@
     resid, cot_ref, count_ref, two_all, grad_all, wm_all,
     acc_out, branch_out, branch_grads, grad_resid, down_out,
     wm, grads, twos, hidden, pair, part, branch, p2, p1, grad_branch,
-    stage_d, acc_d, z_over, z_near, stage, acc, send, recv, local_sem, wm_sem,
+    stage_d, acc_d, z_over, z_near, pz_over, pz_near, stage, acc, send, recv, local_sem, wm_sem,
 ):
     me = Place()
     mail = Mail(send, recv)
-    saves = []
+    saves, first_saves = [], []
 
     def save(src, dst):
         copy = pltpu.make_async_copy(src, dst, local_sem.at[len(saves)])
@@ -920,12 +924,13 @@
         out[...] = terms.reshape(8, 2, 16, PAIR).astype(LOW)
 
     def kept(i):
-        save(acc.at[order[i]], acc_out.at[order[i]])
+        first_saves.append(save(acc.at[order[i]], acc_out.at[order[i]]))
 
     scatter = scatter_y(me, mail, part, p2, p1, write)
     twin_d = twin_sum(me, mail, stage_d, acc_d, order, down_product)
     twin = twin_sum(me, mail, stage, acc, order, pair_product, kept)
-    sums = scatter_z(me, mail, acc_d, z_over, z_near)
+    sums = scatter_z(me, mail, acc_d, (me.x_far, me.x_up, me.x_down, me.x), z_over, z_near)
+    early = scatter_z(me, mail, acc, (me.x_far, me.x_up), pz_over, pz_near)
     gather = gather_seq(me, mail, grad_branch, branch_grads)
     lax.fori_loop(0, 5, ahead_tile, 0)
     ahead(10, 1)
@@ -943,21 +948,29 @@
     step(scatter)
     step(gather)
     keep = save(grad_branch, branch_grads.at[me.seq])
-    step(sums, 2)
+    step(sums)
     run(twin)
+    step(early, 2)
+    step(sums)
     step(gather)
+    for copy in first_saves:
+        copy.wait()
     for i in range(5):
         if i < 4:
             lax.fori_loop(2 * i, 2 * i + 2, down_back, 0)
-        step(sums)
+        step(sums if i < 3 else early)
         step(gather)
     save(branch, branch_out)
-    run(sums)
+    finish(gather, sums, early)
+    run(sums, early)
     for x in range(4):
         save(acc_d.at[x % 2 * 4 : x % 2 * 4 + 4, me.z * 2 + x // 2], down_out.at[x])
-    run(gather)
+    for x in (me.x_far, me.x_up):
+        place = pl.ds(x % 2 * 4, 4), me.z * 2 + x // 2
+        save(acc.at[place], acc_out.at[place])
     for copy in saves[2:]:
-        copy.wait()
+        if not any(copy is first for first in first_saves):
+            copy.wait()
     mail.finish()
 
 
@@ -965,7 +978,7 @@
     vmem, anywhere = pl.BlockSpec(memory_space=pltpu.VMEM), pl.BlockSpec(memory_space=pl.ANY)
     shape = jax.ShapeDtypeStruct
     blocks = (4, ROWS, MODEL)
-    count = 6 + 8 + 8 + 24 + 18
+    count = 6 + 8 + 8 + 24 + 12 + 18
     return pl.pallas_call(
         mlp_kernel,
         out_shape=(
@@ -981,8 +994,9 @@
             pltpu.VMEM((ROWS, MODEL), LOW),
             pltpu.VMEM((2, 8, 2, 16, UNITS), LOW), pltpu.VMEM((8, 8, 16, UNITS), LOW),
             pltpu.VMEM((4, 2, 2, 16, UNITS), LOW), pltpu.VMEM((4, 2, 4, 16, UNITS), LOW),
+            pltpu.VMEM((2, 2, 2, 16, PAIR), LOW), pltpu.VMEM((2, 2, 4, 16, PAIR), LOW),
             pltpu.VMEM((2, 8, 2, 16, PAIR), LOW), pltpu.VMEM((8, 8, 16, PAIR), LOW),
-            pltpu.SemaphoreType.DMA((count,)), pltpu.SemaphoreType.DMA((count,)), pltpu.SemaphoreType.DMA((16,)), pltpu.SemaphoreType.DMA((12,)),
+            pltpu.SemaphoreType.DMA((count,)), pltpu.SemaphoreType.DMA((count,)), pltpu.SemaphoreType.DMA((18,)), pltpu.SemaphoreType.DMA((12,)),
         ],
         compiler_params=pltpu.CompilerParams(collective_id=2, has_side_effects=True, vmem_limit_bytes=62 * 2**20),
         name="mlp",
@@ -1005,7 +1019,7 @@
         loads.append(copy)
         return copy
 
-    load_acc = [load(acc_all.at[pl.ds(col * 4, 4)], acc.at[pl.ds(col * 4, 4)]) for col in (me.a, me.b)]
+    load_acc = [load(acc_all.at[pl.ds(col * 4, 4)], acc.at[pl.ds(col * 4, 4)]) for col in (me.b, me.a)]
     load_down = load(down_all, down)
     load_branch = load(branch_all, branch)
     ready = greet(me.peers() + [me.h_dev, me.z_up_dev, me.z_down_dev, me.x_up_dev, me.x_down_dev, me.twin_dev])
@@ -1023,7 +1037,7 @@
         yield from send_y(me, mail, down.at[me.x], down_own)
 
     def pair_sums():
-        yield from scatter_z(me, mail, acc, z_over, z_near)
+        yield from scatter_z(me, mail, acc, (me.x_down, me.x), z_over, z_near)
         yield from scatter_x(me, mail, lambda x: acc.at[pl.ds(x % 2 * 4, 4), me.z * 2 + x // 2], x_over, x_near)
         yield from send_y(me, mail, acc.at[pl.ds(me.a * 4, 4), me.z * 2 + me.h], pair_own)
 
@@ -1123,6 +1137,7 @@
     step(twin, 3)
     step(grad_sum)
     step(downs)
+    step(sums)
     step(twin, 3)
     step(grad_sum)
     step(sums)
@@ -1135,11 +1150,11 @@
 
     rest = proj_sums()
     step(rest)
-    finish(grad_sum, sums, rest)
+    run(grad_sum, sums, rest)
     own = acc_a.at[:, me.z * 2 + me.h]
     gain = column(gain_one)
     sum_one = jnp.zeros((16, 1), WIDE)
-    run(sums, out_sum, downs)
+    run(beside(sums, rest), out_sum, downs)
     units = mlp_ref.shape[2] // 4
     spare = jnp.zeros((16, mlp_ref.shape[2] - UNITS), WIDE)
     gain_mlp = column(gain_two)
@@ -1177,7 +1192,7 @@
 def back(grad_resid, x, counts, resid, attn_weight, mlp_weight, gain_one, gain_two, down, grads, branch, acc, ones, wa, qkv, probs, att):
     vmem, anywhere = pl.BlockSpec(memory_space=pltpu.VMEM), pl.BlockSpec(memory_space=pl.ANY)
     shape = jax.ShapeDtypeStruct
-    count = 9 + 30 + 3 + 6 + 23 + 8 + 13 + 7
+    count = 9 + 18 + 3 + 6 + 23 + 8 + 13 + 7
     return pl.pallas_call(
         back_kernel,
         out_shape=(
@@ -1188,7 +1203,7 @@
         out_specs=(vmem,) * 5,
         scratch_shapes=[
             pltpu.VMEM((4, 4, 16, UNITS), LOW), pltpu.VMEM((2, 2, 16, UNITS), LOW), pltpu.VMEM((2, 4, 16, UNITS), LOW),
-            pltpu.VMEM((4, 16, UNITS), LOW), pltpu.VMEM((4, 16, PAIR), LOW), pltpu.VMEM((8, 16, PROJ), LOW), pltpu.VMEM((8, 8, 16, PAIR), LOW), pltpu.VMEM((4, 2, 2, 16, PAIR), LOW), pltpu.VMEM((4, 2, 4, 16, PAIR), LOW),
+            pltpu.VMEM((4, 16, UNITS), LOW), pltpu.VMEM((4, 16, PAIR), LOW), pltpu.VMEM((8, 16, PROJ), LOW), pltpu.VMEM((8, 8, 16, PAIR), LOW), pltpu.VMEM((2, 2, 2, 16, PAIR), LOW), pltpu.VMEM((2, 2, 4, 16, PAIR), LOW),
             pltpu.VMEM((2, 2, 16, PAIR), LOW), pltpu.VMEM((2, 4, 16, PAIR), LOW), pltpu.VMEM((8, ROWS, MODEL), LOW),
             pltpu.VMEM((4, ROWS, MODEL), LOW), pltpu.VMEM((2, ROWS, MID), LOW), pltpu.VMEM((2, ROWS, MODEL), LOW),
             pltpu.VMEM((8, ROWS, MODEL), LOW),

time: 322 us -> 302 us (0.938)
  Pallas kernels: 306 us -> 286 us
    pallas_call x1, Pallas kernels: 99.8 us -> 76.3 us  [back(): pl.pallas_call(back_kernel, out_shape=(shape((ROWS, MODEL), LOW), shape((...]
where the time goes in v6:
time: 302 us; the launch traced here: 297 us
  Pallas kernels  286 us (95%)
  local copies, waits for them, and re-layouts  9.67 us (3%)
    pallas_call x1, Pallas kernels, front(): pl.pallas_call(front_kernel, out_shape=(shape((8, 256, 1024), LOW), shape...  120 us
    pallas_call x1, Pallas kernels, mlp(): pl.pallas_call(mlp_kernel, out_shape=(shape((8, 8, 16, PAIR), LOW), shape...  89.2 us
    pallas_call x1, Pallas kernels, back(): pl.pallas_call(back_kernel, out_shape=(shape((ROWS, MODEL), LOW), shape((...  76.3 us
    unnamed x9, local copies, waits for them, and re-layouts  8.21 us

profile of v6, /device:TPU:0, one launch (start us, length us, event | category | flops | bytes accessed | tf_op | source)
XLA Modules:
  0.0 297.0 jit_solution(4456908211305109473)
XLA Ops:
  1.3 2.2 copy.17.mlp_ref
  3.4 120.0 %front.1 = (bf16[8,256,1024]{2,1,0:T(8,128)(2,1)}, bf16[8,16,16,1024]{3,2,1,0:T(8,128)(2,1)}, bf16[4,128,2048]{2,1,0:T(8,128)(2,1)}, bf16[8,16,16,4224]{3,2,1,0:...) custom-call(bf16[128,2048]{1,0:T(8,128)(2,1)} %bitcast.6, ...), custom_call_target="tpu_custom_call" | custom-call | tf_op jit(solution)/shard_map/front/pallas_call | solution.py:805
  123.4 89.2 %mlp.1 = (bf16[8,8,16,2816]{3,2,1,0:T(8,128)(2,1)}, bf16[4,128,2048]{2,1,0:T(8,128)(2,1)}, bf16[8,128,2048]{2,1,0:T(8,128)(2,1)}, f32[128,2048]{1,0:T(8,128)}, bf16[4,4,16,1408]{3,2,1,0:T(8,128)(2,1)}) custom-call(f32[128,2048]{1,0:T(8,128)} %get-tuple-element.25.resid, bf16[128,2048]{1,0:T(8,128)(2,1)} %bitcast.9, s32[1,1]{1,0:T(1,128)S(6)} %copy.23.count_ref, ...), custom_call_target="tpu_custom_call" | custom-call | tf_op jit(solution)/shard_map/mlp/pallas_call | solution.py:982
  212.7 76.3 %back.1 = (bf16[128,2048]{1,0:T(8,128)(2,1)}, f32[128,2048]{1,0:T(8,128)}, f32[16,4,2048]{2,1,0:T(4,128)}, f32[16,3,5504]{2,1,0:T(4,128)}, f32[16,256]{1,0:T(8,128)}) custom-call(f32[128,2048]{1,0:T(8,128)} %get-tuple-element.29.grad_resid, bf16[128,2048]{1,0:T(8,128)(2,1)} %bitcast.7, s32[1,1]{1,0:T(1,128)S(6)} %copy.23.count_ref, ...), custom_call_target="tpu_custom_call" | custom-call | tf_op jit(solution)/shard_map/back/pallas_call | solution.py:1196
  289.0 0.0 copy-start
  289.0 0.0 copy-start.1
  289.0 1.5 slice_reduce_fusion
  290.5 2.4 copy.19
  292.9 1.9 copy.24
  294.8 0.0 copy-done
  294.8 1.0 copy.25
  295.7 0.0 copy-done.1
  295.7 0.8 copy.26
Async XLA Ops:
  289.0 5.8 %copy-start = (f32[128,2048]{1,0:T(8,128)S(1)}, f32[128,2048]{1,0:T(8,128)}, u32[]{:S(2)}) copy-start(f32[128,2048]{1,0:T(8,128)} %get-tuple-element.40) | copy-start | bytes 3145732
  289.0 6.7 %copy-start.1 = (f32[16,4,2048]{2,1,0:T(4,128)S(1)}, f32[16,4,2048]{2,1,0:T(4,128)}, u32[]{:S(2)}) copy-start(f32[16,4,2048]{2,1,0:T(4,128)} %get-tuple-element.67) | copy-start | bytes 1572868

commit v7 on v6

--- a/solution.py
+++ b/solution.py
@@ -18,7 +18,7 @@
 UNITS = 1408
 SLAB = 3 * UNITS
 PAIR = 2 * UNITS
-FIRST = 96
+FIRST = 112
 MID = MODEL // 2
 
 

time: 302 us -> 313 us (1.036)
  Pallas kernels: 286 us -> 296 us
    pallas_call x1, Pallas kernels: 89.2 us -> 93.9 us  [mlp(): pl.pallas_call(mlp_kernel, out_shape=(shape((8, 8, 16, PAIR), LOW), shape...]
    pallas_call x1, Pallas kernels: 120 us -> 124 us  [front(): pl.pallas_call(front_kernel, out_shape=(shape((8, 256, 1024), LOW), shape...]
where the time goes in v7:
time: 313 us; the launch traced here: 308 us
  Pallas kernels  296 us (95%)
  local copies, waits for them, and re-layouts  9.67 us (3%)
    pallas_call x1, Pallas kernels, front(): pl.pallas_call(front_kernel, out_shape=(shape((8, 256, 1024), LOW), shape...  124 us
    pallas_call x1, Pallas kernels, mlp(): pl.pallas_call(mlp_kernel, out_shape=(shape((8, 8, 16, PAIR), LOW), shape...  93.9 us
    pallas_call x1, Pallas kernels, back(): pl.pallas_call(back_kernel, out_shape=(shape((ROWS, MODEL), LOW), shape((...  78.2 us
    unnamed x9, local copies, waits for them, and re-layouts  8.21 us

profile of v7, /device:TPU:0, one launch (start us, length us, event | category | flops | bytes accessed | tf_op | source)
XLA Modules:
  0.0 307.9 jit_solution(4177659002668833909)
XLA Ops:
  1.3 2.2 copy.17.mlp_ref
  3.4 124.3 %front.1 = (bf16[8,256,1024]{2,1,0:T(8,128)(2,1)}, bf16[8,16,16,1024]{3,2,1,0:T(8,128)(2,1)}, bf16[4,128,2048]{2,1,0:T(8,128)(2,1)}, bf16[8,16,16,4224]{3,2,1,0:...) custom-call(bf16[128,2048]{1,0:T(8,128)(2,1)} %bitcast.6, ...), custom_call_target="tpu_custom_call" | custom-call | tf_op jit(solution)/shard_map/front/pallas_call | solution.py:805
  127.8 93.9 %mlp.1 = (bf16[8,8,16,2816]{3,2,1,0:T(8,128)(2,1)}, bf16[4,128,2048]{2,1,0:T(8,128)(2,1)}, bf16[8,128,2048]{2,1,0:T(8,128)(2,1)}, f32[128,2048]{1,0:T(8,128)}, bf16[4,4,16,1408]{3,2,1,0:T(8,128)(2,1)}) custom-call(f32[128,2048]{1,0:T(8,128)} %get-tuple-element.25.resid, bf16[128,2048]{1,0:T(8,128)(2,1)} %bitcast.9, s32[1,1]{1,0:T(1,128)S(6)} %copy.23.count_ref, ...), custom_call_target="tpu_custom_call" | custom-call | tf_op jit(solution)/shard_map/mlp/pallas_call | solution.py:982
  221.7 78.2 %back.1 = (bf16[128,2048]{1,0:T(8,128)(2,1)}, f32[128,2048]{1,0:T(8,128)}, f32[16,4,2048]{2,1,0:T(4,128)}, f32[16,3,5504]{2,1,0:T(4,128)}, f32[16,256]{1,0:T(8,128)}) custom-call(f32[128,2048]{1,0:T(8,128)} %get-tuple-element.29.grad_resid, bf16[128,2048]{1,0:T(8,128)(2,1)} %bitcast.7, s32[1,1]{1,0:T(1,128)S(6)} %copy.23.count_ref, ...), custom_call_target="tpu_custom_call" | custom-call | tf_op jit(solution)/shard_map/back/pallas_call | solution.py:1196
  299.9 0.0 copy-start
  299.9 0.0 copy-start.1
  299.9 1.5 slice_reduce_fusion
  301.4 2.4 copy.19
  303.8 1.9 copy.24
  305.7 0.0 copy-done
  305.7 1.0 copy.25
  306.6 0.0 copy-done.1
  306.6 0.8 copy.26
Async XLA Ops:
  299.9 5.8 %copy-start = (f32[128,2048]{1,0:T(8,128)S(1)}, f32[128,2048]{1,0:T(8,128)}, u32[]{:S(2)}) copy-start(f32[128,2048]{1,0:T(8,128)} %get-tuple-element.40) | copy-start | bytes 3145732
  299.9 6.7 %copy-start.1 = (f32[16,4,2048]{2,1,0:T(4,128)S(1)}, f32[16,4,2048]{2,1,0:T(4,128)}, u32[]{:S(2)}) copy-start(f32[16,4,2048]{2,1,0:T(4,128)} %get-tuple-element.67) | copy-start | bytes 1572868
